TPU v7x, 32 devices: a whole 2x2x4 slice. The times are simulated.
32 devices in a mesh: groups: 2 (over y), dp: 16 (over z, x, core).
Axes of the slice: x: 2, y: 2, z: 4, core: 2. Of those that a mesh axis runs over, the one named last changes fastest.
Arguments:
- acts: bfloat16 [8192, 5120], P(('groups', 'dp')), parts along dimension 0, may hold values from -6 to 6
- cotan: bfloat16 [8192, 1024], P(('groups', 'dp')), parts along dimension 0, may hold values from -4 to 4
- frozen_key_weight: bfloat16 [5120, 1024], P('dp'), may hold values from -0.078125 to 0.078125
- adapter_down_slots: bfloat16 [64, 5120, 128], P(('groups', 'dp')), parts along dimension 0, may hold values from -0.078125 to 0.078125
- adapter_up_slots: bfloat16 [64, 128, 1024], P(('groups', 'dp')), parts along dimension 0, may hold values from -0.5 to 0.5
- token_row_jobs: int32 [8192, 1], P(('groups', 'dp')), parts along dimension 0, may hold values from 0 to 31; in each aligned block of 256 rows (0 to 255, 256 to 511, ...) at most 16 rows name the same one
- slot_owner_jobs: int32 [64], P('groups'), parts along dimension 0, may hold values from 0 to 31, each once
- loss_token_count: int32 [64], P('groups'), parts along dimension 0, may hold values from 128 to 1023
Outputs:
- grad_acts: bfloat16 [8192, 5120], P(('groups', 'dp')), parts along dimension 0
- grad_a: bfloat16 [64, 5120, 128], P(('groups', 'dp')), parts along dimension 0
- grad_b: bfloat16 [64, 128, 1024], P(('groups', 'dp')), parts along dimension 0
There are 2 independent parts, one for each index of `groups`. A program takes and returns all parts, laid end to end along the dimension named above; an argument that names none is the same for every part. Nothing has to cross between parts.
Inputs may be any that keep to these rules, and one draw needn't show every extreme that they name: `token_row_jobs`: among the rows of one device no job is named by more than 16 rows, a bound that some block reaches; every job is named by some row. `slot_owner_jobs`: each job appears once; slot s lies on index s // 2 of dp.
All inputs are finite; a program needn't handle non-finite values.
Results may differ from a plain program's by a relative error of at most 0.0059.
Values may be sent and summed in bfloat16 or wider, within the bound.
No kernel may reach another device: no remote copies, remote signals or barrier semaphores. Data moves between devices by JAX's collectives and lax.ppermute only.
A program may use at most 128 MiB of HBM per device.

v0:
```python
import jax
import jax.numpy as jnp
from jax import lax
from jax.sharding import PartitionSpec as P

DELTA_MULTIPLIER = 0.25


def project_base(frozen_key_weight, left_operand):
    return lax.dot_general(
        left_operand,
        lax.all_gather(frozen_key_weight, "dp", axis=0, tiled=True),
        (((1,), (1,)), ((), ())),
        preferred_element_type=jnp.float32,
    )


def shards(
    acts,
    cotan,
    frozen_key_weight,
    adapter_down_slots,
    adapter_up_slots,
    token_row_jobs,
    slot_owner_jobs,
    loss_token_count,
):
    devices = lax.axis_size("dp")
    tok_rows = acts.shape[0]
    width = acts.shape[1]
    out_width = cotan.shape[1]
    local_tasks_present = adapter_down_slots.shape[0]
    jobs_all = slot_owner_jobs.shape[0]
    depth = 2 * tok_rows // (local_tasks_present * devices)
    per_peer = local_tasks_present * depth
    ids = token_row_jobs[:, 0]
    lengths = loss_token_count.astype(jnp.float32)
    weights = jnp.mean(lengths) / lengths
    numbers = jnp.arange(jobs_all, dtype=jnp.int32)
    row_weight = jnp.sum(jnp.where(ids[:, None] == numbers[None, :], weights[None, :], 0.0), axis=1)
    row_slot = jnp.sum(
        jnp.where(ids[:, None] == slot_owner_jobs[None, :], numbers[None, :], 0), axis=1
    )
    same = ids[:, None] == ids[None, :]
    earlier = jnp.arange(tok_rows)[None, :] < jnp.arange(tok_rows)[:, None]
    ranks = jnp.sum(jnp.where(same & earlier, 1, 0), axis=1).astype(jnp.int32)
    position = (
        row_slot // local_tasks_present * per_peer + row_slot % local_tasks_present * depth + ranks
    )
    sources = (
        jnp.full((devices * per_peer,), tok_rows, jnp.int32)
        .at[position]
        .set(jnp.arange(tok_rows, dtype=jnp.int32))
    )
    scaled = (row_weight[:, None] * cotan.astype(jnp.float32)).astype(jnp.bfloat16)
    acts_pad = jnp.concatenate([acts, jnp.zeros((1, width), acts.dtype)], axis=0)
    scaled_pad = jnp.concatenate([scaled, jnp.zeros((1, out_width), scaled.dtype)], axis=0)
    send_acts = jnp.take(acts_pad, sources, axis=0)
    send_scaled = jnp.take(scaled_pad, sources, axis=0)
    recv_acts, recv_scaled = (
        lax.all_to_all(send_acts, "dp", split_axis=0, concat_axis=0, tiled=True),
        lax.all_to_all(send_scaled, "dp", split_axis=0, concat_axis=0, tiled=True),
    )
    left_operand = recv_acts.reshape(devices, local_tasks_present, depth, width)
    second_factor_input = recv_scaled.reshape(devices, local_tasks_present, depth, out_width)
    thin_update_carry = jnp.einsum(
        "zqbo,qov->zqbv", left_operand, adapter_down_slots, preferred_element_type=jnp.float32
    ).astype(jnp.bfloat16)
    thin_update_reverse_pass = (
        DELTA_MULTIPLIER
        * jnp.einsum(
            "upih,pgh->upig",
            second_factor_input,
            adapter_up_slots,
            preferred_element_type=jnp.float32,
        )
    ).astype(jnp.bfloat16)
    grad_a = jnp.einsum(
        "skmd,skmr->kdr", left_operand, thin_update_reverse_pass, preferred_element_type=jnp.float32
    ).astype(jnp.bfloat16)
    grad_b = (
        DELTA_MULTIPLIER
        * jnp.einsum(
            "skmr,skmv->krv",
            thin_update_carry,
            second_factor_input,
            preferred_element_type=jnp.float32,
        )
    ).astype(jnp.bfloat16)
    adapter_term = jnp.einsum(
        "lciq,cnq->lcin",
        thin_update_reverse_pass,
        adapter_down_slots,
        preferred_element_type=jnp.float32,
    )
    adapter_term = adapter_term.reshape(devices * per_peer, width).astype(jnp.bfloat16)
    base_grad = project_base(frozen_key_weight, scaled)
    returned = lax.all_to_all(adapter_term, "dp", split_axis=0, concat_axis=0, tiled=True)
    grad_acts = (base_grad + jnp.take(returned, position, axis=0).astype(jnp.float32)).astype(
        jnp.bfloat16
    )
    return (grad_acts, grad_a, grad_b)


def solution(mesh):
    return jax.shard_map(
        shards,
        mesh=mesh,
        in_specs=(
            P(("groups", "dp"), None),
            P(("groups", "dp"), None),
            P("dp", None),
            P(("groups", "dp"), None, None),
            P(("groups", "dp"), None, None),
            P(("groups", "dp"), None),
            P("groups"),
            P("groups"),
        ),
        out_specs=(
            P(("groups", "dp"), None),
            P(("groups", "dp"), None, None),
            P(("groups", "dp"), None, None),
        ),
        check_vma=False,
    )
```

profile of v0, /device:TPU:11, one launch (start us, length us, event | category | flops | bytes accessed | tf_op | source)
XLA Modules:
  0.0 384.7 jit_solution(16368962852981013773)
XLA Ops:
  7.2 1.0 select_reduce_fusion
  9.0 1.4 scatter_custom_fusion
  10.5 1.3 convert_reduce_fusion
  13.9 1.2 multiply_convert_fusion
  15.1 0.8 copy-done.2
  15.9 2.8 gather_fusion
  18.7 2.4 broadcast_select_fusion.1
  21.1 6.6 %all-to-all-start = ((bf16[16,32,1024]{2,1,0:T(8,128)(2,1)}), bf16[16,32,1024]{2,1,0:T(8,128)(2,1)}, u32[]{:S(2)}, u32[]{:S(2)}) async-start(bf16[16,32,1024]{2,1,0:T(8,128)(2,1)} %broadcast_select_fusion.1), calls=%async_computation | async-start | bytes 2097152 | tf_op jit(solution)/shard_map/all_to_all | solution.py:62
  27.6 3.5 concatenate.7
  31.2 12.6 %gather_fusion.2 = bf16[512,5120]{1,0:T(8,128)(2,1)} fusion(bf16[257,5120]{1,0:T(8,128)(2,1)} %concatenate.7, s32[1024]{0:T(1024)S(1)} %pad_clamp_fusion.1), kind=kCustom, calls=%fused_computation.2 | custom fusion | bytes 10487808 | tf_op jit(solution)/shard_map/jit(_take)/gather | solution.py:58
  43.8 5.3 %broadcast_select_fusion = bf16[16,32,5120]{2,1,0:T(8,128)(2,1)} fusion(bf16[16,32,5120]{2,1,0:T(8,128)(2,1)} %bitcast.56, pred[16,32]{1,0:T(8,128)(4,1)S(1)} %broadcast_in_dim.84), kind=kLoop, calls=%fused_computation.10 | loop fusion | flops 2621440 | bytes 10486272 | tf_op jit(solution)/shard_map/jit(_take)/select_n | solution.py:58
  49.0 3.6 all-to-all-done
  52.6 4.9 %all-to-all-start.2 = ((bf16[16,32,5120]{2,1,0:T(8,128)(2,1)}), bf16[16,32,5120]{2,1,0:T(8,128)(2,1)}, u32[]{:S(2)}, u32[]{:S(2)}) async-start(bf16[16,32,5120]{2,1,0:T(8,128)(2,1)} %broadcast_select_fusion), calls=%async_computation.2 | async-start | bytes 10485760 | tf_op jit(solution)/shard_map/all_to_all | solution.py:61
  58.3 1.8 fusion.15
  60.1 1.5 fusion
  61.6 2.8 copy.27
  64.4 171.3 %all-to-all-done.2 = bf16[16,32,5120]{2,1,0:T(8,128)(2,1)} async-done(((bf16[16,32,5120]{2,1,0:T(8,128)(2,1)}), bf16[16,32,5120]{2,1,0:T(8,128)(2,1)}, u32[]{:S(2)}, u32[]{:S(2)}) %all-to-all-start.2) | async-done | bytes 5242912 | tf_op jit(solution)/shard_map/all_to_all | solution.py:61
  235.7 4.9 %all-to-all-start.1 = ((bf16[16,32,5120]{2,1,0:T(8,128)(2,1)}), bf16[16,32,5120]{2,1,0:T(8,128)(2,1)}, u32[]{:S(2)}, u32[]{:S(2)}) async-start(bf16[16,32,5120]{2,1,0:T(8,128)(2,1)} %bitcast.53), calls=%async_computation.1 | async-start | bytes 10485760 | tf_op jit(solution)/shard_map/all_to_all | solution.py:98
  240.6 7.8 %copy.28 = bf16[16,32,5120]{2,0,1:T(8,128)(2,1)} copy(bf16[16,32,5120]{2,1,0:T(8,128)(2,1)} %all-to-all-done.2) | data formatting | bytes 10485760 | tf_op jit(solution)/shard_map/all_to_all | solution.py:61
  248.4 5.7 %fusion.7 = bf16[2,128,1024]{2,1,0:T(8,128)(2,1)} fusion(bf16[16,2,16,5120]{3,0,2,1:T(8,128)(2,1)} %bitcast.54, bf16[2,5120,128]{2,1,0:T(8,128)(2,1)S(1)} %copy-done, bf16[16,2,16,1024]{3,2,1,0:T(8,128)(2,1)} %bitcast.5), kind=kOutput, calls=%fused_computation.16 | convolution fusion | flops 805896192 | bytes 9437184 | tf_op jit(solution)/shard_map/skmr,skmv->krv/dot_general | solution.py:83
  254.1 6.1 %fusion.1 = bf16[2,5120,128]{2,1,0:T(8,128)(2,1)} fusion(bf16[16,2,16,5120]{3,0,2,1:T(8,128)(2,1)} %bitcast.55, bf16[16,2,16,128]{3,2,0,1:T(8,128)(2,1)S(1)} %fusion.15), kind=kOutput, calls=%fused_computation.8 | convolution fusion | flops 672399360 | bytes 7995392 | tf_op jit(solution)/shard_map/skmd,skmr->kdr/dot_general | solution.py:78
  260.2 95.3 %all-to-all-done.1 = bf16[16,32,5120]{2,1,0:T(8,128)(2,1)} async-done(((bf16[16,32,5120]{2,1,0:T(8,128)(2,1)}), bf16[16,32,5120]{2,1,0:T(8,128)(2,1)}, u32[]{:S(2)}, u32[]{:S(2)}) %all-to-all-start.1) | async-done | bytes 5242912 | tf_op jit(solution)/shard_map/all_to_all | solution.py:98
  355.5 9.6 %gather_fusion.1 = bf16[256,5120]{1,0:T(8,128)(2,1)} fusion(bf16[512,5120]{1,0:T(8,128)(2,1)} %bitcast.13, s32[1024]{0:T(1024)S(1)} %pad_clamp_fusion), kind=kCustom, calls=%fused_computation.1 | custom fusion | bytes 5243904 | tf_op jit(solution)/shard_map/jit(_take)/gather | solution.py:99
  365.2 12.7 %fusion.2 = bf16[256,5120]{1,0:T(8,128)(2,1)} fusion(bf16[256,1024]{1,0:T(8,128)(2,1)S(1)} %copy-done.3, bf16[5120,1024]{1,0:T(8,128)(2,1)} %all-gather.2.cloned.1.call-done, bf16[256,5120]{1,0:T(8,128)(2,1)} %gather_fusion.1, pred[256]{0:T(512)(128)(4,1)S(1)} %compare_and_fusion.1), kind=kOutput, calls=%fused_computation.9 | convolution fusion | flops 2689597440 | bytes 16253184 | tf_op jit(solution)/shard_map/dot_general | solution.py:10
  (22 shorter events, 3.1 us)
Async XLA Ops:
  7.2 52.9 %copy-start = (bf16[2,5120,128]{2,1,0:T(8,128)(2,1)S(1)}, bf16[2,5120,128]{2,1,0:T(8,128)(2,1)}, u32[]{:S(2)}) copy-start(bf16[2,5120,128]{2,1,0:T(8,128)(2,1)} %param.11) | copy-start | bytes 7864324
  15.1 0.8 copy-start.2
  21.1 31.5 %all-to-all-start = ((bf16[16,32,1024]{2,1,0:T(8,128)(2,1)}), bf16[16,32,1024]{2,1,0:T(8,128)(2,1)}, u32[]{:S(2)}, u32[]{:S(2)}) async-start(bf16[16,32,1024]{2,1,0:T(8,128)(2,1)} %broadcast_select_fusion.1), calls=%async_computation | async-start | bytes 2097152 | tf_op jit(solution)/shard_map/all_to_all | solution.py:62
  52.6 183.1 %all-to-all-start.2 = ((bf16[16,32,5120]{2,1,0:T(8,128)(2,1)}), bf16[16,32,5120]{2,1,0:T(8,128)(2,1)}, u32[]{:S(2)}, u32[]{:S(2)}) async-start(bf16[16,32,5120]{2,1,0:T(8,128)(2,1)} %broadcast_select_fusion), calls=%async_computation.2 | async-start | bytes 10485760 | tf_op jit(solution)/shard_map/all_to_all | solution.py:61
  57.5 307.6 %all-gather.2.cloned.1.call-start = ((), (), s32[]{:S(2)}) async-start(), calls=%async_computation.3 | async-start | bytes 11141120 | tf_op jit(solution)/shard_map/all_gather | solution.py:12
  235.7 119.8 %all-to-all-start.1 = ((bf16[16,32,5120]{2,1,0:T(8,128)(2,1)}), bf16[16,32,5120]{2,1,0:T(8,128)(2,1)}, u32[]{:S(2)}, u32[]{:S(2)}) async-start(bf16[16,32,5120]{2,1,0:T(8,128)(2,1)} %bitcast.53), calls=%async_computation.1 | async-start | bytes 10485760 | tf_op jit(solution)/shard_map/all_to_all | solution.py:98
  355.5 9.6 %copy-start.3 = (bf16[256,1024]{1,0:T(8,128)(2,1)S(1)}, bf16[256,1024]{1,0:T(8,128)(2,1)}, u32[]{:S(2)}) copy-start(bf16[256,1024]{1,0:T(8,128)(2,1)} %copy-done.2) | copy-start | bytes 1572868
  365.2 12.7 %copy-start.1 = (bf16[2,5120,128]{2,1,0:T(8,128)(2,1)S(1)}, bf16[2,5120,128]{2,1,0:T(8,128)(2,1)}, u32[]{:S(2)}) copy-start(bf16[2,5120,128]{2,1,0:T(8,128)(2,1)} %param.11) | copy-start | bytes 7864324
Sparse Core Ops, SparseCore 0:
  60.7 159.4 all-gather.1
where the time goes:
time: 385 us
  waiting for transfers between devices  271 us (70%)
  local copies, waits for them, and re-layouts  41.4 us (11%)
  matrix products  27.9 us (7%)
  starting transfers between devices  16.4 us (4%)
  between operations  14.8 us (4%)
  other arithmetic  13.4 us (3%)
    all_to_all x1, waiting for transfers between devices, shards(): lax.all_to_all(send_acts, 'dp', split_axis=0, concat_axis=0, tiled=True)  171 us
    all_to_all x1, waiting for transfers between devices, shards(): lax.all_to_all(adapter_term, 'dp', split_axis=0, concat_axis=0, tiled=True)  95.3 us
    dot_general x1, matrix products, project_base(): lax.dot_general(left_operand, lax.all_gather(frozen_key_weight, 'dp', axi...  12.7 us
    gather x1, local copies, waits for them, and re-layouts, shards(): send_acts = jnp.take(acts_pad, sources, axis=0)  12.6 us
    gather x1, local copies, waits for them, and re-layouts, shards(): jnp.take(returned, position, axis=0).astype(jnp.float32)  9.62 us
    all_to_all x1, local copies, waits for them, and re-layouts, shards(): lax.all_to_all(send_acts, 'dp', split_axis=0, concat_axis=0, tiled=True)  7.76 us
  transfers between devices with their start and end apart: 4, of which 3 were waited for; matrix products, arithmetic and copies ran while one was open for 15% of the time, Pallas kernels for 0%

commit v1 on v0

v1 whole, which is shorter than its diff:
```python
import functools

import jax
import jax.numpy as jnp
from jax import lax
from jax.experimental import pallas as pl
from jax.experimental.pallas import tpu as pltpu
from jax.sharding import PartitionSpec as P

DELTA_MULTIPLIER = 0.25
BF = jnp.bfloat16
F32 = jnp.float32
PLANES = 4
PIECES = 4
PARAMS = pltpu.CompilerParams(vmem_limit_bytes=48 * 1024 * 1024)


def whole(shape):
    zeros = (0,) * len(shape)
    return pl.BlockSpec(shape, lambda i: zeros)


def dot(a, b, ca=1, cb=0):
    return lax.dot_general(a, b, (((ca,), (cb,)), ((), ())), preferred_element_type=F32)


def route_body(count, rows_ref, *refs):
    ins, outs = refs[:count], refs[count:]
    held = ins[0][...] if count == 1 else jnp.concatenate([r[...] for r in ins], axis=0)
    moved = dot(rows_ref[...], held).astype(BF)
    at = 0
    for out in outs:
        out[...] = moved[at : at + out.shape[0]]
        at += out.shape[0]


def route(rows, ins, outs, piece=None):
    width = ins[0].shape[1]
    specs = [whole(x.shape) for x in ins]
    if piece is not None:
        at, of = piece
        width = width // of
        specs = [pl.BlockSpec((ins[0].shape[0], width), lambda i: (0, at))]
    shapes = [(n, width) for n in outs]
    return pl.pallas_call(
        functools.partial(route_body, len(ins)),
        grid=(1,),
        in_specs=[whole(rows.shape)] + specs,
        out_specs=[whole(s) for s in shapes],
        out_shape=[jax.ShapeDtypeStruct(s, BF) for s in shapes],
        compiler_params=PARAMS,
    )(rows, *ins)


def back_body(count, up_ref, *refs):
    ins, out = refs[:count], refs[count]
    for job in range(up_ref.shape[0]):
        held = jnp.concatenate([r[job] for r in ins], axis=0)
        out[job] = (DELTA_MULTIPLIER * dot(held, up_ref[job], 1, 1)).astype(BF)


def back_project(up, ins):
    local, depth = up.shape[0], up.shape[1]
    shape = (local, sum(x.shape[1] for x in ins), depth)
    return pl.pallas_call(
        functools.partial(back_body, len(ins)),
        grid=(1,),
        in_specs=[whole(up.shape)] + [whole(x.shape) for x in ins],
        out_specs=whole(shape),
        out_shape=jax.ShapeDtypeStruct(shape, BF),
        compiler_params=PARAMS,
    )(up, *ins)


def term_body(back_ref, down_ref, *outs):
    for job in range(down_ref.shape[0]):
        term = dot(back_ref[job], down_ref[job], 1, 1).astype(BF)
        at = 0
        for out in outs:
            out[job] = term[at : at + out.shape[1]]
            at += out.shape[1]


def adapter_terms(back_low, down, piece, outs):
    at, of = piece
    local, width, rank = down.shape
    width = width // of
    shapes = [(local, n, width) for n in outs]
    return pl.pallas_call(
        term_body,
        grid=(1,),
        in_specs=[
            whole(back_low.shape),
            pl.BlockSpec((local, width, rank), lambda i: (0, at, 0)),
        ],
        out_specs=[whole(s) for s in shapes],
        out_shape=[jax.ShapeDtypeStruct(s, BF) for s in shapes],
        compiler_params=PARAMS,
    )(back_low, down)


def owner_body(count, carried, back_ref, down_ref, *refs):
    ins = refs[:count]
    refs = refs[count:]
    if carried:
        low_in, _, low_ref, grad_ref = refs
    else:
        low_ref, grad_ref = refs
    for job in range(down_ref.shape[0]):
        held = jnp.concatenate([r[job] for r in ins], axis=0)
        low = dot(held, down_ref[job])
        low_ref[job] = low_in[job] + low if carried else low
        grad_ref[job] = dot(held, back_ref[job], 0, 0).astype(BF)


def owner_step(back_low, down, ins, piece, carry):
    at, of = piece
    local, width, rank = down.shape
    part = pl.BlockSpec((local, width // of, rank), lambda i: (0, at, 0))
    low_shape = (local, back_low.shape[1], rank)
    extra, extra_specs, aliases = [], [], {}
    if carry is not None:
        extra = list(carry)
        extra_specs = [whole(low_shape), pl.BlockSpec(memory_space=pl.ANY)]
        aliases = {2 + len(ins): 0, 3 + len(ins): 1}
    return pl.pallas_call(
        functools.partial(owner_body, len(ins), carry is not None),
        grid=(1,),
        in_specs=[whole(back_low.shape), part] + [whole(x.shape) for x in ins] + extra_specs,
        out_specs=[whole(low_shape), part],
        out_shape=[
            jax.ShapeDtypeStruct(low_shape, F32),
            jax.ShapeDtypeStruct(down.shape, BF),
        ],
        input_output_aliases=aliases,
        compiler_params=PARAMS,
    )(back_low, down, *ins, *extra)


def up_body(count, low_ref, *refs):
    ins, out = refs[:count], refs[count]
    for job in range(low_ref.shape[0]):
        held = jnp.concatenate([r[job] for r in ins], axis=0)
        low = low_ref[job].astype(BF)
        out[job] = (DELTA_MULTIPLIER * dot(low, held, 0, 0)).astype(BF)


def up_gradient(low, ins):
    shape = (low.shape[0], low.shape[2], ins[0].shape[2])
    return pl.pallas_call(
        functools.partial(up_body, len(ins)),
        grid=(1,),
        in_specs=[whole(low.shape)] + [whole(x.shape) for x in ins],
        out_specs=whole(shape),
        out_shape=jax.ShapeDtypeStruct(shape, BF),
        compiler_params=PARAMS,
    )(low, *ins)


def final_body(count, scaled_ref, weight_ref, rows_ref, *refs):
    ins, out = refs[:count], refs[-1]
    held = jnp.concatenate([r[...] for r in ins], axis=0)
    base = dot(scaled_ref[...], weight_ref[...], 1, 1)
    out[...] = (base + dot(rows_ref[...], held)).astype(BF)


def final_step(scaled, weight, rows, ins, piece, carry):
    at, of = piece
    width = weight.shape[0] // of
    extra = [] if carry is None else [carry]
    return pl.pallas_call(
        functools.partial(final_body, len(ins)),
        grid=(1,),
        in_specs=[
            whole(scaled.shape),
            pl.BlockSpec((width, weight.shape[1]), lambda i: (at, 0)),
            whole(rows.shape),
        ]
        + [whole(x.shape) for x in ins]
        + [pl.BlockSpec(memory_space=pl.ANY)] * len(extra),
        out_specs=pl.BlockSpec((scaled.shape[0], width), lambda i: (0, at)),
        out_shape=jax.ShapeDtypeStruct((scaled.shape[0], weight.shape[0]), BF),
        input_output_aliases={} if carry is None else {3 + len(ins): 0},
        compiler_params=PARAMS,
    )(scaled, weight, rows, *ins, *extra)


def shards(
    acts,
    cotan,
    frozen_key_weight,
    adapter_down_slots,
    adapter_up_slots,
    token_row_jobs,
    slot_owner_jobs,
    loss_token_count,
):
    devices = lax.axis_size("dp")
    parts = lax.axis_size("groups")
    tok_rows = acts.shape[0]
    local = adapter_down_slots.shape[0]
    jobs_all = slot_owner_jobs.shape[0]
    depth = 2 * tok_rows // (local * devices)
    column = devices // PLANES
    ring = column <= 4
    most = local * column * depth
    segment = PLANES * depth
    me = lax.axis_index("dp")
    plane, place = me // column, me % column

    ids = token_row_jobs[:, 0]
    lengths = loss_token_count.astype(F32)
    weights = jnp.mean(lengths) / lengths
    numbers = jnp.arange(jobs_all, dtype=jnp.int32)
    row_weight = jnp.sum(jnp.where(ids[:, None] == numbers[None, :], weights[None, :], 0.0), axis=1)
    row_slot = jnp.sum(
        jnp.where(ids[:, None] == slot_owner_jobs[None, :], numbers[None, :], 0), axis=1
    )
    scaled = (row_weight[:, None] * cotan.astype(F32)).astype(BF)

    planes = jnp.arange(PLANES, dtype=jnp.int32)
    need = jnp.max(
        jnp.sum((row_slot[:, None] // (local * column) == planes[None, :]).astype(jnp.int32), axis=0)
    )
    note = jnp.concatenate([row_slot, jnp.full((128,), need, jnp.int32)])
    notes = lax.all_to_all(
        jnp.broadcast_to(note[None, None], (parts * devices, 1, tok_rows + 128)),
        ("groups", "dp"),
        split_axis=0,
        concat_axis=0,
        tiled=True,
    )[:, 0]
    need_all = jnp.max(notes[:, tok_rows])
    mine = notes[:, :tok_rows].reshape(parts, PLANES, column, tok_rows)
    mine = lax.dynamic_index_in_dim(mine, lax.axis_index("groups"), 0, keepdims=False)
    mine = lax.dynamic_index_in_dim(mine, place, 1, keepdims=False)
    there = planes ^ plane
    slots = jnp.sum(
        jnp.where(there[:, None, None] == planes[None, :, None], mine[None], 0), axis=1
    )
    slots = jnp.concatenate([row_slot[None], slots[1:]], axis=0)
    goal = slots // (local * column)
    earlier = jnp.arange(tok_rows)[None, :] < jnp.arange(tok_rows)[:, None]
    order = jnp.sum(
        ((goal[:, :, None] == goal[:, None, :]) & earlier[None]).astype(jnp.int32), axis=2
    )
    rank = jnp.sum(
        ((slots[:, :, None] == slots[:, None, :]) & earlier[None]).astype(jnp.int32), axis=2
    )
    owner = (slots // local) % column
    if ring:
        owner = owner ^ place
    spot = (
        owner * (local * segment)
        + (slots % local) * segment
        + planes[:, None] * depth
        + rank
    )
    spot = jnp.where(goal == plane, spot, -1)
    side = goal[0] ^ plane

    def across(bufs):
        return [bufs[0]] + [
            lax.ppermute(
                bufs[s],
                "dp",
                [(d, ((d // column) ^ s) * column + d % column) for d in range(devices)],
            )
            for s in range(1, PLANES)
        ]

    blocks = [[p * column + c for c in range(column)] for p in range(PLANES)]

    def within(x):
        return lax.all_to_all(
            x, "dp", split_axis=0, concat_axis=0, tiled=True, axis_index_groups=blocks
        )

    def near(bufs):
        return [bufs[0]] + [
            lax.ppermute(bufs[s], "dp", [(d, d ^ s) for d in range(devices)])
            for s in range(1, column)
        ]

    spread_outs = [local * segment] * column if ring else [column * local * segment]
    owner_outs = [segment] * column if ring else [column * segment]

    def to_owner(bufs):
        width = bufs[0].shape[1]
        if ring:
            return [x.reshape(local, segment, width) for x in near(bufs)]
        x = within(bufs[0]).reshape(column, local, segment, width)
        return [x.transpose(1, 0, 2, 3).reshape(local, column * segment, width)]

    def from_owner(bufs):
        width = bufs[0].shape[2]
        if ring:
            return near([x.reshape(local * segment, width) for x in bufs])
        x = bufs[0].reshape(local, column, segment, width).transpose(1, 0, 2, 3)
        return [within(x.reshape(column * local * segment, width))]

    def run(size):
        total = PLANES * size
        lanes = jnp.arange(total, dtype=jnp.int32)
        code = side * size + order[0]
        out_rows = (lanes[:, None] == code[None, :]).astype(BF)
        back_rows = (code[:, None] == lanes[None, :]).astype(BF)
        kth = jnp.arange(size, dtype=jnp.int32)
        target = jnp.sum(
            jnp.where(
                (order[:, None, :] == kth[None, :, None]) & (spot[:, None, :] >= 0),
                spot[:, None, :] + 1,
                0,
            ),
            axis=2,
        ).reshape(total) - 1
        spots = jnp.arange(PLANES * most, dtype=jnp.int32)
        spread = (spots[:, None] == target[None, :]).astype(BF)
        gather = (target[:, None] == spots[None, :]).astype(BF)
        sizes = [size] * PLANES

        weight = lax.all_gather(frozen_key_weight, "dp", axis=0, tiled=True)

        def outward(x, piece=None):
            there = across(route(out_rows, [x], sizes, piece))
            return to_owner(route(spread, there, spread_outs))

        got_scaled = outward(scaled)
        back_low = back_project(adapter_up_slots, got_scaled)
        low_grad, result = None, None
        for at in range(PIECES):
            piece = (at, PIECES)
            got = outward(acts, piece)
            terms = adapter_terms(back_low, adapter_down_slots, piece, owner_outs)
            home = across(route(gather, from_owner(terms), sizes))
            low_grad = owner_step(back_low, adapter_down_slots, got, piece, low_grad)
            result = final_step(scaled, weight, back_rows, home, piece, result)
        low, grad_a = low_grad
        grad_b = up_gradient(low, got_scaled)
        return result, grad_a, grad_b

    steps = [most * 5 // 8, most * 3 // 4, most]
    which = sum((need_all > s).astype(jnp.int32) for s in steps[:-1])
    return lax.switch(which, [functools.partial(run, s) for s in steps])


def solution(mesh):
    return jax.shard_map(
        shards,
        mesh=mesh,
        in_specs=(
            P(("groups", "dp"), None),
            P(("groups", "dp"), None),
            P("dp", None),
            P(("groups", "dp"), None, None),
            P(("groups", "dp"), None, None),
            P(("groups", "dp"), None),
            P("groups"),
            P("groups"),
        ),
        out_specs=(
            P(("groups", "dp"), None),
            P(("groups", "dp"), None, None),
            P(("groups", "dp"), None, None),
        ),
        check_vma=False,
    )
```

time: 385 us -> 408 us (1.060)
  the two profiles are of different devices: /device:TPU:11 before, /device:TPU:1 now
where the time goes in v1:
time: 408 us; the launch traced here: 410 us
  waiting for transfers between devices  169 us (41%)
  starting transfers between devices  144 us (35%)
  Pallas kernels  46.2 us (11%)
  loops' own time  18 us (4%)
  between operations  16.3 us (4%)
  other arithmetic  9.02 us (2%)
  local copies, waits for them, and re-layouts  8.24 us (2%)
    ppermute x27, starting transfers between devices, across(): lax.ppermute(bufs[s], 'dp', [(d, (d // column ^ s) * column + d % column)...  87.1 us
    ppermute x27, waiting for transfers between devices, across(): lax.ppermute(bufs[s], 'dp', [(d, (d // column ^ s) * column + d % column)...  83.4 us
    ppermute x27, waiting for transfers between devices, near(): lax.ppermute(bufs[s], 'dp', [(d, d ^ s) for d in range(devices)])  82.2 us
    ppermute x27, starting transfers between devices, near(): lax.ppermute(bufs[s], 'dp', [(d, d ^ s) for d in range(devices)])  49.7 us
    another operation x1, loops' own time, shards(): return lax.switch(which, [functools.partial(run, s) for s in steps])  18 us
    pallas_call x14, Pallas kernels, route(): pl.pallas_call(functools.partial(route_body, len(ins)), grid=(1,), in_spe...  17 us
    pallas_call x4, Pallas kernels, final_step(): pl.pallas_call(functools.partial(final_body, len(ins)), grid=(1,), in_spe...  15.4 us
  transfers between devices with their start and end apart: 56, of which 27 were waited for; matrix products, arithmetic and copies ran while one was open for 2% of the time, Pallas kernels for 10%

profile of v1, /device:TPU:1, one launch (start us, length us, event | category | flops | bytes accessed | tf_op | source)
XLA Modules:
  0.0 410.5 jit_solution(11665918834214076173)
XLA Ops:
  10.0 7.1 %all-to-all-start = ((s32[32,1,384]{2,1,0:T(1,128)}), s32[32,1,384]{2,1,0:T(1,128)S(1)}, u32[]{:S(2)}, u32[]{:S(2)}) async-start(s32[32,1,384]{2,1,0:T(1,128)} %broadcast_in_dim.96), calls=%async_computation | async-start | bytes 98304 | tf_op jit(solution)/shard_map/all_to_all | solution.py:226
  26.8 376.5 %conditional.1 = (bf16[2,5120,128]{2,1,0:T(8,128)(2,1)}, bf16[256,5120]{1,0:T(8,128)(2,1)}, bf16[2,128,1024]{2,1,0:T(8,128)(2,1)}) conditional(s32[]{:T(128)} %clamp.11, (bf16[320,1024]{1,0:T(8,128)(2,1)}, s32[4,256]{1,0:T(4,128)S(1)}, s32[4,256,256]{2,1,0:T(8,128)S(1)}, s32[4,256]{1,0:T(4,128)S(1)}, ...), branch_computations={%region_9.11_spmd, %region_11.13_spmd, %region_13.15_spmd} | conditional | flops 2639620 | bytes 160806240 | solution.py:344
  55.6 11.2 %collective-permute-start.97 = (bf16[96,1280]{1,0:T(8,128)(2,1)}, bf16[96,1280]{1,0:T(8,128)(2,1)S(1)}, u32[]{:S(2)}, u32[]{:S(2)}) collective-permute-start(bf16[96,1280]{1,0:T(8,128)(2,1)} %get-tuple-element.202), channel_id=1, source_target_pairs={{0,8},{1,9},{2,10},{3,11},{4,12},{5,13},{6,14},{7,15},{8,0},{9,1},... | collective-permute-start | bytes 737288 | tf_op jit(solution)/shard_map/cond/branch_1_fun/ppermute | solution.py:264
  72.7 21.2 %collective-permute-done.103.refs_2_ = bf16[96,1280]{1,0:T(8,128)(2,1)S(1)} collective-permute-done((bf16[96,1280]{1,0:T(8,128)(2,1)}, bf16[96,1280]{1,0:T(8,128)(2,1)S(1)}, u32[]{:S(2)}, u32[]{:S(2)}) %collective-permute-start.103) | collective-permute-done | bytes 245792 | tf_op jit(solution)/shard_map/cond/branch_1_fun/ppermute | solution.py:264
  93.9 16.4 %collective-permute-start.91 = (bf16[96,1280]{1,0:T(8,128)(2,1)}, bf16[96,1280]{1,0:T(8,128)(2,1)S(1)}, u32[]{:S(2)}, u32[]{:S(2)}) collective-permute-start(bf16[96,1280]{1,0:T(8,128)(2,1)} %get-tuple-element.194), channel_id=1, source_target_pairs={{0,8},{1,9},{2,10},{3,11},{4,12},{5,13},{6,14},{7,15},{8,0},{9,1},... | collective-permute-start | bytes 737288 | tf_op jit(solution)/shard_map/cond/branch_1_fun/ppermute | solution.py:264
  115.4 16.4 %collective-permute-done.97.refs_2_ = bf16[96,1280]{1,0:T(8,128)(2,1)S(1)} collective-permute-done((bf16[96,1280]{1,0:T(8,128)(2,1)}, bf16[96,1280]{1,0:T(8,128)(2,1)S(1)}, u32[]{:S(2)}, u32[]{:S(2)}) %collective-permute-start.97) | collective-permute-done | bytes 245792 | tf_op jit(solution)/shard_map/cond/branch_1_fun/ppermute | solution.py:264
  131.9 17.4 %collective-permute-start.85 = (bf16[96,1280]{1,0:T(8,128)(2,1)}, bf16[96,1280]{1,0:T(8,128)(2,1)S(1)}, u32[]{:S(2)}, u32[]{:S(2)}) collective-permute-start(bf16[96,1280]{1,0:T(8,128)(2,1)} %copy-done.17), channel_id=1, source_target_pairs={{0,8},{1,9},{2,10},{3,11},{4,12},{5,13},{6,14},{7,15},{8,0},{9,1},... | collective-permute-start | bytes 737288 | tf_op jit(solution)/shard_map/cond/branch_1_fun/ppermute | solution.py:264
  152.0 14.4 %collective-permute-start.57 = (bf16[128,1024]{1,0:T(8,128)(2,1)S(1)}, bf16[128,1024]{1,0:T(8,128)(2,1)S(1)}, u32[]{:S(2)}, u32[]{:S(2)}) collective-permute-start(bf16[128,1024]{1,0:T(8,128)(2,1)S(1)} %get-tuple-element.147), channel_id=1, source_target_pairs={{0,1},{1,0},{2,3},{3,2},{4,5},{5,4},{6,7},{7,6},{8,9},{9,8},{10,11... | collective-permute-start | bytes 786440 | tf_op jit(solution)/shard_map/cond/branch_1_fun/ppermute | solution.py:281
  166.4 9.8 %collective-permute-done.91.refs_2_ = bf16[96,1280]{1,0:T(8,128)(2,1)S(1)} collective-permute-done((bf16[96,1280]{1,0:T(8,128)(2,1)}, bf16[96,1280]{1,0:T(8,128)(2,1)S(1)}, u32[]{:S(2)}, u32[]{:S(2)}) %collective-permute-start.91) | collective-permute-done | bytes 245792 | tf_op jit(solution)/shard_map/cond/branch_1_fun/ppermute | solution.py:264
  177.1 9.0 %collective-permute-start.105 = (bf16[128,1280]{1,0:T(8,128)(2,1)S(1)}, bf16[128,1280]{1,0:T(8,128)(2,1)S(1)}, u32[]{:S(2)}, u32[]{:S(2)}) collective-permute-start(bf16[128,1280]{1,0:T(8,128)(2,1)S(1)} %get-tuple-element.213), channel_id=1, source_target_pairs={{0,1},{1,0},{2,3},{3,2},{4,5},{5,4},{6,7},{7,6},{8,9},{9,8},{10,11... | collective-permute-start | bytes 983048 | tf_op jit(solution)/shard_map/cond/branch_1_fun/ppermute | solution.py:281
  186.2 13.8 %collective-permute-done.85.refs_2_ = bf16[96,1280]{1,0:T(8,128)(2,1)S(1)} collective-permute-done((bf16[96,1280]{1,0:T(8,128)(2,1)}, bf16[96,1280]{1,0:T(8,128)(2,1)S(1)}, u32[]{:S(2)}, u32[]{:S(2)}) %collective-permute-start.85) | collective-permute-done | bytes 245792 | tf_op jit(solution)/shard_map/cond/branch_1_fun/ppermute | solution.py:264
  217.5 6.3 %collective-permute-done.107 = bf16[128,1280]{1,0:T(8,128)(2,1)S(1)} collective-permute-done((bf16[128,1280]{1,0:T(8,128)(2,1)S(1)}, bf16[128,1280]{1,0:T(8,128)(2,1)S(1)}, u32[]{:S(2)}, u32[]{:S(2)}) %collective-permute-start.107) | collective-permute-done | bytes 327712 | tf_op jit(solution)/shard_map/cond/branch_1_fun/ppermute | solution.py:281
  231.5 6.3 %collective-permute-done.101 = bf16[128,1280]{1,0:T(8,128)(2,1)S(1)} collective-permute-done((bf16[128,1280]{1,0:T(8,128)(2,1)S(1)}, bf16[128,1280]{1,0:T(8,128)(2,1)S(1)}, u32[]{:S(2)}, u32[]{:S(2)}) %collective-permute-start.101) | collective-permute-done | bytes 327712 | tf_op jit(solution)/shard_map/cond/branch_1_fun/ppermute | solution.py:281
  245.6 6.3 %collective-permute-done.95 = bf16[128,1280]{1,0:T(8,128)(2,1)S(1)} collective-permute-done((bf16[128,1280]{1,0:T(8,128)(2,1)S(1)}, bf16[128,1280]{1,0:T(8,128)(2,1)S(1)}, u32[]{:S(2)}, u32[]{:S(2)}) %collective-permute-start.95) | collective-permute-done | bytes 327712 | tf_op jit(solution)/shard_map/cond/branch_1_fun/ppermute | solution.py:281
  260.2 5.8 %collective-permute-done.89 = bf16[128,1280]{1,0:T(8,128)(2,1)S(1)} collective-permute-done((bf16[128,1280]{1,0:T(8,128)(2,1)S(1)}, bf16[128,1280]{1,0:T(8,128)(2,1)S(1)}, u32[]{:S(2)}, u32[]{:S(2)}) %collective-permute-start.89) | collective-permute-done | bytes 327712 | tf_op jit(solution)/shard_map/cond/branch_1_fun/ppermute | solution.py:281
  269.0 4.7 %collective-permute-done.79.refs_2_ = bf16[128,1280]{1,0:T(8,128)(2,1)S(1)} collective-permute-done((bf16[128,1280]{1,0:T(8,128)(2,1)S(1)}, bf16[128,1280]{1,0:T(8,128)(2,1)S(1)}, u32[]{:S(2)}, u32[]{:S(2)}) %collective-permute-start.79) | collective-permute-done | bytes 327712 | tf_op jit(solution)/shard_map/cond/branch_1_fun/ppermute | solution.py:281
  273.7 6.3 %collective-permute-done.80.refs_3_ = bf16[128,1280]{1,0:T(8,128)(2,1)S(1)} collective-permute-done((bf16[128,1280]{1,0:T(8,128)(2,1)S(1)}, bf16[128,1280]{1,0:T(8,128)(2,1)S(1)}, u32[]{:S(2)}, u32[]{:S(2)}) %collective-permute-start.80) | collective-permute-done | bytes 327712 | tf_op jit(solution)/shard_map/cond/branch_1_fun/ppermute | solution.py:281
  287.7 6.3 %collective-permute-done.74.refs_3_ = bf16[128,1280]{1,0:T(8,128)(2,1)S(1)} collective-permute-done((bf16[128,1280]{1,0:T(8,128)(2,1)S(1)}, bf16[128,1280]{1,0:T(8,128)(2,1)S(1)}, u32[]{:S(2)}, u32[]{:S(2)}) %collective-permute-start.74) | collective-permute-done | bytes 327712 | tf_op jit(solution)/shard_map/cond/branch_1_fun/ppermute | solution.py:281
  301.8 6.3 %collective-permute-done.68.refs_3_ = bf16[128,1280]{1,0:T(8,128)(2,1)S(1)} collective-permute-done((bf16[128,1280]{1,0:T(8,128)(2,1)S(1)}, bf16[128,1280]{1,0:T(8,128)(2,1)S(1)}, u32[]{:S(2)}, u32[]{:S(2)}) %collective-permute-start.68) | collective-permute-done | bytes 327712 | tf_op jit(solution)/shard_map/cond/branch_1_fun/ppermute | solution.py:281
  315.8 6.3 %collective-permute-done.62.refs_3_ = bf16[128,1280]{1,0:T(8,128)(2,1)S(1)} collective-permute-done((bf16[128,1280]{1,0:T(8,128)(2,1)S(1)}, bf16[128,1280]{1,0:T(8,128)(2,1)S(1)}, u32[]{:S(2)}, u32[]{:S(2)}) %collective-permute-start.62) | collective-permute-done | bytes 327712 | tf_op jit(solution)/shard_map/cond/branch_1_fun/ppermute | solution.py:281
  328.7 14.9 %collective-permute-start.70 = (bf16[96,1280]{1,0:T(8,128)(2,1)}, bf16[96,1280]{1,0:T(8,128)(2,1)}, u32[]{:S(2)}, u32[]{:S(2)}) collective-permute-start(bf16[96,1280]{1,0:T(8,128)(2,1)} %get-tuple-element.165), channel_id=1, source_target_pairs={{0,8},{1,9},{2,10},{3,11},{4,12},{5,13},{6,14},{7,15},{8,0},{9,1},... | collective-permute-start | bytes 737288 | tf_op jit(solution)/shard_map/cond/branch_1_fun/ppermute | solution.py:264
  345.4 13.4 %collective-permute-done.76.refs_2_ = bf16[96,1280]{1,0:T(8,128)(2,1)S(1)} collective-permute-done((bf16[96,1280]{1,0:T(8,128)(2,1)S(1)}, bf16[96,1280]{1,0:T(8,128)(2,1)S(1)}, u32[]{:S(2)}, u32[]{:S(2)}) %collective-permute-start.76) | collective-permute-done | bytes 245792 | tf_op jit(solution)/shard_map/cond/branch_1_fun/ppermute | solution.py:264
  359.5 6.0 %collective-permute-start.64 = (bf16[96,1280]{1,0:T(8,128)(2,1)}, bf16[96,1280]{1,0:T(8,128)(2,1)}, u32[]{:S(2)}, u32[]{:S(2)}) collective-permute-start(bf16[96,1280]{1,0:T(8,128)(2,1)} %get-tuple-element.157), channel_id=1, source_target_pairs={{0,8},{1,9},{2,10},{3,11},{4,12},{5,13},{6,14},{7,15},{8,0},{9,1},... | collective-permute-start | bytes 737288 | tf_op jit(solution)/shard_map/cond/branch_1_fun/ppermute | solution.py:264
  390.6 3.9 branch_1_fun.42
  (206 shorter events, 146.2 us)
Async XLA Ops:
  35.6 341.4 %all-gather.6.cloned.1.call-start = ((), (), s32[]{:S(2)}) async-start(), calls=%async_computation.2 | async-start | bytes 11141120 | tf_op jit(solution)/shard_map/cond/branch_1_fun/all_gather | solution.py:322
  44.1 49.8 %collective-permute-start.103 = (bf16[96,1280]{1,0:T(8,128)(2,1)}, bf16[96,1280]{1,0:T(8,128)(2,1)S(1)}, u32[]{:S(2)}, u32[]{:S(2)}) collective-permute-start(bf16[96,1280]{1,0:T(8,128)(2,1)} %get-tuple-element.210), channel_id=1, source_target_pairs={{0,8},{1,9},{2,10},{3,11},{4,12},{5,13},{6,14},{7,15},{8,0},{9,1},... | collective-permute-start | bytes 737288 | tf_op jit(solution)/shard_map/cond/branch_1_fun/ppermute | solution.py:264
  49.3 44.6 %collective-permute-start.104 = (bf16[96,1280]{1,0:T(8,128)(2,1)}, bf16[96,1280]{1,0:T(8,128)(2,1)S(1)}, u32[]{:S(2)}, u32[]{:S(2)}) collective-permute-start(bf16[96,1280]{1,0:T(8,128)(2,1)} %get-tuple-element.211), channel_id=1, source_target_pairs={{0,12},{1,13},{2,14},{3,15},{4,8},{5,9},{6,10},{7,11},{8,4},{9,5},... | collective-permute-start | bytes 737288 | tf_op jit(solution)/shard_map/cond/branch_1_fun/ppermute | solution.py:264
  53.4 59.4 %collective-permute-start.96 = (bf16[96,1280]{1,0:T(8,128)(2,1)}, bf16[96,1280]{1,0:T(8,128)(2,1)S(1)}, u32[]{:S(2)}, u32[]{:S(2)}) collective-permute-start(bf16[96,1280]{1,0:T(8,128)(2,1)} %get-tuple-element.201), channel_id=1, source_target_pairs={{0,4},{1,5},{2,6},{3,7},{4,0},{5,1},{6,2},{7,3},{8,12},{9,13},{10,... | collective-permute-start | bytes 737288 | tf_op jit(solution)/shard_map/cond/branch_1_fun/ppermute | solution.py:264
  55.6 76.3 %collective-permute-start.97 = (bf16[96,1280]{1,0:T(8,128)(2,1)}, bf16[96,1280]{1,0:T(8,128)(2,1)S(1)}, u32[]{:S(2)}, u32[]{:S(2)}) collective-permute-start(bf16[96,1280]{1,0:T(8,128)(2,1)} %get-tuple-element.202), channel_id=1, source_target_pairs={{0,8},{1,9},{2,10},{3,11},{4,12},{5,13},{6,14},{7,15},{8,0},{9,1},... | collective-permute-start | bytes 737288 | tf_op jit(solution)/shard_map/cond/branch_1_fun/ppermute | solution.py:264
  66.8 65.1 %collective-permute-start.98 = (bf16[96,1280]{1,0:T(8,128)(2,1)}, bf16[96,1280]{1,0:T(8,128)(2,1)S(1)}, u32[]{:S(2)}, u32[]{:S(2)}) collective-permute-start(bf16[96,1280]{1,0:T(8,128)(2,1)} %get-tuple-element.203), channel_id=1, source_target_pairs={{0,12},{1,13},{2,14},{3,15},{4,8},{5,9},{6,10},{7,11},{8,4},{9,5},... | collective-permute-start | bytes 737288 | tf_op jit(solution)/shard_map/cond/branch_1_fun/ppermute | solution.py:264
  93.9 58.1 %collective-permute-start.90 = (bf16[96,1280]{1,0:T(8,128)(2,1)}, bf16[96,1280]{1,0:T(8,128)(2,1)S(1)}, u32[]{:S(2)}, u32[]{:S(2)}) collective-permute-start(bf16[96,1280]{1,0:T(8,128)(2,1)} %get-tuple-element.193), channel_id=1, source_target_pairs={{0,4},{1,5},{2,6},{3,7},{4,0},{5,1},{6,2},{7,3},{8,12},{9,13},{10,... | collective-permute-start | bytes 737288 | tf_op jit(solution)/shard_map/cond/branch_1_fun/ppermute | solution.py:264
  93.9 82.3 %collective-permute-start.91 = (bf16[96,1280]{1,0:T(8,128)(2,1)}, bf16[96,1280]{1,0:T(8,128)(2,1)S(1)}, u32[]{:S(2)}, u32[]{:S(2)}) collective-permute-start(bf16[96,1280]{1,0:T(8,128)(2,1)} %get-tuple-element.194), channel_id=1, source_target_pairs={{0,8},{1,9},{2,10},{3,11},{4,12},{5,13},{6,14},{7,15},{8,0},{9,1},... | collective-permute-start | bytes 737288 | tf_op jit(solution)/shard_map/cond/branch_1_fun/ppermute | solution.py:264
  112.8 63.4 %collective-permute-start.92 = (bf16[96,1280]{1,0:T(8,128)(2,1)}, bf16[96,1280]{1,0:T(8,128)(2,1)S(1)}, u32[]{:S(2)}, u32[]{:S(2)}) collective-permute-start(bf16[96,1280]{1,0:T(8,128)(2,1)} %copy-done.18), channel_id=1, source_target_pairs={{0,12},{1,13},{2,14},{3,15},{4,8},{5,9},{6,10},{7,11},{8,4},{9,5},... | collective-permute-start | bytes 737288 | tf_op jit(solution)/shard_map/cond/branch_1_fun/ppermute | solution.py:264
  131.8 45.3 %collective-permute-start.84 = (bf16[96,1280]{1,0:T(8,128)(2,1)}, bf16[96,1280]{1,0:T(8,128)(2,1)S(1)}, u32[]{:S(2)}, u32[]{:S(2)}) collective-permute-start(bf16[96,1280]{1,0:T(8,128)(2,1)} %copy-done.19), channel_id=1, source_target_pairs={{0,4},{1,5},{2,6},{3,7},{4,0},{5,1},{6,2},{7,3},{8,12},{9,13},{10,... | collective-permute-start | bytes 737288 | tf_op jit(solution)/shard_map/cond/branch_1_fun/ppermute | solution.py:264
  131.9 68.2 %collective-permute-start.85 = (bf16[96,1280]{1,0:T(8,128)(2,1)}, bf16[96,1280]{1,0:T(8,128)(2,1)S(1)}, u32[]{:S(2)}, u32[]{:S(2)}) collective-permute-start(bf16[96,1280]{1,0:T(8,128)(2,1)} %copy-done.17), channel_id=1, source_target_pairs={{0,8},{1,9},{2,10},{3,11},{4,12},{5,13},{6,14},{7,15},{8,0},{9,1},... | collective-permute-start | bytes 737288 | tf_op jit(solution)/shard_map/cond/branch_1_fun/ppermute | solution.py:264
  152.0 52.0 %collective-permute-start.57 = (bf16[128,1024]{1,0:T(8,128)(2,1)S(1)}, bf16[128,1024]{1,0:T(8,128)(2,1)S(1)}, u32[]{:S(2)}, u32[]{:S(2)}) collective-permute-start(bf16[128,1024]{1,0:T(8,128)(2,1)S(1)} %get-tuple-element.147), channel_id=1, source_target_pairs={{0,1},{1,0},{2,3},{3,2},{4,5},{5,4},{6,7},{7,6},{8,9},{9,8},{10,11... | collective-permute-start | bytes 786440 | tf_op jit(solution)/shard_map/cond/branch_1_fun/ppermute | solution.py:281
  176.2 28.9 %collective-permute-start.58 = (bf16[128,1024]{1,0:T(8,128)(2,1)S(1)}, bf16[128,1024]{1,0:T(8,128)(2,1)S(1)}, u32[]{:S(2)}, u32[]{:S(2)}) collective-permute-start(bf16[128,1024]{1,0:T(8,128)(2,1)S(1)} %get-tuple-element.148), channel_id=1, source_target_pairs={{0,2},{1,3},{2,0},{3,1},{4,6},{5,7},{6,4},{7,5},{8,10},{9,11},{10,... | collective-permute-start | bytes 786440 | tf_op jit(solution)/shard_map/cond/branch_1_fun/ppermute | solution.py:281
  177.1 33.7 %collective-permute-start.105 = (bf16[128,1280]{1,0:T(8,128)(2,1)S(1)}, bf16[128,1280]{1,0:T(8,128)(2,1)S(1)}, u32[]{:S(2)}, u32[]{:S(2)}) collective-permute-start(bf16[128,1280]{1,0:T(8,128)(2,1)S(1)} %get-tuple-element.213), channel_id=1, source_target_pairs={{0,1},{1,0},{2,3},{3,2},{4,5},{5,4},{6,7},{7,6},{8,9},{9,8},{10,11... | collective-permute-start | bytes 983048 | tf_op jit(solution)/shard_map/cond/branch_1_fun/ppermute | solution.py:281
  210.8 27.1 %collective-permute-start.101 = (bf16[128,1280]{1,0:T(8,128)(2,1)S(1)}, bf16[128,1280]{1,0:T(8,128)(2,1)S(1)}, u32[]{:S(2)}, u32[]{:S(2)}) collective-permute-start(bf16[128,1280]{1,0:T(8,128)(2,1)S(1)} %get-tuple-element.207), channel_id=1, source_target_pairs={{0,3},{1,2},{2,1},{3,0},{4,7},{5,6},{6,5},{7,4},{8,11},{9,10},{10,... | collective-permute-start | bytes 983048 | tf_op jit(solution)/shard_map/cond/branch_1_fun/ppermute | solution.py:281
  224.8 27.1 %collective-permute-start.95 = (bf16[128,1280]{1,0:T(8,128)(2,1)S(1)}, bf16[128,1280]{1,0:T(8,128)(2,1)S(1)}, u32[]{:S(2)}, u32[]{:S(2)}) collective-permute-start(bf16[128,1280]{1,0:T(8,128)(2,1)S(1)} %get-tuple-element.199), channel_id=1, source_target_pairs={{0,3},{1,2},{2,1},{3,0},{4,7},{5,6},{6,5},{7,4},{8,11},{9,10},{10,... | collective-permute-start | bytes 983048 | tf_op jit(solution)/shard_map/cond/branch_1_fun/ppermute | solution.py:281
  315.8 27.8 %collective-permute-start.75 = (bf16[96,1280]{1,0:T(8,128)(2,1)S(1)}, bf16[96,1280]{1,0:T(8,128)(2,1)S(1)}, u32[]{:S(2)}, u32[]{:S(2)}) collective-permute-start(bf16[96,1280]{1,0:T(8,128)(2,1)S(1)} %get-tuple-element.172), channel_id=1, source_target_pairs={{0,4},{1,5},{2,6},{3,7},{4,0},{5,1},{6,2},{7,3},{8,12},{9,13},{10,... | collective-permute-start | bytes 737288 | tf_op jit(solution)/shard_map/cond/branch_1_fun/ppermute | solution.py:264
  322.1 36.7 %collective-permute-start.76 = (bf16[96,1280]{1,0:T(8,128)(2,1)S(1)}, bf16[96,1280]{1,0:T(8,128)(2,1)S(1)}, u32[]{:S(2)}, u32[]{:S(2)}) collective-permute-start(bf16[96,1280]{1,0:T(8,128)(2,1)S(1)} %get-tuple-element.173), channel_id=1, source_target_pairs={{0,8},{1,9},{2,10},{3,11},{4,12},{5,13},{6,14},{7,15},{8,0},{9,1},... | collective-permute-start | bytes 737288 | tf_op jit(solution)/shard_map/cond/branch_1_fun/ppermute | solution.py:264
  322.1 36.7 %collective-permute-start.77 = (bf16[96,1280]{1,0:T(8,128)(2,1)S(1)}, bf16[96,1280]{1,0:T(8,128)(2,1)S(1)}, u32[]{:S(2)}, u32[]{:S(2)}) collective-permute-start(bf16[96,1280]{1,0:T(8,128)(2,1)S(1)} %get-tuple-element.174), channel_id=1, source_target_pairs={{0,12},{1,13},{2,14},{3,15},{4,8},{5,9},{6,10},{7,11},{8,4},{9,5},... | collective-permute-start | bytes 737288 | tf_op jit(solution)/shard_map/cond/branch_1_fun/ppermute | solution.py:264
  327.2 38.3 %collective-permute-start.69 = (bf16[96,1280]{1,0:T(8,128)(2,1)S(1)}, bf16[96,1280]{1,0:T(8,128)(2,1)S(1)}, u32[]{:S(2)}, u32[]{:S(2)}) collective-permute-start(bf16[96,1280]{1,0:T(8,128)(2,1)S(1)} %get-tuple-element.164), channel_id=1, source_target_pairs={{0,4},{1,5},{2,6},{3,7},{4,0},{5,1},{6,2},{7,3},{8,12},{9,13},{10,... | collective-permute-start | bytes 737288 | tf_op jit(solution)/shard_map/cond/branch_1_fun/ppermute | solution.py:264
  328.7 55.9 %collective-permute-start.70 = (bf16[96,1280]{1,0:T(8,128)(2,1)}, bf16[96,1280]{1,0:T(8,128)(2,1)}, u32[]{:S(2)}, u32[]{:S(2)}) collective-permute-start(bf16[96,1280]{1,0:T(8,128)(2,1)} %get-tuple-element.165), channel_id=1, source_target_pairs={{0,8},{1,9},{2,10},{3,11},{4,12},{5,13},{6,14},{7,15},{8,0},{9,1},... | collective-permute-start | bytes 737288 | tf_op jit(solution)/shard_map/cond/branch_1_fun/ppermute | solution.py:264
  343.6 41.1 %collective-permute-start.71 = (bf16[96,1280]{1,0:T(8,128)(2,1)}, bf16[96,1280]{1,0:T(8,128)(2,1)}, u32[]{:S(2)}, u32[]{:S(2)}) collective-permute-start(bf16[96,1280]{1,0:T(8,128)(2,1)} %get-tuple-element.166), channel_id=1, source_target_pairs={{0,12},{1,13},{2,14},{3,15},{4,8},{5,9},{6,10},{7,11},{8,4},{9,5},... | collective-permute-start | bytes 737288 | tf_op jit(solution)/shard_map/cond/branch_1_fun/ppermute | solution.py:264
  358.8 29.8 %collective-permute-start.63 = (bf16[96,1280]{1,0:T(8,128)(2,1)}, bf16[96,1280]{1,0:T(8,128)(2,1)}, u32[]{:S(2)}, u32[]{:S(2)}) collective-permute-start(bf16[96,1280]{1,0:T(8,128)(2,1)} %get-tuple-element.156), channel_id=1, source_target_pairs={{0,4},{1,5},{2,6},{3,7},{4,0},{5,1},{6,2},{7,3},{8,12},{9,13},{10,... | collective-permute-start | bytes 737288 | tf_op jit(solution)/shard_map/cond/branch_1_fun/ppermute | solution.py:264
  359.5 31.0 %collective-permute-start.64 = (bf16[96,1280]{1,0:T(8,128)(2,1)}, bf16[96,1280]{1,0:T(8,128)(2,1)}, u32[]{:S(2)}, u32[]{:S(2)}) collective-permute-start(bf16[96,1280]{1,0:T(8,128)(2,1)} %get-tuple-element.157), channel_id=1, source_target_pairs={{0,8},{1,9},{2,10},{3,11},{4,12},{5,13},{6,14},{7,15},{8,0},{9,1},... | collective-permute-start | bytes 737288 | tf_op jit(solution)/shard_map/cond/branch_1_fun/ppermute | solution.py:264
  (56 other events, 1017.6 us)
Sparse Core Ops, SparseCore 0:
  38.8 160.9 all-gather.5

commit v2 on v1

v2 whole, which is shorter than its diff:
```python
import functools

import jax
import jax.numpy as jnp
from jax import lax
from jax.experimental import pallas as pl
from jax.experimental.pallas import tpu as pltpu
from jax.sharding import PartitionSpec as P

DELTA_MULTIPLIER = 0.25
BF = jnp.bfloat16
F32 = jnp.float32
PLANES = 4
PIECES = 4
PARAMS = pltpu.CompilerParams(vmem_limit_bytes=48 * 1024 * 1024)


def whole(shape):
    zeros = (0,) * len(shape)
    return pl.BlockSpec(shape, lambda i: zeros)


def dot(a, b, ca=1, cb=0):
    return lax.dot_general(a, b, (((ca,), (cb,)), ((), ())), preferred_element_type=F32)


HERE = pl.BlockSpec(memory_space=pl.ANY)
FAR = pl.BlockSpec(memory_space=pltpu.HBM)


def route_body(count, rows_ref, *refs):
    ins, outs = refs[:count], refs[count:]
    held = ins[0][...] if count == 1 else jnp.concatenate([r[...] for r in ins], axis=0)
    moved = dot(rows_ref[...], held).astype(BF)
    at = 0
    for out in outs:
        out[...] = moved[at : at + out.shape[0]]
        at += out.shape[0]


class Line:
    def __init__(self):
        self.last = []

    def call(self, body, operands, in_specs, out_specs, out_shape, aliases=None):
        after = self.last
        first = len(operands)

        def kernel(*refs):
            return body(*refs[:first], *refs[first + len(after) :])

        out = pl.pallas_call(
            kernel,
            grid=(1,),
            in_specs=in_specs + [HERE] * len(after),
            out_specs=out_specs,
            out_shape=out_shape,
            input_output_aliases=aliases or {},
            cost_estimate=pl.CostEstimate(flops=1, bytes_accessed=1, transcendentals=0),
            compiler_params=PARAMS,
        )(*operands, *after)
        self.last = [out[0] if isinstance(out, (list, tuple)) else out]
        return out


def hold_body(ref, out):
    pass


def hold(line, x):
    last = line.last
    out = line.call(hold_body, [x], [FAR], FAR, jax.ShapeDtypeStruct(x.shape, x.dtype), {0: 0})
    line.last = last
    return out


def route(line, rows, ins, outs, piece=None):
    width = ins[0].shape[1]
    specs = [whole(x.shape) for x in ins]
    if piece is not None:
        at, of = piece
        width = width // of
        specs = [pl.BlockSpec((ins[0].shape[0], width), lambda i: (0, at))]
    shapes = [(n, width) for n in outs]
    return line.call(
        functools.partial(route_body, len(ins)),
        [rows, *ins],
        [whole(rows.shape)] + specs,
        [whole(x) for x in shapes],
        [jax.ShapeDtypeStruct(x, BF) for x in shapes],
    )


def job_rows(refs, job):
    return jnp.concatenate([ref[job] for ref in refs], axis=0)


def back_body(count, up_ref, *refs):
    out = refs[count]
    for job in range(up_ref.shape[0]):
        held = job_rows(refs[:count], job)
        out[job] = (DELTA_MULTIPLIER * dot(held, up_ref[job], 1, 1)).astype(BF)


def back_project(line, up, rows):
    local, rank = up.shape[0], up.shape[1]
    shape = (local, sum(x.shape[1] for x in rows), rank)
    return line.call(
        functools.partial(back_body, len(rows)),
        [up, *rows],
        [whole(up.shape)] + [whole(x.shape) for x in rows],
        whole(shape),
        jax.ShapeDtypeStruct(shape, BF),
    )


def term_body(back_ref, down_ref, *outs):
    for job in range(down_ref.shape[0]):
        term = dot(back_ref[job], down_ref[job], 1, 1).astype(BF)
        at = 0
        for out in outs:
            out[job] = term[at : at + out.shape[1]]
            at += out.shape[1]


def adapter_terms(line, back_low, down, piece, outs):
    at, of = piece
    local, width, rank = down.shape
    width = width // of
    shapes = [(local, n, width) for n in outs]
    return line.call(
        term_body,
        [back_low, down],
        [whole(back_low.shape), pl.BlockSpec((local, width, rank), lambda i: (0, at, 0))],
        [whole(x) for x in shapes],
        [jax.ShapeDtypeStruct(x, BF) for x in shapes],
    )


def owner_body(count, carried, back_ref, down_ref, *refs):
    ins, refs = refs[:count], refs[count:]
    if carried:
        low_in, _, low_ref, grad_ref = refs
    else:
        low_ref, grad_ref = refs
    for job in range(down_ref.shape[0]):
        held = job_rows(ins, job)
        low = dot(held, down_ref[job])
        low_ref[job] = low_in[job] + low if carried else low
        grad_ref[job] = dot(held, back_ref[job], 0, 0).astype(BF)


def owner_step(line, back_low, down, rows, piece, carry):
    at, of = piece
    local, width, rank = down.shape
    part = pl.BlockSpec((local, width // of, rank), lambda i: (0, at, 0))
    low_shape = (local, back_low.shape[1], rank)
    extra, extra_specs, aliases = [], [], {}
    if carry is not None:
        extra = list(carry)
        extra_specs = [whole(low_shape), FAR]
        aliases = {2 + len(rows): 0, 3 + len(rows): 1}
    return line.call(
        functools.partial(owner_body, len(rows), carry is not None),
        [back_low, down, *rows, *extra],
        [whole(back_low.shape), part] + [whole(x.shape) for x in rows] + extra_specs,
        [whole(low_shape), part],
        [jax.ShapeDtypeStruct(low_shape, F32), jax.ShapeDtypeStruct(down.shape, BF)],
        aliases,
    )


def up_body(count, low_ref, *refs):
    out = refs[count]
    for job in range(low_ref.shape[0]):
        low = low_ref[job].astype(BF)
        held = job_rows(refs[:count], job)
        out[job] = (DELTA_MULTIPLIER * dot(low, held, 0, 0)).astype(BF)


def up_gradient(line, low, rows):
    shape = (low.shape[0], low.shape[2], rows[0].shape[2])
    return line.call(
        functools.partial(up_body, len(rows)),
        [low, *rows],
        [whole(low.shape)] + [whole(x.shape) for x in rows],
        whole(shape),
        jax.ShapeDtypeStruct(shape, BF),
    )


def final_body(count, scaled_ref, weight_ref, rows_ref, *refs):
    ins, out = refs[:count], refs[-1]
    held = jnp.concatenate([r[...] for r in ins], axis=0)
    weight = weight_ref[...].reshape(-1, weight_ref.shape[-1])
    base = dot(scaled_ref[...], weight, 1, 1)
    out[...] = (base + dot(rows_ref[...], held)).astype(BF)


def final_step(line, scaled, weight, rows, ins, piece, carry):
    at, of = piece
    column, parts, planes, share, deep = weight.shape
    width = column * parts * planes * share // of
    extra = [] if carry is None else [carry]
    return line.call(
        functools.partial(final_body, len(ins)),
        [scaled, weight, rows, *ins, *extra],
        [
            whole(scaled.shape),
            pl.BlockSpec((column, parts, planes // of, share, deep), lambda i: (0, 0, at, 0, 0)),
            whole(rows.shape),
        ]
        + [whole(x.shape) for x in ins]
        + [FAR] * len(extra),
        pl.BlockSpec((scaled.shape[0], width), lambda i: (0, at)),
        jax.ShapeDtypeStruct((scaled.shape[0], width * of), BF),
        {} if carry is None else {3 + len(ins): 0},
    )


def shards(
    acts,
    cotan,
    frozen_key_weight,
    adapter_down_slots,
    adapter_up_slots,
    token_row_jobs,
    slot_owner_jobs,
    loss_token_count,
):
    devices = lax.axis_size("dp")
    parts = lax.axis_size("groups")
    tok_rows = acts.shape[0]
    local = adapter_down_slots.shape[0]
    jobs_all = slot_owner_jobs.shape[0]
    depth = 2 * tok_rows // (local * devices)
    column = devices // PLANES
    ring = column <= 4
    most = local * column * depth
    segment = PLANES * depth
    me = lax.axis_index("dp")
    plane, place = me // column, me % column

    ids = token_row_jobs[:, 0]
    lengths = loss_token_count.astype(F32)
    weights = jnp.mean(lengths) / lengths
    numbers = jnp.arange(jobs_all, dtype=jnp.int32)
    row_weight = jnp.sum(jnp.where(ids[:, None] == numbers[None, :], weights[None, :], 0.0), axis=1)
    row_slot = jnp.sum(
        jnp.where(ids[:, None] == slot_owner_jobs[None, :], numbers[None, :], 0), axis=1
    )
    scaled = (row_weight[:, None] * cotan.astype(F32)).astype(BF)

    planes = jnp.arange(PLANES, dtype=jnp.int32)
    need = jnp.max(
        jnp.sum((row_slot[:, None] // (local * column) == planes[None, :]).astype(jnp.int32), axis=0)
    )
    note = jnp.concatenate([row_slot, jnp.full((128,), need, jnp.int32)])
    notes = lax.all_to_all(
        jnp.broadcast_to(note[None, None], (parts * devices, 1, tok_rows + 128)),
        ("groups", "dp"),
        split_axis=0,
        concat_axis=0,
        tiled=True,
    )[:, 0]
    need_all = jnp.max(notes[:, tok_rows])
    mine = notes[:, :tok_rows].reshape(parts, PLANES, column, tok_rows)
    mine = lax.dynamic_index_in_dim(mine, lax.axis_index("groups"), 0, keepdims=False)
    mine = lax.dynamic_index_in_dim(mine, place, 1, keepdims=False)
    there = planes ^ plane
    slots = jnp.sum(
        jnp.where(there[:, None, None] == planes[None, :, None], mine[None], 0), axis=1
    )
    slots = jnp.concatenate([row_slot[None], slots[1:]], axis=0)
    goal = slots // (local * column)
    earlier = jnp.arange(tok_rows)[None, :] < jnp.arange(tok_rows)[:, None]
    order = jnp.sum(
        ((goal[:, :, None] == goal[:, None, :]) & earlier[None]).astype(jnp.int32), axis=2
    )
    rank = jnp.sum(
        ((slots[:, :, None] == slots[:, None, :]) & earlier[None]).astype(jnp.int32), axis=2
    )
    owner = (slots // local) % column
    if ring:
        owner = owner ^ place
    spot = (
        owner * (local * segment)
        + (slots % local) * segment
        + planes[:, None] * depth
        + rank
    )
    spot = jnp.where(goal == plane, spot, -1)
    own_goal = row_slot // (local * column)
    own_order = jnp.sum(
        ((own_goal[:, None] == own_goal[None, :]) & earlier).astype(jnp.int32), axis=1
    )
    side = own_goal ^ plane

    def across(bufs):
        return [bufs[0]] + [
            lax.ppermute(
                bufs[s],
                "dp",
                [(d, ((d // column) ^ s) * column + d % column) for d in range(devices)],
            )
            for s in range(1, PLANES)
        ]

    blocks = [[p * column + c for c in range(column)] for p in range(PLANES)]

    def within(x):
        return lax.all_to_all(
            x, "dp", split_axis=0, concat_axis=0, tiled=True, axis_index_groups=blocks
        )

    blocks_out = [local * segment] * column if ring else [column * local * segment]
    owner_outs = [segment] * column if ring else [column * segment]

    def near(bufs):
        if not ring:
            return [within(bufs[0])]
        return [bufs[0]] + [
            lax.ppermute(bufs[s], "dp", [(d, d ^ s) for d in range(devices)])
            for s in range(1, column)
        ]

    def at_owner(bufs):
        width = bufs[0].shape[1]
        if ring:
            return [x.reshape(local, segment, width) for x in bufs]
        x = bufs[0].reshape(column, local, segment, width).transpose(1, 0, 2, 3)
        return [x.reshape(local, column * segment, width)]

    def from_owner(bufs):
        width = bufs[0].shape[2]
        if ring:
            return [x.reshape(local * segment, width) for x in bufs]
        x = bufs[0].reshape(local, column, segment, width).transpose(1, 0, 2, 3)
        return [x.reshape(column * local * segment, width)]

    stripes = [[p * column + c for p in range(PLANES)] for c in range(column)]

    share = frozen_key_weight.shape[0] // parts
    deep = frozen_key_weight.shape[1]
    own_share = lax.dynamic_slice_in_dim(
        frozen_key_weight, lax.axis_index("groups") * share, share, 0
    )

    def shape_weight(w):
        w = w.reshape(column, parts, PLANES, share, deep)
        if share % 16 == 0:
            return w
        w = w.transpose(2, 0, 1, 3, 4)
        return w.reshape(1, 1, PLANES, column * parts * share, deep)

    def outward(size):
        lanes = jnp.arange(PLANES * size, dtype=jnp.int32)
        code = side * size + own_order
        return (lanes[:, None] == code[None, :]).astype(BF), (
            code[:, None] == lanes[None, :]
        ).astype(BF)

    def inward(size):
        kth = jnp.arange(size, dtype=jnp.int32)
        target = jnp.sum(
            jnp.where(
                (order[:, None, :] == kth[None, :, None]) & (spot[:, None, :] >= 0),
                spot[:, None, :] + 1,
                0,
            ),
            axis=2,
        ).reshape(PLANES * size) - 1
        spots = jnp.arange(PLANES * most, dtype=jnp.int32)
        return (spots[:, None] == target[None, :]).astype(BF), (
            target[:, None] == spots[None, :]
        ).astype(BF)

    scaled_z = across(route(Line(), outward(most)[0], [scaled], [most] * PLANES))
    scaled_sent = route(Line(), inward(most)[0], scaled_z, blocks_out)

    def run(size):
        out_rows, back_rows = outward(size)
        spread, gather = inward(size)
        sizes = [size] * PLANES
        line = Line()
        pieces = [(at, PIECES) for at in range(PIECES)]

        def leave(at):
            return route(line, out_rows, [acts], sizes, pieces[at])

        def spread_out(bufs):
            return route(line, spread, bufs, blocks_out)

        def term(at):
            return from_owner(
                adapter_terms(line, back_low, adapter_down_slots, pieces[at], owner_outs)
            )

        def home(came):
            return route(line, gather, came, sizes)

        def own(at, got, carry):
            return owner_step(line, back_low, adapter_down_slots, at_owner(got), pieces[at], carry)

        def final(at, carry):
            return final_step(line, scaled, weight, back_rows, terms_z[at], pieces[at], carry)

        def fly(far, close):
            far, close = across(far) if far else [], near(close)
            return far, close, far[1:] + (close[1:] if ring else close)

        acts_z, acts_o, acts_x, terms_z, terms_x = {}, {}, {}, {}, {}
        weight = lax.all_gather(
            own_share, "dp", axis=0, tiled=True, axis_index_groups=stripes
        )
        out = leave(0)
        acts_z[0], got_scaled, landed = fly(out, scaled_sent)
        out = leave(1)
        line.last += landed
        got_scaled = at_owner(got_scaled)
        back_low = back_project(line, adapter_up_slots, got_scaled)
        terms_o = term(0)

        acts_z[1], terms_x[0], landed = fly(out, terms_o)
        acts_o[0] = spread_out(acts_z[0])
        terms_o = term(1)
        line.last += landed
        back = home(terms_x[0])

        terms_z[0], terms_x[1], landed = fly(back, terms_o)
        acts_o[1] = spread_out(acts_z[1])
        out = leave(2)
        weight = lax.all_gather(hold(line, weight), "groups", axis=0, tiled=True)
        line.last += landed
        back = home(terms_x[1])

        terms_z[1], acts_x[0], landed = fly(back, acts_o[0])
        terms_o = term(2)
        line.last += landed
        carry = own(0, acts_x[0], None)

        acts_z[2], terms_x[2], landed = fly(out, terms_o)
        out = leave(3)
        weight = lax.all_gather(
            hold(line, weight), "dp", axis=0, tiled=True, axis_index_groups=blocks
        )
        line.last += landed
        back = home(terms_x[2])
        terms_o = term(3)

        terms_z[2], acts_x[1], landed = fly(back, acts_o[1])
        acts_o[2] = spread_out(acts_z[2])
        line.last += landed
        carry = own(1, acts_x[1], carry)

        acts_z[3], terms_x[3], landed = fly(out, terms_o)
        line.last += landed
        back = home(terms_x[3])
        acts_o[3] = spread_out(acts_z[3])

        terms_z[3], acts_x[2], landed = fly(back, acts_o[2])
        weight = shape_weight(weight)
        result = final(0, None)
        result = final(1, result)
        line.last += landed
        carry = own(2, acts_x[2], carry)

        _, acts_x[3], landed = fly([], acts_o[3])
        result = final(2, result)
        result = final(3, result)
        line.last += landed
        low, grad_a = own(3, acts_x[3], carry)
        grad_b = up_gradient(line, low, got_scaled)
        return result, grad_a, grad_b

    steps = [most * 5 // 8, most * 3 // 4, most]
    which = sum((need_all > s).astype(jnp.int32) for s in steps[:-1])
    return lax.switch(which, [functools.partial(run, s) for s in steps])


def solution(mesh):
    return jax.shard_map(
        shards,
        mesh=mesh,
        in_specs=(
            P(("groups", "dp"), None),
            P(("groups", "dp"), None),
            P("dp", None),
            P(("groups", "dp"), None, None),
            P(("groups", "dp"), None, None),
            P(("groups", "dp"), None),
            P("groups"),
            P("groups"),
        ),
        out_specs=(
            P(("groups", "dp"), None),
            P(("groups", "dp"), None, None),
            P(("groups", "dp"), None, None),
        ),
        check_vma=False,
    )
```

time: 408 us -> 385 us (0.944)
  the two profiles are of different devices: /device:TPU:1 before, /device:TPU:15 now
where the time goes in v2:
time: 385 us; the launch traced here: 378 us
  waiting for transfers between devices  190 us (49%)
  starting transfers between devices  77.3 us (20%)
  Pallas kernels  38.6 us (10%)
  local copies, waits for them, and re-layouts  30.8 us (8%)
  between operations  16.4 us (4%)
  loops' own time  15.6 us (4%)
  other arithmetic  9.04 us (2%)
    ppermute x27, waiting for transfers between devices, across(): lax.ppermute(bufs[s], 'dp', [(d, (d // column ^ s) * column + d % column)...  131 us
    ppermute x27, waiting for transfers between devices, near(): lax.ppermute(bufs[s], 'dp', [(d, d ^ s) for d in range(devices)])  57.9 us
    ppermute x27, starting transfers between devices, near(): lax.ppermute(bufs[s], 'dp', [(d, d ^ s) for d in range(devices)])  43.8 us
    pallas_call x30, Pallas kernels, call(): pl.pallas_call(kernel, grid=(1,), in_specs=in_specs + [HERE] * len(after)...  38.6 us
    cond x166, local copies, waits for them, and re-layouts  27.7 us
    ppermute x27, starting transfers between devices, across(): lax.ppermute(bufs[s], 'dp', [(d, (d // column ^ s) * column + d % column)...  27 us
    another operation x1, loops' own time, shards(): return lax.switch(which, [functools.partial(run, s) for s in steps])  15.6 us
  transfers between devices with their start and end apart: 58, of which 26 were waited for; matrix products, arithmetic and copies ran while one was open for 1% of the time, Pallas kernels for 9%

profile of v2, /device:TPU:15, one launch (start us, length us, event | category | flops | bytes accessed | tf_op | source)
XLA Modules:
  0.0 378.1 jit_solution(17037548789848026800)
XLA Ops:
  15.0 6.3 %all-to-all-start = ((s32[32,1,384]{2,1,0:T(1,128)}), s32[32,1,384]{2,1,0:T(1,128)S(1)}, u32[]{:S(2)}, u32[]{:S(2)}) async-start(s32[32,1,384]{2,1,0:T(1,128)} %broadcast_in_dim.94), calls=%async_computation | async-start | bytes 98304 | tf_op jit(solution)/shard_map/all_to_all | solution.py:259
  29.0 4.3 %collective-permute-done.153.refs_2_ = bf16[128,1024]{1,0:T(8,128)(2,1)S(1)} collective-permute-done((bf16[128,1024]{1,0:T(8,128)(2,1)S(1)}, bf16[128,1024]{1,0:T(8,128)(2,1)S(1)}, u32[]{:S(2)}, u32[]{:S(2)}) %collective-permute-start.153) | collective-permute-done | bytes 262176 | tf_op jit(solution)/shard_map/ppermute | solution.py:301
  36.6 10.7 %collective-permute-done.155.refs_4_ = bf16[128,1024]{1,0:T(8,128)(2,1)S(1)} collective-permute-done((bf16[128,1024]{1,0:T(8,128)(2,1)S(1)}, bf16[128,1024]{1,0:T(8,128)(2,1)S(1)}, u32[]{:S(2)}, u32[]{:S(2)}) %collective-permute-start.155) | collective-permute-done | bytes 262176 | tf_op jit(solution)/shard_map/ppermute | solution.py:301
  48.9 321.3 %conditional.1 = (bf16[2,5120,128]{2,1,0:T(8,128)(2,1)}, bf16[256,5120]{1,0:T(8,128)(2,1)}, bf16[2,128,1024]{2,1,0:T(8,128)(2,1)S(1)}) conditional(s32[]{:T(128)} %clamp.11, (bf16[320,1024]{1,0:T(8,128)(2,1)S(1)}, s32[256]{0:T(256)S(1)}, s32[256]{0:T(256)S(1)}, s32[4,256]{1,0:T(4,128)S(1)}, s32[4,256]{1,0:T(4,128)S(1)}, ...), branch_computations={%region_11.13_spmd, %region_13.15_spmd, %region_15.17_spmd} | conditional | flops 2099743 | bytes 324705600 | solution.py:478
  64.1 9.2 %collective-permute-done.57.refs_6_.refs_2_ = bf16[96,1280]{1,0:T(8,128)(2,1)S(1)} collective-permute-done((bf16[96,1280]{1,0:T(8,128)(2,1)S(1)}, bf16[96,1280]{1,0:T(8,128)(2,1)S(1)}, u32[]{:S(2)}, u32[]{:S(2)}) %collective-permute-start.57) | collective-permute-done | bytes 245792 | tf_op jit(solution)/shard_map/cond/branch_1_fun/ppermute | solution.py:301
  77.8 21.5 %collective-permute-done.59.refs_8_.refs_4_ = bf16[96,1280]{1,0:T(8,128)(2,1)S(1)} collective-permute-done((bf16[96,1280]{1,0:T(8,128)(2,1)S(1)}, bf16[96,1280]{1,0:T(8,128)(2,1)S(1)}, u32[]{:S(2)}, u32[]{:S(2)}) %collective-permute-start.59) | collective-permute-done | bytes 245792 | tf_op jit(solution)/shard_map/cond/branch_1_fun/ppermute | solution.py:301
  102.2 4.7 %collective-permute-start.60 = (bf16[128,1280]{1,0:T(8,128)(2,1)S(1)}, bf16[128,1280]{1,0:T(8,128)(2,1)S(1)}, u32[]{:S(2)}, u32[]{:S(2)}) collective-permute-start(bf16[128,1280]{1,0:T(8,128)(2,1)S(1)} %bitcast.225), channel_id=1, source_target_pairs={{0,1},{1,0},{2,3},{3,2},{4,5},{5,4},{6,7},{7,6},{8,9},{9,8},{10,11... | collective-permute-start | bytes 983048 | tf_op jit(solution)/shard_map/cond/branch_1_fun/ppermute | solution.py:323
  113.8 6.8 %collective-permute-done.52.refs_7_.refs_3_ = bf16[96,1280]{1,0:T(8,128)(2,1)S(1)} collective-permute-done((bf16[96,1280]{1,0:T(8,128)(2,1)}, bf16[96,1280]{1,0:T(8,128)(2,1)S(1)}, u32[]{:S(2)}, u32[]{:S(2)}) %collective-permute-start.52) | collective-permute-done | bytes 245792 | tf_op jit(solution)/shard_map/cond/branch_1_fun/ppermute | solution.py:301
  120.6 5.8 %collective-permute-done.53.refs_8_.refs_4_ = bf16[96,1280]{1,0:T(8,128)(2,1)S(1)} collective-permute-done((bf16[96,1280]{1,0:T(8,128)(2,1)}, bf16[96,1280]{1,0:T(8,128)(2,1)S(1)}, u32[]{:S(2)}, u32[]{:S(2)}) %collective-permute-start.53) | collective-permute-done | bytes 245792 | tf_op jit(solution)/shard_map/cond/branch_1_fun/ppermute | solution.py:301
  139.4 5.3 %collective-permute-done.67.refs_3_.refs_10_ = bf16[128,1280]{1,0:T(8,128)(2,1)S(1)} collective-permute-done((bf16[128,1280]{1,0:T(8,128)(2,1)}, bf16[128,1280]{1,0:T(8,128)(2,1)S(1)}, u32[]{:S(2)}, u32[]{:S(2)}) %collective-permute-start.67) | collective-permute-done | bytes 327712 | tf_op jit(solution)/shard_map/cond/branch_1_fun/ppermute | solution.py:323
  146.7 6.6 %collective-permute-done.68.refs_4_.refs_11_ = bf16[128,1280]{1,0:T(8,128)(2,1)S(1)} collective-permute-done((bf16[128,1280]{1,0:T(8,128)(2,1)}, bf16[128,1280]{1,0:T(8,128)(2,1)S(1)}, u32[]{:S(2)}, u32[]{:S(2)}) %collective-permute-start.68) | collective-permute-done | bytes 327712 | tf_op jit(solution)/shard_map/cond/branch_1_fun/ppermute | solution.py:323
  153.9 14.9 %collective-permute-done.71.refs_8_.refs_6_ = bf16[96,1280]{1,0:T(8,128)(2,1)S(1)} collective-permute-done((bf16[96,1280]{1,0:T(8,128)(2,1)}, bf16[96,1280]{1,0:T(8,128)(2,1)S(1)}, u32[]{:S(2)}, u32[]{:S(2)}) %collective-permute-start.71) | collective-permute-done | bytes 245792 | tf_op jit(solution)/shard_map/cond/branch_1_fun/ppermute | solution.py:301
  172.8 4.3 %collective-permute-done.72.refs_7_.refs_4_ = bf16[96,1280]{1,0:T(8,128)(2,1)S(1)} collective-permute-done((bf16[96,1280]{1,0:T(8,128)(2,1)S(1)}, bf16[96,1280]{1,0:T(8,128)(2,1)S(1)}, u32[]{:S(2)}, u32[]{:S(2)}) %collective-permute-start.72) | collective-permute-done | bytes 245792 | tf_op jit(solution)/shard_map/cond/branch_1_fun/ppermute | solution.py:301
  180.3 12.8 %collective-permute-done.74.refs_9_.refs_6_ = bf16[96,1280]{1,0:T(8,128)(2,1)S(1)} collective-permute-done((bf16[96,1280]{1,0:T(8,128)(2,1)S(1)}, bf16[96,1280]{1,0:T(8,128)(2,1)S(1)}, u32[]{:S(2)}, u32[]{:S(2)}) %collective-permute-start.74) | collective-permute-done | bytes 245792 | tf_op jit(solution)/shard_map/cond/branch_1_fun/ppermute | solution.py:301
  206.5 5.3 %collective-permute-start.75 = (bf16[128,1280]{1,0:T(8,128)(2,1)}, bf16[128,1280]{1,0:T(8,128)(2,1)S(1)}, u32[]{:S(2)}, u32[]{:S(2)}) collective-permute-start(bf16[128,1280]{1,0:T(8,128)(2,1)} %bitcast.195), channel_id=1, source_target_pairs={{0,1},{1,0},{2,3},{3,2},{4,5},{5,4},{6,7},{7,6},{8,9},{9,8},{10,11... | collective-permute-start | bytes 983048 | tf_op jit(solution)/shard_map/cond/branch_1_fun/ppermute | solution.py:323
  211.8 9.2 %collective-permute-start.77 = (bf16[128,1280]{1,0:T(8,128)(2,1)}, bf16[128,1280]{1,0:T(8,128)(2,1)S(1)}, u32[]{:S(2)}, u32[]{:S(2)}) collective-permute-start(bf16[128,1280]{1,0:T(8,128)(2,1)} %bitcast.193), channel_id=1, source_target_pairs={{0,3},{1,2},{2,1},{3,0},{4,7},{5,6},{6,5},{7,4},{8,11},{9,10},{10,... | collective-permute-start | bytes 983048 | tf_op jit(solution)/shard_map/cond/branch_1_fun/ppermute | solution.py:323
  228.5 8.1 %collective-permute-done.77.refs_4_.refs_11_ = bf16[128,1280]{1,0:T(8,128)(2,1)S(1)} collective-permute-done((bf16[128,1280]{1,0:T(8,128)(2,1)}, bf16[128,1280]{1,0:T(8,128)(2,1)S(1)}, u32[]{:S(2)}, u32[]{:S(2)}) %collective-permute-start.77) | collective-permute-done | bytes 327712 | tf_op jit(solution)/shard_map/cond/branch_1_fun/ppermute | solution.py:323
  238.5 13.3 %collective-permute-done.85.refs_13_ = bf16[128,1280]{1,0:T(8,128)(2,1)S(1)} collective-permute-done((bf16[128,1280]{1,0:T(8,128)(2,1)}, bf16[128,1280]{1,0:T(8,128)(2,1)S(1)}, u32[]{:S(2)}, u32[]{:S(2)}) %collective-permute-start.85) | collective-permute-done | bytes 327712 | tf_op jit(solution)/shard_map/cond/branch_1_fun/ppermute | solution.py:323
  255.4 9.3 %collective-permute-done.86.refs_14_ = bf16[128,1280]{1,0:T(8,128)(2,1)S(1)} collective-permute-done((bf16[128,1280]{1,0:T(8,128)(2,1)S(1)}, bf16[128,1280]{1,0:T(8,128)(2,1)S(1)}, u32[]{:S(2)}, u32[]{:S(2)}) %collective-permute-start.86) | collective-permute-done | bytes 327712 | tf_op jit(solution)/shard_map/cond/branch_1_fun/ppermute | solution.py:323
  273.2 11.9 %collective-permute-done.88.refs_10_.refs_5_ = bf16[96,1280]{1,0:T(8,128)(2,1)S(1)} collective-permute-done((bf16[96,1280]{1,0:T(8,128)(2,1)S(1)}, bf16[96,1280]{1,0:T(8,128)(2,1)S(1)}, u32[]{:S(2)}, u32[]{:S(2)}) %collective-permute-start.88) | collective-permute-done | bytes 245792 | tf_op jit(solution)/shard_map/cond/branch_1_fun/ppermute | solution.py:301
  285.7 5.8 %collective-permute-done.89.refs_11_.refs_6_ = bf16[96,1280]{1,0:T(8,128)(2,1)S(1)} collective-permute-done((bf16[96,1280]{1,0:T(8,128)(2,1)S(1)}, bf16[96,1280]{1,0:T(8,128)(2,1)S(1)}, u32[]{:S(2)}, u32[]{:S(2)}) %collective-permute-start.89) | collective-permute-done | bytes 245792 | tf_op jit(solution)/shard_map/cond/branch_1_fun/ppermute | solution.py:301
  304.8 4.3 %collective-permute-done.97.refs_13_ = bf16[128,1280]{1,0:T(8,128)(2,1)S(1)} collective-permute-done((bf16[128,1280]{1,0:T(8,128)(2,1)S(1)}, bf16[128,1280]{1,0:T(8,128)(2,1)S(1)}, u32[]{:S(2)}, u32[]{:S(2)}) %collective-permute-start.97) | collective-permute-done | bytes 327712 | tf_op jit(solution)/shard_map/cond/branch_1_fun/ppermute | solution.py:323
  312.7 9.0 %collective-permute-done.98.refs_14_ = bf16[128,1280]{1,0:T(8,128)(2,1)S(1)} collective-permute-done((bf16[128,1280]{1,0:T(8,128)(2,1)S(1)}, bf16[128,1280]{1,0:T(8,128)(2,1)S(1)}, u32[]{:S(2)}, u32[]{:S(2)}) %collective-permute-start.98) | collective-permute-done | bytes 327712 | tf_op jit(solution)/shard_map/cond/branch_1_fun/ppermute | solution.py:323
  339.6 7.2 %collective-permute-done.95.refs_11_.refs_6_ = bf16[96,1280]{1,0:T(8,128)(2,1)} collective-permute-done((bf16[96,1280]{1,0:T(8,128)(2,1)}, bf16[96,1280]{1,0:T(8,128)(2,1)}, u32[]{:S(2)}, u32[]{:S(2)}) %collective-permute-start.95) | collective-permute-done | bytes 245792 | tf_op jit(solution)/shard_map/cond/branch_1_fun/ppermute | solution.py:301
  (341 shorter events, 149.3 us)
Async XLA Ops:
  54.0 79.5 %all-gather.16.cloned.1.call-start = ((), (), s32[]{:S(2)}) async-start(), calls=%async_computation.4 | async-start | bytes 1638400 | tf_op jit(solution)/shard_map/cond/branch_1_fun/all_gather | solution.py:413
  54.9 142.5 %all-gather.18.cloned.1.call-start = ((), (), s32[]{:S(2)}) async-start(), calls=%async_computation.5 | async-start | bytes 3932160 | tf_op jit(solution)/shard_map/cond/branch_1_fun/all_gather | solution.py:433
  54.9 44.3 %collective-permute-start.54 = (bf16[128,1024]{1,0:T(8,128)(2,1)}, bf16[128,1024]{1,0:T(8,128)(2,1)S(1)}, u32[]{:S(2)}, u32[]{:S(2)}) collective-permute-start(bf16[128,1024]{1,0:T(8,128)(2,1)} %get-tuple-element.177), channel_id=1, source_target_pairs={{0,1},{1,0},{2,3},{3,2},{4,5},{5,4},{6,7},{7,6},{8,9},{9,8},{10,11... | collective-permute-start | bytes 786440 | tf_op jit(solution)/shard_map/cond/branch_1_fun/ppermute | solution.py:323
  56.4 43.4 %collective-permute-start.55 = (bf16[128,1024]{1,0:T(8,128)(2,1)}, bf16[128,1024]{1,0:T(8,128)(2,1)S(1)}, u32[]{:S(2)}, u32[]{:S(2)}) collective-permute-start(bf16[128,1024]{1,0:T(8,128)(2,1)} %get-tuple-element.178), channel_id=1, source_target_pairs={{0,2},{1,3},{2,0},{3,1},{4,6},{5,7},{6,4},{7,5},{8,10},{9,11},{10,... | collective-permute-start | bytes 786440 | tf_op jit(solution)/shard_map/cond/branch_1_fun/ppermute | solution.py:323
  56.7 43.1 %collective-permute-start.56 = (bf16[128,1024]{1,0:T(8,128)(2,1)}, bf16[128,1024]{1,0:T(8,128)(2,1)S(1)}, u32[]{:S(2)}, u32[]{:S(2)}) collective-permute-start(bf16[128,1024]{1,0:T(8,128)(2,1)} %get-tuple-element.179), channel_id=1, source_target_pairs={{0,3},{1,2},{2,1},{3,0},{4,7},{5,6},{6,5},{7,4},{8,11},{9,10},{10,... | collective-permute-start | bytes 786440 | tf_op jit(solution)/shard_map/cond/branch_1_fun/ppermute | solution.py:323
  73.3 25.9 %collective-permute-start.59 = (bf16[96,1280]{1,0:T(8,128)(2,1)S(1)}, bf16[96,1280]{1,0:T(8,128)(2,1)S(1)}, u32[]{:S(2)}, u32[]{:S(2)}) collective-permute-start(bf16[96,1280]{1,0:T(8,128)(2,1)S(1)} %get-tuple-element.182), channel_id=1, source_target_pairs={{0,12},{1,13},{2,14},{3,15},{4,8},{5,9},{6,10},{7,11},{8,4},{9,5},... | collective-permute-start | bytes 737288 | tf_op jit(solution)/shard_map/cond/branch_1_fun/ppermute | solution.py:301
  77.5 29.5 %collective-permute-start.51 = (bf16[96,1280]{1,0:T(8,128)(2,1)S(1)}, bf16[96,1280]{1,0:T(8,128)(2,1)S(1)}, u32[]{:S(2)}, u32[]{:S(2)}) collective-permute-start(bf16[96,1280]{1,0:T(8,128)(2,1)S(1)} %get-tuple-element.172), channel_id=1, source_target_pairs={{0,4},{1,5},{2,6},{3,7},{4,0},{5,1},{6,2},{7,3},{8,12},{9,13},{10,... | collective-permute-start | bytes 737288 | tf_op jit(solution)/shard_map/cond/branch_1_fun/ppermute | solution.py:301
  99.3 27.1 %collective-permute-start.53 = (bf16[96,1280]{1,0:T(8,128)(2,1)}, bf16[96,1280]{1,0:T(8,128)(2,1)S(1)}, u32[]{:S(2)}, u32[]{:S(2)}) collective-permute-start(bf16[96,1280]{1,0:T(8,128)(2,1)} %get-tuple-element.174), channel_id=1, source_target_pairs={{0,12},{1,13},{2,14},{3,15},{4,8},{5,9},{6,10},{7,11},{8,4},{9,5},... | collective-permute-start | bytes 737288 | tf_op jit(solution)/shard_map/cond/branch_1_fun/ppermute | solution.py:301
  101.9 24.5 %collective-permute-start.61 = (bf16[128,1280]{1,0:T(8,128)(2,1)S(1)}, bf16[128,1280]{1,0:T(8,128)(2,1)S(1)}, u32[]{:S(2)}, u32[]{:S(2)}) collective-permute-start(bf16[128,1280]{1,0:T(8,128)(2,1)S(1)} %bitcast.227), channel_id=1, source_target_pairs={{0,2},{1,3},{2,0},{3,1},{4,6},{5,7},{6,4},{7,5},{8,10},{9,11},{10,... | collective-permute-start | bytes 983048 | tf_op jit(solution)/shard_map/cond/branch_1_fun/ppermute | solution.py:323
  136.0 189.1 %all-gather.20.cloned.1.call-start = ((), (), s32[]{:S(2)}) async-start(), calls=%async_computation.6 | async-start | bytes 13107200 | tf_op jit(solution)/shard_map/cond/branch_1_fun/all_gather | solution.py:444
  138.9 31.1 %collective-permute-start.63 = (bf16[128,1280]{1,0:T(8,128)(2,1)}, bf16[128,1280]{1,0:T(8,128)(2,1)S(1)}, u32[]{:S(2)}, u32[]{:S(2)}) collective-permute-start(bf16[128,1280]{1,0:T(8,128)(2,1)} %copy-done.155), channel_id=1, source_target_pairs={{0,1},{1,0},{2,3},{3,2},{4,5},{5,4},{6,7},{7,6},{8,9},{9,8},{10,11... | collective-permute-start | bytes 983048 | tf_op jit(solution)/shard_map/cond/branch_1_fun/ppermute | solution.py:323
  211.8 24.8 %collective-permute-start.77 = (bf16[128,1280]{1,0:T(8,128)(2,1)}, bf16[128,1280]{1,0:T(8,128)(2,1)S(1)}, u32[]{:S(2)}, u32[]{:S(2)}) collective-permute-start(bf16[128,1280]{1,0:T(8,128)(2,1)} %bitcast.193), channel_id=1, source_target_pairs={{0,3},{1,2},{2,1},{3,0},{4,7},{5,6},{6,5},{7,4},{8,11},{9,10},{10,... | collective-permute-start | bytes 983048 | tf_op jit(solution)/shard_map/cond/branch_1_fun/ppermute | solution.py:323
  224.3 27.5 %collective-permute-start.85 = (bf16[128,1280]{1,0:T(8,128)(2,1)}, bf16[128,1280]{1,0:T(8,128)(2,1)S(1)}, u32[]{:S(2)}, u32[]{:S(2)}) collective-permute-start(bf16[128,1280]{1,0:T(8,128)(2,1)} %copy-done.134), channel_id=1, source_target_pairs={{0,2},{1,3},{2,0},{3,1},{4,6},{5,7},{6,4},{7,5},{8,10},{9,11},{10,... | collective-permute-start | bytes 983048 | tf_op jit(solution)/shard_map/cond/branch_1_fun/ppermute | solution.py:323
  224.6 40.1 %collective-permute-start.86 = (bf16[128,1280]{1,0:T(8,128)(2,1)S(1)}, bf16[128,1280]{1,0:T(8,128)(2,1)S(1)}, u32[]{:S(2)}, u32[]{:S(2)}) collective-permute-start(bf16[128,1280]{1,0:T(8,128)(2,1)S(1)} %copy-done.131), channel_id=1, source_target_pairs={{0,3},{1,2},{2,1},{3,0},{4,7},{5,6},{6,5},{7,4},{8,11},{9,10},{10,... | collective-permute-start | bytes 983048 | tf_op jit(solution)/shard_map/cond/branch_1_fun/ppermute | solution.py:323
  227.9 38.2 %collective-permute-start.90 = (bf16[96,1280]{1,0:T(8,128)(2,1)}, bf16[96,1280]{1,0:T(8,128)(2,1)S(1)}, u32[]{:S(2)}, u32[]{:S(2)}) collective-permute-start(bf16[96,1280]{1,0:T(8,128)(2,1)} %copy-done.182), channel_id=1, source_target_pairs={{0,4},{1,5},{2,6},{3,7},{4,0},{5,1},{6,2},{7,3},{8,12},{9,13},{10,... | collective-permute-start | bytes 737288 | tf_op jit(solution)/shard_map/cond/branch_1_fun/ppermute | solution.py:301
  227.9 41.2 %collective-permute-start.91 = (bf16[96,1280]{1,0:T(8,128)(2,1)}, bf16[96,1280]{1,0:T(8,128)(2,1)S(1)}, u32[]{:S(2)}, u32[]{:S(2)}) collective-permute-start(bf16[96,1280]{1,0:T(8,128)(2,1)} %copy-done.181), channel_id=1, source_target_pairs={{0,8},{1,9},{2,10},{3,11},{4,12},{5,13},{6,14},{7,15},{8,0},{9,1},... | collective-permute-start | bytes 737288 | tf_op jit(solution)/shard_map/cond/branch_1_fun/ppermute | solution.py:301
  236.6 33.8 %collective-permute-start.92 = (bf16[96,1280]{1,0:T(8,128)(2,1)}, bf16[96,1280]{1,0:T(8,128)(2,1)S(1)}, u32[]{:S(2)}, u32[]{:S(2)}) collective-permute-start(bf16[96,1280]{1,0:T(8,128)(2,1)} %copy-done.180), channel_id=1, source_target_pairs={{0,12},{1,13},{2,14},{3,15},{4,8},{5,9},{6,10},{7,11},{8,4},{9,5},... | collective-permute-start | bytes 737288 | tf_op jit(solution)/shard_map/cond/branch_1_fun/ppermute | solution.py:301
  264.7 26.8 %collective-permute-start.82 = (bf16[128,1280]{1,0:T(8,128)(2,1)S(1)}, bf16[128,1280]{1,0:T(8,128)(2,1)S(1)}, u32[]{:S(2)}, u32[]{:S(2)}) collective-permute-start(bf16[128,1280]{1,0:T(8,128)(2,1)S(1)} %bitcast.218), channel_id=1, source_target_pairs={{0,2},{1,3},{2,0},{3,1},{4,6},{5,7},{6,4},{7,5},{8,10},{9,11},{10,... | collective-permute-start | bytes 983048 | tf_op jit(solution)/shard_map/cond/branch_1_fun/ppermute | solution.py:323
  270.4 24.9 %collective-permute-start.81 = (bf16[128,1280]{1,0:T(8,128)(2,1)S(1)}, bf16[128,1280]{1,0:T(8,128)(2,1)S(1)}, u32[]{:S(2)}, u32[]{:S(2)}) collective-permute-start(bf16[128,1280]{1,0:T(8,128)(2,1)S(1)} %bitcast.211), channel_id=1, source_target_pairs={{0,1},{1,0},{2,3},{3,2},{4,5},{5,4},{6,7},{7,6},{8,9},{9,8},{10,11... | collective-permute-start | bytes 983048 | tf_op jit(solution)/shard_map/cond/branch_1_fun/ppermute | solution.py:323
  271.5 25.7 %collective-permute-start.83 = (bf16[128,1280]{1,0:T(8,128)(2,1)S(1)}, bf16[128,1280]{1,0:T(8,128)(2,1)S(1)}, u32[]{:S(2)}, u32[]{:S(2)}) collective-permute-start(bf16[128,1280]{1,0:T(8,128)(2,1)S(1)} %bitcast.206), channel_id=1, source_target_pairs={{0,3},{1,2},{2,1},{3,0},{4,7},{5,6},{6,5},{7,4},{8,11},{9,10},{10,... | collective-permute-start | bytes 983048 | tf_op jit(solution)/shard_map/cond/branch_1_fun/ppermute | solution.py:323
  291.5 30.2 %collective-permute-start.98 = (bf16[128,1280]{1,0:T(8,128)(2,1)S(1)}, bf16[128,1280]{1,0:T(8,128)(2,1)S(1)}, u32[]{:S(2)}, u32[]{:S(2)}) collective-permute-start(bf16[128,1280]{1,0:T(8,128)(2,1)S(1)} %get-tuple-element.239), channel_id=1, source_target_pairs={{0,3},{1,2},{2,1},{3,0},{4,7},{5,6},{6,5},{7,4},{8,11},{9,10},{10,... | collective-permute-start | bytes 983048 | tf_op jit(solution)/shard_map/cond/branch_1_fun/ppermute | solution.py:323
  304.2 52.9 %collective-permute-start.99 = (bf16[128,1280]{1,0:T(8,128)(2,1)}, bf16[128,1280]{1,0:T(8,128)(2,1)}, u32[]{:S(2)}, u32[]{:S(2)}) collective-permute-start(bf16[128,1280]{1,0:T(8,128)(2,1)} %get-tuple-element.242), channel_id=1, source_target_pairs={{0,1},{1,0},{2,3},{3,2},{4,5},{5,4},{6,7},{7,6},{8,9},{9,8},{10,11... | collective-permute-start | bytes 983048 | tf_op jit(solution)/shard_map/cond/branch_1_fun/ppermute | solution.py:323
  304.2 52.9 %collective-permute-start.100 = (bf16[128,1280]{1,0:T(8,128)(2,1)}, bf16[128,1280]{1,0:T(8,128)(2,1)}, u32[]{:S(2)}, u32[]{:S(2)}) collective-permute-start(bf16[128,1280]{1,0:T(8,128)(2,1)} %get-tuple-element.243), channel_id=1, source_target_pairs={{0,2},{1,3},{2,0},{3,1},{4,6},{5,7},{6,4},{7,5},{8,10},{9,11},{10,... | collective-permute-start | bytes 983048 | tf_op jit(solution)/shard_map/cond/branch_1_fun/ppermute | solution.py:323
  309.8 47.3 %collective-permute-start.101 = (bf16[128,1280]{1,0:T(8,128)(2,1)}, bf16[128,1280]{1,0:T(8,128)(2,1)}, u32[]{:S(2)}, u32[]{:S(2)}) collective-permute-start(bf16[128,1280]{1,0:T(8,128)(2,1)} %get-tuple-element.244), channel_id=1, source_target_pairs={{0,3},{1,2},{2,1},{3,0},{4,7},{5,6},{6,5},{7,4},{8,11},{9,10},{10,... | collective-permute-start | bytes 983048 | tf_op jit(solution)/shard_map/cond/branch_1_fun/ppermute | solution.py:323
  (119 other events, 1395.6 us)
Sparse Core Ops, SparseCore 0:
  57.0 61.3 all-gather.15
  136.1 38.2 all-gather.17
  200.8 119.9 all-gather.19

commit v3 on v2

--- a/solution.py
+++ b/solution.py
@@ -42,7 +42,7 @@
     def __init__(self):
         self.last = []
 
-    def call(self, body, operands, in_specs, out_specs, out_shape, aliases=None):
+    def call(self, body, operands, in_specs, out_specs, out_shape, pieces=1, aliases=None):
         after = self.last
         first = len(operands)
 
@@ -51,7 +51,7 @@
 
         out = pl.pallas_call(
             kernel,
-            grid=(1,),
+            grid=(pieces,),
             in_specs=in_specs + [HERE] * len(after),
             out_specs=out_specs,
             out_shape=out_shape,
@@ -69,25 +69,26 @@
 
 def hold(line, x):
     last = line.last
-    out = line.call(hold_body, [x], [FAR], FAR, jax.ShapeDtypeStruct(x.shape, x.dtype), {0: 0})
+    out = line.call(hold_body, [x], [FAR], FAR, jax.ShapeDtypeStruct(x.shape, x.dtype), 1, {0: 0})
     line.last = last
     return out
 
 
-def route(line, rows, ins, outs, piece=None):
+def route(line, rows, ins, outs):
     width = ins[0].shape[1]
-    specs = [whole(x.shape) for x in ins]
-    if piece is not None:
-        at, of = piece
-        width = width // of
-        specs = [pl.BlockSpec((ins[0].shape[0], width), lambda i: (0, at))]
-    shapes = [(n, width) for n in outs]
+    pieces = PIECES if width % (128 * PIECES) == 0 else 1
+    step = width // pieces
+
+    def block(n):
+        return pl.BlockSpec((n, step), lambda i: (0, i))
+
     return line.call(
         functools.partial(route_body, len(ins)),
         [rows, *ins],
-        [whole(rows.shape)] + specs,
-        [whole(x) for x in shapes],
-        [jax.ShapeDtypeStruct(x, BF) for x in shapes],
+        [whole(rows.shape)] + [block(x.shape[0]) for x in ins],
+        [block(n) for n in outs],
+        [jax.ShapeDtypeStruct((n, width), BF) for n in outs],
+        pieces,
     )
 
 
@@ -123,50 +124,45 @@
             at += out.shape[1]
 
 
-def adapter_terms(line, back_low, down, piece, outs):
-    at, of = piece
+def adapter_terms(line, back_low, down, outs):
     local, width, rank = down.shape
-    width = width // of
-    shapes = [(local, n, width) for n in outs]
+    step = width // PIECES
     return line.call(
         term_body,
         [back_low, down],
-        [whole(back_low.shape), pl.BlockSpec((local, width, rank), lambda i: (0, at, 0))],
-        [whole(x) for x in shapes],
-        [jax.ShapeDtypeStruct(x, BF) for x in shapes],
-    )
-
-
-def owner_body(count, carried, back_ref, down_ref, *refs):
-    ins, refs = refs[:count], refs[count:]
-    if carried:
-        low_in, _, low_ref, grad_ref = refs
-    else:
-        low_ref, grad_ref = refs
+        [whole(back_low.shape), pl.BlockSpec((local, step, rank), lambda i: (0, i, 0))],
+        [pl.BlockSpec((local, n, step), lambda i: (0, 0, i)) for n in outs],
+        [jax.ShapeDtypeStruct((local, n, width), BF) for n in outs],
+        PIECES,
+    )
+
+
+def owner_body(count, back_ref, down_ref, *refs):
+    ins, (low_ref, grad_ref) = refs[:count], refs[count:]
+
+    @pl.when(pl.program_id(0) == 0)
+    def _():
+        low_ref[...] = jnp.zeros_like(low_ref)
+
     for job in range(down_ref.shape[0]):
         held = job_rows(ins, job)
-        low = dot(held, down_ref[job])
-        low_ref[job] = low_in[job] + low if carried else low
+        low_ref[job] += dot(held, down_ref[job])
         grad_ref[job] = dot(held, back_ref[job], 0, 0).astype(BF)
 
 
-def owner_step(line, back_low, down, rows, piece, carry):
-    at, of = piece
+def owner_step(line, back_low, down, rows):
     local, width, rank = down.shape
-    part = pl.BlockSpec((local, width // of, rank), lambda i: (0, at, 0))
+    step = width // PIECES
+    part = pl.BlockSpec((local, step, rank), lambda i: (0, i, 0))
     low_shape = (local, back_low.shape[1], rank)
-    extra, extra_specs, aliases = [], [], {}
-    if carry is not None:
-        extra = list(carry)
-        extra_specs = [whole(low_shape), FAR]
-        aliases = {2 + len(rows): 0, 3 + len(rows): 1}
-    return line.call(
-        functools.partial(owner_body, len(rows), carry is not None),
-        [back_low, down, *rows, *extra],
-        [whole(back_low.shape), part] + [whole(x.shape) for x in rows] + extra_specs,
+    return line.call(
+        functools.partial(owner_body, len(rows)),
+        [back_low, down, *rows],
+        [whole(back_low.shape), part]
+        + [pl.BlockSpec((local, x.shape[1], step), lambda i: (0, 0, i)) for x in rows],
         [whole(low_shape), part],
         [jax.ShapeDtypeStruct(low_shape, F32), jax.ShapeDtypeStruct(down.shape, BF)],
-        aliases,
+        PIECES,
     )
 
 
@@ -189,32 +185,36 @@
     )
 
 
-def final_body(count, scaled_ref, weight_ref, rows_ref, *refs):
-    ins, out = refs[:count], refs[-1]
-    held = jnp.concatenate([r[...] for r in ins], axis=0)
-    weight = weight_ref[...].reshape(-1, weight_ref.shape[-1])
+def final_body(scaled_ref, weight_ref, rows_ref, ref, out):
+    cores, parts, height = weight_ref.shape[:3]
+    weight = jnp.concatenate(
+        [
+            weight_ref[core, part, at, 0]
+            for at in range(height)
+            for core in range(cores)
+            for part in range(parts)
+        ],
+        axis=0,
+    )
     base = dot(scaled_ref[...], weight, 1, 1)
-    out[...] = (base + dot(rows_ref[...], held)).astype(BF)
-
-
-def final_step(line, scaled, weight, rows, ins, piece, carry):
-    at, of = piece
-    column, parts, planes, share, deep = weight.shape
-    width = column * parts * planes * share // of
-    extra = [] if carry is None else [carry]
-    return line.call(
-        functools.partial(final_body, len(ins)),
-        [scaled, weight, rows, *ins, *extra],
+    out[...] = (base + dot(rows_ref[...], ref[...])).astype(BF)
+
+
+def final_step(line, scaled, weight, rows, came):
+    cores, parts, height, planes, share, deep = weight.shape
+    step = cores * parts * height * share
+    return line.call(
+        final_body,
+        [scaled, weight, rows, came],
         [
             whole(scaled.shape),
-            pl.BlockSpec((column, parts, planes // of, share, deep), lambda i: (0, 0, at, 0, 0)),
+            pl.BlockSpec((cores, parts, height, 1, share, deep), lambda i: (0, 0, 0, i, 0, 0)),
             whole(rows.shape),
-        ]
-        + [whole(x.shape) for x in ins]
-        + [FAR] * len(extra),
-        pl.BlockSpec((scaled.shape[0], width), lambda i: (0, at)),
-        jax.ShapeDtypeStruct((scaled.shape[0], width * of), BF),
-        {} if carry is None else {3 + len(ins): 0},
+            pl.BlockSpec((came.shape[0], step), lambda i: (0, i)),
+        ],
+        pl.BlockSpec((scaled.shape[0], step), lambda i: (0, i)),
+        jax.ShapeDtypeStruct((scaled.shape[0], step * planes), BF),
+        planes,
     )
 
 
@@ -267,11 +267,7 @@
     mine = notes[:, :tok_rows].reshape(parts, PLANES, column, tok_rows)
     mine = lax.dynamic_index_in_dim(mine, lax.axis_index("groups"), 0, keepdims=False)
     mine = lax.dynamic_index_in_dim(mine, place, 1, keepdims=False)
-    there = planes ^ plane
-    slots = jnp.sum(
-        jnp.where(there[:, None, None] == planes[None, :, None], mine[None], 0), axis=1
-    )
-    slots = jnp.concatenate([row_slot[None], slots[1:]], axis=0)
+    slots = mine
     goal = slots // (local * column)
     earlier = jnp.arange(tok_rows)[None, :] < jnp.arange(tok_rows)[:, None]
     order = jnp.sum(
@@ -294,7 +290,6 @@
     own_order = jnp.sum(
         ((own_goal[:, None] == own_goal[None, :]) & earlier).astype(jnp.int32), axis=1
     )
-    side = own_goal ^ plane
 
     def across(bufs):
         return [bufs[0]] + [
@@ -339,28 +334,43 @@
         return [x.reshape(column * local * segment, width)]
 
     stripes = [[p * column + c for p in range(PLANES)] for c in range(column)]
+    pairs = [[d, d + 1] for d in range(0, devices, 2)]
+    lanes_of = [
+        [p * column + 2 * h + c for h in range(column // 2)]
+        for p in range(PLANES)
+        for c in range(2)
+    ]
+
+    def planes_swap(x):
+        return lax.all_to_all(
+            x, "dp", split_axis=0, concat_axis=0, tiled=True, axis_index_groups=stripes
+        )
+
+    def gather_all(x, axis, groups=None):
+        return lax.all_gather(x, axis, axis=0, tiled=True, axis_index_groups=groups)
 
     share = frozen_key_weight.shape[0] // parts
     deep = frozen_key_weight.shape[1]
-    own_share = lax.dynamic_slice_in_dim(
+    weight = lax.dynamic_slice_in_dim(
         frozen_key_weight, lax.axis_index("groups") * share, share, 0
     )
+    weight_z = gather_all(weight, "dp", stripes)
 
     def shape_weight(w):
-        w = w.reshape(column, parts, PLANES, share, deep)
+        w = w.reshape(2, parts, column // 2, PLANES, share, deep)
         if share % 16 == 0:
             return w
-        w = w.transpose(2, 0, 1, 3, 4)
-        return w.reshape(1, 1, PLANES, column * parts * share, deep)
-
-    def outward(size):
+        w = w.transpose(3, 2, 0, 1, 4, 5)
+        return w.reshape(1, 1, 1, PLANES, column * parts * share, deep)
+
+    def outward(size, side):
         lanes = jnp.arange(PLANES * size, dtype=jnp.int32)
         code = side * size + own_order
         return (lanes[:, None] == code[None, :]).astype(BF), (
             code[:, None] == lanes[None, :]
         ).astype(BF)
 
-    def inward(size):
+    def inward(size, turned=False):
         kth = jnp.arange(size, dtype=jnp.int32)
         target = jnp.sum(
             jnp.where(
@@ -369,108 +379,37 @@
                 0,
             ),
             axis=2,
-        ).reshape(PLANES * size) - 1
+        )
+        if turned:
+            there = (planes ^ plane)[:, None, None] == planes[None, :, None]
+            target = jnp.sum(jnp.where(there, target[None], 0), axis=1)
+        target = target.reshape(PLANES * size) - 1
         spots = jnp.arange(PLANES * most, dtype=jnp.int32)
         return (spots[:, None] == target[None, :]).astype(BF), (
             target[:, None] == spots[None, :]
         ).astype(BF)
 
-    scaled_z = across(route(Line(), outward(most)[0], [scaled], [most] * PLANES))
-    scaled_sent = route(Line(), inward(most)[0], scaled_z, blocks_out)
+    scaled_z = across(route(Line(), outward(most, own_goal ^ plane)[0], [scaled], [most] * PLANES))
+    scaled_sent = route(Line(), inward(most, True)[0], scaled_z, blocks_out)
 
     def run(size):
-        out_rows, back_rows = outward(size)
+        out_rows, back_rows = outward(size, own_goal)
         spread, gather = inward(size)
-        sizes = [size] * PLANES
         line = Line()
-        pieces = [(at, PIECES) for at in range(PIECES)]
-
-        def leave(at):
-            return route(line, out_rows, [acts], sizes, pieces[at])
-
-        def spread_out(bufs):
-            return route(line, spread, bufs, blocks_out)
-
-        def term(at):
-            return from_owner(
-                adapter_terms(line, back_low, adapter_down_slots, pieces[at], owner_outs)
-            )
-
-        def home(came):
-            return route(line, gather, came, sizes)
-
-        def own(at, got, carry):
-            return owner_step(line, back_low, adapter_down_slots, at_owner(got), pieces[at], carry)
-
-        def final(at, carry):
-            return final_step(line, scaled, weight, back_rows, terms_z[at], pieces[at], carry)
-
-        def fly(far, close):
-            far, close = across(far) if far else [], near(close)
-            return far, close, far[1:] + (close[1:] if ring else close)
-
-        acts_z, acts_o, acts_x, terms_z, terms_x = {}, {}, {}, {}, {}
-        weight = lax.all_gather(
-            own_share, "dp", axis=0, tiled=True, axis_index_groups=stripes
-        )
-        out = leave(0)
-        acts_z[0], got_scaled, landed = fly(out, scaled_sent)
-        out = leave(1)
-        line.last += landed
-        got_scaled = at_owner(got_scaled)
+        total = PLANES * size
+        acts_z = planes_swap(route(line, out_rows, [acts], [total])[0])
+        weight = gather_all(weight_z, "dp", lanes_of)
+        got_scaled = at_owner(near(scaled_sent))
         back_low = back_project(line, adapter_up_slots, got_scaled)
-        terms_o = term(0)
-
-        acts_z[1], terms_x[0], landed = fly(out, terms_o)
-        acts_o[0] = spread_out(acts_z[0])
-        terms_o = term(1)
-        line.last += landed
-        back = home(terms_x[0])
-
-        terms_z[0], terms_x[1], landed = fly(back, terms_o)
-        acts_o[1] = spread_out(acts_z[1])
-        out = leave(2)
-        weight = lax.all_gather(hold(line, weight), "groups", axis=0, tiled=True)
-        line.last += landed
-        back = home(terms_x[1])
-
-        terms_z[1], acts_x[0], landed = fly(back, acts_o[0])
-        terms_o = term(2)
-        line.last += landed
-        carry = own(0, acts_x[0], None)
-
-        acts_z[2], terms_x[2], landed = fly(out, terms_o)
-        out = leave(3)
-        weight = lax.all_gather(
-            hold(line, weight), "dp", axis=0, tiled=True, axis_index_groups=blocks
-        )
-        line.last += landed
-        back = home(terms_x[2])
-        terms_o = term(3)
-
-        terms_z[2], acts_x[1], landed = fly(back, acts_o[1])
-        acts_o[2] = spread_out(acts_z[2])
-        line.last += landed
-        carry = own(1, acts_x[1], carry)
-
-        acts_z[3], terms_x[3], landed = fly(out, terms_o)
-        line.last += landed
-        back = home(terms_x[3])
-        acts_o[3] = spread_out(acts_z[3])
-
-        terms_z[3], acts_x[2], landed = fly(back, acts_o[2])
-        weight = shape_weight(weight)
-        result = final(0, None)
-        result = final(1, result)
-        line.last += landed
-        carry = own(2, acts_x[2], carry)
-
-        _, acts_x[3], landed = fly([], acts_o[3])
-        result = final(2, result)
-        result = final(3, result)
-        line.last += landed
-        low, grad_a = own(3, acts_x[3], carry)
+        terms = adapter_terms(line, back_low, adapter_down_slots, owner_outs)
+        terms = near(from_owner(terms))
+        weight = gather_all(hold(line, weight), "groups")
+        terms_z = planes_swap(route(line, gather, terms, [total])[0])
+        got = at_owner(near(route(line, spread, [acts_z], blocks_out)))
+        weight = gather_all(hold(line, weight), "dp", pairs)
+        low, grad_a = owner_step(line, back_low, adapter_down_slots, got)
         grad_b = up_gradient(line, low, got_scaled)
+        result = final_step(line, scaled, shape_weight(weight), back_rows, terms_z)
         return result, grad_a, grad_b
 
     steps = [most * 5 // 8, most * 3 // 4, most]

time: 385 us -> 306 us (0.79)
  the two profiles are of different devices: /device:TPU:15 before, /device:TPU:1 now
where the time goes in v3:
time: 306 us; the launch traced here: 304 us
  waiting for transfers between devices  196 us (64%)
  Pallas kernels  37.4 us (12%)
  starting transfers between devices  28.6 us (9%)
  local copies, waits for them, and re-layouts  18.4 us (6%)
  between operations  15.9 us (5%)
  other arithmetic  8.36 us (3%)
    ppermute x9, waiting for transfers between devices, near(): lax.ppermute(bufs[s], 'dp', [(d, d ^ s) for d in range(devices)])  138 us
    pallas_call x12, Pallas kernels, call(): pl.pallas_call(kernel, grid=(pieces,), in_specs=in_specs + [HERE] * len(a...  37.4 us
    all_to_all x2, waiting for transfers between devices, planes_swap(): lax.all_to_all(x, 'dp', split_axis=0, concat_axis=0, tiled=True, axis_ind...  21.4 us
    all_gather x4, waiting for transfers between devices, gather_all(): return lax.all_gather(x, axis, axis=0, tiled=True, axis_index_groups=groups)  19 us
    all_to_all x1, waiting for transfers between devices, shards(): lax.all_to_all(jnp.broadcast_to(note[None, None], (parts * devices, 1, to...  16.7 us
    cond x28, local copies, waits for them, and re-layouts  15.1 us
    all_to_all x2, starting transfers between devices, planes_swap(): lax.all_to_all(x, 'dp', split_axis=0, concat_axis=0, tiled=True, axis_ind...  9.81 us
    all_to_all x1, starting transfers between devices, shards(): lax.all_to_all(jnp.broadcast_to(note[None, None], (parts * devices, 1, to...  7.05 us
  transfers between devices with their start and end apart: 19, of which 12 were waited for; matrix products, arithmetic and copies ran while one was open for 2% of the time, Pallas kernels for 9%

profile of v3, /device:TPU:1, one launch (start us, length us, event | category | flops | bytes accessed | tf_op | source)
XLA Modules:
  0.0 304.5 jit_solution(18444544563011119586)
XLA Ops:
  14.0 2.2 collective-permute-start.27
  16.2 2.3 collective-permute-start.28
  20.6 7.1 %all-to-all-start.6 = ((s32[32,1,384]{2,1,0:T(1,128)}), s32[32,1,384]{2,1,0:T(1,128)S(1)}, u32[]{:S(2)}, u32[]{:S(2)}) async-start(s32[32,1,384]{2,1,0:T(1,128)} %broadcast_in_dim.92), calls=%async_computation.6 | async-start | bytes 98304 | tf_op jit(solution)/shard_map/all_to_all | solution.py:259
  28.6 16.7 %all-to-all-done.6 = s32[32,1,384]{2,1,0:T(1,128)S(1)} async-done(((s32[32,1,384]{2,1,0:T(1,128)}), s32[32,1,384]{2,1,0:T(1,128)S(1)}, u32[]{:S(2)}, u32[]{:S(2)}) %all-to-all-start.6) | async-done | bytes 49184 | tf_op jit(solution)/shard_map/all_to_all | solution.py:259
  48.7 2.4 shard_map.110
  51.1 13.7 %all-gather.29.cloned.1.call-done = bf16[640,1024]{1,0:T(8,128)(2,1)} async-done(((bf16[160,1024]{1,0:T(8,128)(2,1)}), bf16[640,1024]{1,0:T(8,128)(2,1)}) %all-gather.29.cloned.1.call-update) | async-done | bytes 1310736 | tf_op jit(solution)/shard_map/all_gather | solution.py:350
  64.8 232.1 %conditional.1 = (bf16[2,5120,128]{2,1,0:T(8,128)(2,1)}, bf16[256,5120]{1,0:T(8,128)(2,1)}, bf16[2,128,1024]{2,1,0:T(8,128)(2,1)}) conditional(s32[]{:T(128)} %clamp.11, (bf16[640,1024]{1,0:T(8,128)(2,1)}, bf16[128,1024]{1,0:T(8,128)(2,1)S(1)}, bf16[128,1024]{1,0:T(8,128)(2,1)S(1)}, bf16[128,1024]{1,0:T(8,128)(2,1)S(1)}, ...), branch_computations={%region_11.13_spmd, %region_13.15_spmd, %region_15.17_spmd} | conditional | flops 2099722 | bytes 260354016 | solution.py:417
  65.6 3.7 %branch_1_fun.10.refs_5_ = bf16[384,5120]{1,0:T(8,128)(2,1)S(1)} custom-call(bf16[384,256]{1,0:T(8,128)(2,1)S(1)} %fusion.7.refs_0_, bf16[256,5120]{1,0:T(8,128)(2,1)} %get-tuple-element.110.refs_1_), custom_call_target="tpu_custom_call" | custom-call | flops 1 | bytes 1 | tf_op jit(solution)/shard_map/cond/branch_1_fun/pallas_call | solution.py:52
  71.2 5.0 %all-to-all-start.2 = ((bf16[4,96,5120]{2,1,0:T(8,128)(2,1)}), bf16[4,96,5120]{2,1,0:T(8,128)(2,1)}, u32[]{:S(2)}, u32[]{:S(2)}) async-start(bf16[4,96,5120]{2,1,0:T(8,128)(2,1)} %bitcast.70), calls=%async_computation.2 | async-start | bytes 7864320 | tf_op jit(solution)/shard_map/cond/branch_1_fun/all_to_all | solution.py:345
  78.5 11.9 %collective-permute-done.10 = bf16[128,1024]{1,0:T(8,128)(2,1)S(1)} collective-permute-done((bf16[128,1024]{1,0:T(8,128)(2,1)S(1)}, bf16[128,1024]{1,0:T(8,128)(2,1)S(1)}, u32[]{:S(2)}, u32[]{:S(2)}) %collective-permute-start.10) | collective-permute-done | bytes 262176 | tf_op jit(solution)/shard_map/cond/branch_1_fun/ppermute | solution.py:318
  90.5 11.9 %collective-permute-done.11 = bf16[128,1024]{1,0:T(8,128)(2,1)S(1)} collective-permute-done((bf16[128,1024]{1,0:T(8,128)(2,1)S(1)}, bf16[128,1024]{1,0:T(8,128)(2,1)S(1)}, u32[]{:S(2)}, u32[]{:S(2)}) %collective-permute-start.11) | collective-permute-done | bytes 262176 | tf_op jit(solution)/shard_map/cond/branch_1_fun/ppermute | solution.py:318
  102.4 2.1 copy-done.5
  106.2 2.6 branch_1_fun.12
  112.0 5.3 %all-gather.17.cloned.1.call-done.refs_0_ = bf16[1280,1024]{1,0:T(8,128)(2,1)} async-done(((bf16[640,1024]{1,0:T(8,128)(2,1)}), bf16[1280,1024]{1,0:T(8,128)(2,1)}) %all-gather.17.cloned.1.call-update) | async-done | bytes 2621456 | tf_op jit(solution)/shard_map/cond/branch_1_fun/all_gather | solution.py:350
  124.6 27.7 %collective-permute-done.13.refs_3_ = bf16[128,5120]{1,0:T(8,128)(2,1)} collective-permute-done((bf16[128,5120]{1,0:T(8,128)(2,1)}, bf16[128,5120]{1,0:T(8,128)(2,1)}, u32[]{:S(2)}, u32[]{:S(2)}) %collective-permute-start.13) | collective-permute-done | bytes 1310752 | tf_op jit(solution)/shard_map/cond/branch_1_fun/ppermute | solution.py:318
  152.3 28.5 %collective-permute-done.14.refs_4_ = bf16[128,5120]{1,0:T(8,128)(2,1)} collective-permute-done((bf16[128,5120]{1,0:T(8,128)(2,1)}, bf16[128,5120]{1,0:T(8,128)(2,1)}, u32[]{:S(2)}, u32[]{:S(2)}) %collective-permute-start.14) | collective-permute-done | bytes 1310752 | tf_op jit(solution)/shard_map/cond/branch_1_fun/ppermute | solution.py:318
  180.8 5.9 %branch_1_fun.14.refs_2_ = bf16[384,5120]{1,0:T(8,128)(2,1)} custom-call(bf16[384,512]{1,0:T(8,128)(2,1)S(1)} %fusion.6.refs_0_, bf16[128,5120]{1,0:T(8,128)(2,1)S(1)} %bitcast.77, bf16[128,5120]{1,0:T(8,128)(2,1)} %collective-permute-done.12.refs_2_, bf16[128,5120]{1,0:T(8,128)(2,1)} %collective-permute-done.13.refs_3_, ...), custom_call_target="tpu_custom_call" | custom-call | flops 1 | bytes 1 | tf_op jit(solution)/shard_map/cond/branch_1_fun/pallas_call | solution.py:52
  186.7 5.3 %branch_1_fun.15 = (bf16[128,5120]{1,0:T(8,128)(2,1)S(1)}, bf16[128,5120]{1,0:T(8,128)(2,1)S(1)}, bf16[128,5120]{1,0:T(8,128)(2,1)S(1)}, bf16[128,5120]{1,0:T(8,128)(2,1)S(1)}) custom-call(bf16[512,384]{1,0:T(8,128)(2,1)S(1)} %fusion.5.refs_0_, bf16[384,5120]{1,0:T(8,128)(2,1)} %bitcast.22.refs_1_, bf16[384,5120]{1,0:T(8,128)(2,1)} %branch_1_fun.14.refs_2_), custom_call_target="tpu_custom_call" | custom-call | flops 1 | bytes 1 | tf_op jit(solution)/shard_map/cond/branch_1_fun/pallas_call | solution.py:52
  195.3 4.8 %all-to-all-start.3 = ((bf16[4,96,5120]{2,1,0:T(8,128)(2,1)}), bf16[4,96,5120]{2,1,0:T(8,128)(2,1)}, u32[]{:S(2)}, u32[]{:S(2)}) async-start(bf16[4,96,5120]{2,1,0:T(8,128)(2,1)} %bitcast.115), calls=%async_computation.3 | async-start | bytes 7864320 | tf_op jit(solution)/shard_map/cond/branch_1_fun/all_to_all | solution.py:345
  203.4 27.1 %collective-permute-done.16 = bf16[128,5120]{1,0:T(8,128)(2,1)S(1)} collective-permute-done((bf16[128,5120]{1,0:T(8,128)(2,1)}, bf16[128,5120]{1,0:T(8,128)(2,1)S(1)}, u32[]{:S(2)}, u32[]{:S(2)}) %collective-permute-start.16) | collective-permute-done | bytes 1310752 | tf_op jit(solution)/shard_map/cond/branch_1_fun/ppermute | solution.py:318
  230.5 29.0 %collective-permute-done.17 = bf16[128,5120]{1,0:T(8,128)(2,1)S(1)} collective-permute-done((bf16[128,5120]{1,0:T(8,128)(2,1)}, bf16[128,5120]{1,0:T(8,128)(2,1)S(1)}, u32[]{:S(2)}, u32[]{:S(2)}) %collective-permute-start.17) | collective-permute-done | bytes 1310752 | tf_op jit(solution)/shard_map/cond/branch_1_fun/ppermute | solution.py:318
  259.4 6.0 %branch_1_fun.17 = (f32[2,256,128]{2,1,0:T(8,128)S(1)}, bf16[2,5120,128]{2,1,0:T(8,128)(2,1)}) custom-call(bf16[2,256,128]{2,1,0:T(8,128)(2,1)S(1)} %branch_1_fun.11.refs_0_.refs_2_, bf16[2,5120,128]{2,1,0:T(8,128)(2,1)} %get-tuple-element.111.refs_1_, bf16[2,64,5120]{2,1,0:T(8,128)(2,1)S(1)} %bitcast.75, bf16[2,64,5120]{2,1,0:T(8,128)(2,1)S(1)} %bitcast.79, ...), custom_call_target="tpu_custom_call" | custom-call | flops 1 | bytes 1 | tf_op jit(solution)/shard_map/cond/branch_1_fun/pallas_call | solution.py:52
  266.5 21.4 %all-to-all-done.3 = bf16[4,96,5120]{2,1,0:T(8,128)(2,1)} async-done(((bf16[4,96,5120]{2,1,0:T(8,128)(2,1)}), bf16[4,96,5120]{2,1,0:T(8,128)(2,1)}, u32[]{:S(2)}, u32[]{:S(2)}) %all-to-all-start.3) | async-done | bytes 3932192 | tf_op jit(solution)/shard_map/cond/branch_1_fun/all_to_all | solution.py:345
  287.9 8.9 %branch_1_fun.19 = bf16[256,5120]{1,0:T(8,128)(2,1)} custom-call(bf16[256,1024]{1,0:T(8,128)(2,1)S(1)} %copy-done.36, bf16[2,2,2,4,160,1024]{5,4,3,2,1,0:T(8,128)(2,1)} %bitcast.117, bf16[256,384]{1,0:T(8,128)(2,1)S(1)} %fusion.9.refs_2_, bf16[384,5120]{1,0:T(8,128)(2,1)} %bitcast.33.refs_3_, bf16[2,128,1024]{2,1,0:T(8,128)(2,1)} %branch_1_fun.18.refs_4_), custom_call_target="tpu_custom_call" | custom-call | flops 1 | bytes 1 | tf_op jit(solution)/shard_map/cond/branch_1_fun/pallas_call | solution.py:52
  (107 shorter events, 37.1 us)
Async XLA Ops:
  7.2 20.5 %copy-start = (bf16[320,1024]{1,0:T(8,128)(2,1)S(1)}, bf16[320,1024]{1,0:T(8,128)(2,1)}, u32[]{:S(2)}) copy-start(bf16[320,1024]{1,0:T(8,128)(2,1)} %param.13) | copy-start | bytes 1966084
  14.0 34.7 %collective-permute-start.27 = (bf16[128,1024]{1,0:T(8,128)(2,1)S(1)}, bf16[128,1024]{1,0:T(8,128)(2,1)S(1)}, u32[]{:S(2)}, u32[]{:S(2)}) collective-permute-start(bf16[128,1024]{1,0:T(8,128)(2,1)S(1)} %get-tuple-element.159), channel_id=1, source_target_pairs={{0,4},{1,5},{2,6},{3,7},{4,0},{5,1},{6,2},{7,3},{8,12},{9,13},{10,... | collective-permute-start | bytes 786440 | tf_op jit(solution)/shard_map/ppermute | solution.py:296
  16.2 32.5 %collective-permute-start.28 = (bf16[128,1024]{1,0:T(8,128)(2,1)S(1)}, bf16[128,1024]{1,0:T(8,128)(2,1)S(1)}, u32[]{:S(2)}, u32[]{:S(2)}) collective-permute-start(bf16[128,1024]{1,0:T(8,128)(2,1)S(1)} %get-tuple-element.160), channel_id=1, source_target_pairs={{0,8},{1,9},{2,10},{3,11},{4,12},{5,13},{6,14},{7,15},{8,0},{9,1},... | collective-permute-start | bytes 786440 | tf_op jit(solution)/shard_map/ppermute | solution.py:296
  18.5 30.2 %collective-permute-start.29 = (bf16[128,1024]{1,0:T(8,128)(2,1)S(1)}, bf16[128,1024]{1,0:T(8,128)(2,1)S(1)}, u32[]{:S(2)}, u32[]{:S(2)}) collective-permute-start(bf16[128,1024]{1,0:T(8,128)(2,1)S(1)} %get-tuple-element.161), channel_id=1, source_target_pairs={{0,12},{1,13},{2,14},{3,15},{4,8},{5,9},{6,10},{7,11},{8,4},{9,5},... | collective-permute-start | bytes 786440 | tf_op jit(solution)/shard_map/ppermute | solution.py:296
  20.6 24.8 %all-to-all-start.6 = ((s32[32,1,384]{2,1,0:T(1,128)}), s32[32,1,384]{2,1,0:T(1,128)S(1)}, u32[]{:S(2)}, u32[]{:S(2)}) async-start(s32[32,1,384]{2,1,0:T(1,128)} %broadcast_in_dim.92), calls=%async_computation.6 | async-start | bytes 98304 | tf_op jit(solution)/shard_map/all_to_all | solution.py:259
  27.6 37.1 %all-gather.29.cloned.1.call-start = ((), (), s32[]{:S(2)}) async-start(), calls=%async_computation.16 | async-start | bytes 1638400 | tf_op jit(solution)/shard_map/all_gather | solution.py:350
  64.8 52.6 %all-gather.17.cloned.1.call-start = ((), (), s32[]{:S(2)}) async-start(), calls=%async_computation.10 | async-start | bytes 3932160 | tf_op jit(solution)/shard_map/cond/branch_1_fun/all_gather | solution.py:350
  71.2 6.8 %copy-start.44 = (bf16[128,1024]{1,0:T(8,128)(2,1)S(1)}, bf16[128,1024]{1,0:T(8,128)(2,1)}, u32[]{:S(2)}) copy-start(bf16[128,1024]{1,0:T(8,128)(2,1)} %get-tuple-element.107) | copy-start | bytes 786436 | tf_op jit(solution)/shard_map/cond
  71.2 31.2 %copy-start.39 = (bf16[2,128,1024]{2,1,0:T(8,128)(2,1)S(1)}, bf16[2,128,1024]{2,1,0:T(8,128)(2,1)}, u32[]{:S(2)}) copy-start(bf16[2,128,1024]{2,1,0:T(8,128)(2,1)} %get-tuple-element.103.refs_0_) | copy-start | bytes 1572868 | tf_op jit(solution)/shard_map/cond
  71.2 115.5 %all-to-all-start.2 = ((bf16[4,96,5120]{2,1,0:T(8,128)(2,1)}), bf16[4,96,5120]{2,1,0:T(8,128)(2,1)}, u32[]{:S(2)}, u32[]{:S(2)}) async-start(bf16[4,96,5120]{2,1,0:T(8,128)(2,1)} %bitcast.70), calls=%async_computation.2 | async-start | bytes 7864320 | tf_op jit(solution)/shard_map/cond/branch_1_fun/all_to_all | solution.py:345
  76.2 119.0 %all-gather.19.cloned.1.call-start = ((), (), s32[]{:S(2)}) async-start(), calls=%async_computation.11 | async-start | bytes 7864320 | tf_op jit(solution)/shard_map/cond/branch_1_fun/all_gather | solution.py:350
  76.3 2.3 collective-permute-start.9
  76.8 13.7 %collective-permute-start.10 = (bf16[128,1024]{1,0:T(8,128)(2,1)S(1)}, bf16[128,1024]{1,0:T(8,128)(2,1)S(1)}, u32[]{:S(2)}, u32[]{:S(2)}) collective-permute-start(bf16[128,1024]{1,0:T(8,128)(2,1)S(1)} %get-tuple-element.106), channel_id=1, source_target_pairs={{0,2},{1,3},{2,0},{3,1},{4,6},{5,7},{6,4},{7,5},{8,10},{9,11},{10,... | collective-permute-start | bytes 786440 | tf_op jit(solution)/shard_map/cond/branch_1_fun/ppermute | solution.py:318
  78.1 24.3 %collective-permute-start.11 = (bf16[128,1024]{1,0:T(8,128)(2,1)S(1)}, bf16[128,1024]{1,0:T(8,128)(2,1)S(1)}, u32[]{:S(2)}, u32[]{:S(2)}) collective-permute-start(bf16[128,1024]{1,0:T(8,128)(2,1)S(1)} %copy-done.44), channel_id=1, source_target_pairs={{0,3},{1,2},{2,1},{3,0},{4,7},{5,6},{6,5},{7,4},{8,11},{9,10},{10,... | collective-permute-start | bytes 786440 | tf_op jit(solution)/shard_map/cond/branch_1_fun/ppermute | solution.py:318
  102.4 2.1 copy-start.5
  120.6 167.3 %all-gather.21.cloned.1.call-start = ((), (), s32[]{:S(2)}) async-start(), calls=%async_computation.12 | async-start | bytes 15728640 | tf_op jit(solution)/shard_map/cond/branch_1_fun/all_gather | solution.py:350
  120.8 3.7 %collective-permute-start.12 = (bf16[128,5120]{1,0:T(8,128)(2,1)}, bf16[128,5120]{1,0:T(8,128)(2,1)}, u32[]{:S(2)}, u32[]{:S(2)}) collective-permute-start(bf16[128,5120]{1,0:T(8,128)(2,1)} %bitcast.112), channel_id=1, source_target_pairs={{0,1},{1,0},{2,3},{3,2},{4,5},{5,4},{6,7},{7,6},{8,9},{9,8},{10,11... | collective-permute-start | bytes 3932168 | tf_op jit(solution)/shard_map/cond/branch_1_fun/ppermute | solution.py:318
  121.6 30.7 %collective-permute-start.13 = (bf16[128,5120]{1,0:T(8,128)(2,1)}, bf16[128,5120]{1,0:T(8,128)(2,1)}, u32[]{:S(2)}, u32[]{:S(2)}) collective-permute-start(bf16[128,5120]{1,0:T(8,128)(2,1)} %bitcast.110), channel_id=1, source_target_pairs={{0,2},{1,3},{2,0},{3,1},{4,6},{5,7},{6,4},{7,5},{8,10},{9,11},{10,... | collective-permute-start | bytes 3932168 | tf_op jit(solution)/shard_map/cond/branch_1_fun/ppermute | solution.py:318
  121.6 59.2 %collective-permute-start.14 = (bf16[128,5120]{1,0:T(8,128)(2,1)}, bf16[128,5120]{1,0:T(8,128)(2,1)}, u32[]{:S(2)}, u32[]{:S(2)}) collective-permute-start(bf16[128,5120]{1,0:T(8,128)(2,1)} %bitcast.107), channel_id=1, source_target_pairs={{0,3},{1,2},{2,1},{3,0},{4,7},{5,6},{6,5},{7,4},{8,11},{9,10},{10,... | collective-permute-start | bytes 3932168 | tf_op jit(solution)/shard_map/cond/branch_1_fun/ppermute | solution.py:318
  195.3 92.6 %all-to-all-start.3 = ((bf16[4,96,5120]{2,1,0:T(8,128)(2,1)}), bf16[4,96,5120]{2,1,0:T(8,128)(2,1)}, u32[]{:S(2)}, u32[]{:S(2)}) async-start(bf16[4,96,5120]{2,1,0:T(8,128)(2,1)} %bitcast.115), calls=%async_computation.3 | async-start | bytes 7864320 | tf_op jit(solution)/shard_map/cond/branch_1_fun/all_to_all | solution.py:345
  200.1 3.3 %collective-permute-start.15 = (bf16[128,5120]{1,0:T(8,128)(2,1)}, bf16[128,5120]{1,0:T(8,128)(2,1)S(1)}, u32[]{:S(2)}, u32[]{:S(2)}) collective-permute-start(bf16[128,5120]{1,0:T(8,128)(2,1)} %copy-done.29), channel_id=1, source_target_pairs={{0,1},{1,0},{2,3},{3,2},{4,5},{5,4},{6,7},{7,6},{8,9},{9,8},{10,11... | collective-permute-start | bytes 3932168 | tf_op jit(solution)/shard_map/cond/branch_1_fun/ppermute | solution.py:318
  200.2 30.3 %collective-permute-start.16 = (bf16[128,5120]{1,0:T(8,128)(2,1)}, bf16[128,5120]{1,0:T(8,128)(2,1)S(1)}, u32[]{:S(2)}, u32[]{:S(2)}) collective-permute-start(bf16[128,5120]{1,0:T(8,128)(2,1)} %copy-done.25), channel_id=1, source_target_pairs={{0,2},{1,3},{2,0},{3,1},{4,6},{5,7},{6,4},{7,5},{8,10},{9,11},{10,... | collective-permute-start | bytes 3932168 | tf_op jit(solution)/shard_map/cond/branch_1_fun/ppermute | solution.py:318
  200.3 59.2 %collective-permute-start.17 = (bf16[128,5120]{1,0:T(8,128)(2,1)}, bf16[128,5120]{1,0:T(8,128)(2,1)S(1)}, u32[]{:S(2)}, u32[]{:S(2)}) collective-permute-start(bf16[128,5120]{1,0:T(8,128)(2,1)} %copy-done.20), channel_id=1, source_target_pairs={{0,3},{1,2},{2,1},{3,0},{4,7},{5,6},{6,5},{7,4},{8,11},{9,10},{10,... | collective-permute-start | bytes 3932168 | tf_op jit(solution)/shard_map/cond/branch_1_fun/ppermute | solution.py:318
  265.4 22.5 %copy-start.36 = (bf16[256,1024]{1,0:T(8,128)(2,1)S(1)}, bf16[256,1024]{1,0:T(8,128)(2,1)}, u32[]{:S(2)}) copy-start(bf16[256,1024]{1,0:T(8,128)(2,1)} %get-tuple-element.101.refs_0_) | copy-start | bytes 1572868 | tf_op jit(solution)/shard_map/cond
  (12 other events, 15.7 us)
Sparse Core Ops, SparseCore 0:
  30.6 34.1 all-gather.28
  67.2 50.1 all-gather.16
  120.7 68.5 all-gather.18
  195.4 22.7 all-gather.20

commit v4 on v3

--- a/solution.py
+++ b/solution.py
@@ -13,6 +13,10 @@
 PLANES = 4
 PIECES = 4
 PARAMS = pltpu.CompilerParams(vmem_limit_bytes=48 * 1024 * 1024)
+
+
+def far(shape, dtype=BF):
+    return pltpu.HBM(shape, dtype)
 
 
 def whole(shape):
@@ -69,25 +73,25 @@
 
 def hold(line, x):
     last = line.last
-    out = line.call(hold_body, [x], [FAR], FAR, jax.ShapeDtypeStruct(x.shape, x.dtype), 1, {0: 0})
+    out = line.call(hold_body, [x], [FAR], FAR, far(x.shape, x.dtype), 1, {0: 0})
     line.last = last
     return out
 
 
-def route(line, rows, ins, outs):
-    width = ins[0].shape[1]
-    pieces = PIECES if width % (128 * PIECES) == 0 else 1
-    step = width // pieces
-
-    def block(n):
-        return pl.BlockSpec((n, step), lambda i: (0, i))
-
+def route(line, rows, ins, outs, part=(0, 1, 1)):
+    lowest, highest, of = part
+    if of == 1 and ins[0].shape[1] % (128 * PIECES) == 0:
+        highest = of = PIECES
+    step = ins[0].shape[1] // of
+    pieces = highest - lowest
+    width = pieces * step
     return line.call(
         functools.partial(route_body, len(ins)),
         [rows, *ins],
-        [whole(rows.shape)] + [block(x.shape[0]) for x in ins],
-        [block(n) for n in outs],
-        [jax.ShapeDtypeStruct((n, width), BF) for n in outs],
+        [whole(rows.shape)]
+        + [pl.BlockSpec((x.shape[0], step), lambda i: (0, i + lowest)) for x in ins],
+        [pl.BlockSpec((n, step), lambda i: (0, i)) for n in outs],
+        [far((n, width)) for n in outs],
         pieces,
     )
 
@@ -132,7 +136,7 @@
         [back_low, down],
         [whole(back_low.shape), pl.BlockSpec((local, step, rank), lambda i: (0, i, 0))],
         [pl.BlockSpec((local, n, step), lambda i: (0, 0, i)) for n in outs],
-        [jax.ShapeDtypeStruct((local, n, width), BF) for n in outs],
+        [far((local, n, width)) for n in outs],
         PIECES,
     )
 
@@ -185,7 +189,7 @@
     )
 
 
-def final_body(scaled_ref, weight_ref, rows_ref, ref, out):
+def final_body(scaled_ref, weight_ref, rows_ref, main_ref, last_ref, out):
     cores, parts, height = weight_ref.shape[:3]
     weight = jnp.concatenate(
         [
@@ -197,20 +201,29 @@
         axis=0,
     )
     base = dot(scaled_ref[...], weight, 1, 1)
-    out[...] = (base + dot(rows_ref[...], ref[...])).astype(BF)
-
-
-def final_step(line, scaled, weight, rows, came):
+    last = pl.program_id(0) == PLANES - 1
+
+    @pl.when(last)
+    def _():
+        out[...] = (base + dot(rows_ref[...], last_ref[...])).astype(BF)
+
+    @pl.when(jnp.logical_not(last))
+    def _():
+        out[...] = (base + dot(rows_ref[...], main_ref[...])).astype(BF)
+
+
+def final_step(line, scaled, weight, rows, main, last):
     cores, parts, height, planes, share, deep = weight.shape
     step = cores * parts * height * share
     return line.call(
         final_body,
-        [scaled, weight, rows, came],
+        [scaled, weight, rows, main, last],
         [
             whole(scaled.shape),
             pl.BlockSpec((cores, parts, height, 1, share, deep), lambda i: (0, 0, 0, i, 0, 0)),
             whole(rows.shape),
-            pl.BlockSpec((came.shape[0], step), lambda i: (0, i)),
+            pl.BlockSpec((main.shape[0], step), lambda i: (0, jnp.minimum(i, planes - 2))),
+            pl.BlockSpec((last.shape[0], step), lambda i: (0, 0)),
         ],
         pl.BlockSpec((scaled.shape[0], step), lambda i: (0, i)),
         jax.ShapeDtypeStruct((scaled.shape[0], step * planes), BF),
@@ -241,6 +254,7 @@
     me = lax.axis_index("dp")
     plane, place = me // column, me % column
 
+    first = Line()
     ids = token_row_jobs[:, 0]
     lengths = loss_token_count.astype(F32)
     weights = jnp.mean(lengths) / lengths
@@ -256,8 +270,10 @@
         jnp.sum((row_slot[:, None] // (local * column) == planes[None, :]).astype(jnp.int32), axis=0)
     )
     note = jnp.concatenate([row_slot, jnp.full((128,), need, jnp.int32)])
+    note = jnp.broadcast_to(note[None, None], (parts * devices, 1, tok_rows + 128))
+    first.last = [note]
     notes = lax.all_to_all(
-        jnp.broadcast_to(note[None, None], (parts * devices, 1, tok_rows + 128)),
+        note,
         ("groups", "dp"),
         split_axis=0,
         concat_axis=0,
@@ -354,7 +370,8 @@
     weight = lax.dynamic_slice_in_dim(
         frozen_key_weight, lax.axis_index("groups") * share, share, 0
     )
-    weight_z = gather_all(weight, "dp", stripes)
+    own_share = weight
+    first.last += [own_share]
 
     def shape_weight(w):
         w = w.reshape(2, parts, column // 2, PLANES, share, deep)
@@ -389,32 +406,44 @@
             target[:, None] == spots[None, :]
         ).astype(BF)
 
-    scaled_z = across(route(Line(), outward(most, own_goal ^ plane)[0], [scaled], [most] * PLANES))
-    scaled_sent = route(Line(), inward(most, True)[0], scaled_z, blocks_out)
-
-    def run(size):
-        out_rows, back_rows = outward(size, own_goal)
+    def run(size, line):
+        total = PLANES * size
+        back_rows = outward(size, own_goal)[1]
+        weight = gather_all(own_share, "dp", stripes)
+        scaled_z = across(
+            route(line, outward(size, own_goal ^ plane)[0], [scaled], [size] * PLANES)
+        )
+        leaving = route(line, outward(size, own_goal)[0], [acts], [total])[0]
+        line.last += scaled_z[1:]
+        acts_z = planes_swap(hold(line, leaving))
+        got_scaled = at_owner(near(route(line, inward(size, True)[0], scaled_z, blocks_out)))
+        weight = gather_all(hold(line, weight), "dp", lanes_of)
         spread, gather = inward(size)
-        line = Line()
-        total = PLANES * size
-        acts_z = planes_swap(route(line, out_rows, [acts], [total])[0])
-        weight = gather_all(weight_z, "dp", lanes_of)
-        got_scaled = at_owner(near(scaled_sent))
         back_low = back_project(line, adapter_up_slots, got_scaled)
         terms = adapter_terms(line, back_low, adapter_down_slots, owner_outs)
         terms = near(from_owner(terms))
+        main = planes_swap(route(line, gather, terms, [total], (0, PLANES - 1, PLANES))[0])
+        got = route(line, spread, [acts_z], blocks_out)
         weight = gather_all(hold(line, weight), "groups")
-        terms_z = planes_swap(route(line, gather, terms, [total])[0])
-        got = at_owner(near(route(line, spread, [acts_z], blocks_out)))
-        weight = gather_all(hold(line, weight), "dp", pairs)
+        last = planes_swap(route(line, gather, terms, [total], (PLANES - 1, PLANES, PLANES))[0])
+        got = at_owner(near(got))
         low, grad_a = owner_step(line, back_low, adapter_down_slots, got)
         grad_b = up_gradient(line, low, got_scaled)
-        result = final_step(line, scaled, shape_weight(weight), back_rows, terms_z)
+        line.last += [main]
+        weight = gather_all(hold(line, weight), "dp", pairs)
+        result = final_step(line, scaled, shape_weight(weight), back_rows, main, last)
         return result, grad_a, grad_b
 
-    steps = [most * 5 // 8, most * 3 // 4, most]
-    which = sum((need_all > s).astype(jnp.int32) for s in steps[:-1])
-    return lax.switch(which, [functools.partial(run, s) for s in steps])
+    size = most * 3 // 4
+
+    def again(state):
+        return (jnp.zeros_like(state[0]), *run(most, Line()))
+
+    return lax.while_loop(
+        lambda state: state[0] > 0,
+        again,
+        ((need_all > size).astype(jnp.int32), *run(size, first)),
+    )[1:]
 
 
 def solution(mesh):

time: 306 us -> 377 us (1.23)
  waiting for transfers between devices: 196 us -> 227 us
  starting transfers between devices: 28.6 us -> 52.6 us
  Pallas kernels: 37.4 us -> 46.1 us
  other arithmetic: 8.36 us -> 13.6 us
    all_gather x4, waiting for transfers between devices: 19 us -> 51.2 us  [gather_all(): return lax.all_gather(x, axis, axis=0, tiled=True, axis_index_groups=groups)]
    all_to_all x2 -> x3, starting transfers between devices: 9.81 us -> 34.2 us  [planes_swap(): lax.all_to_all(x, 'dp', split_axis=0, concat_axis=0, tiled=True, axis_ind...]
    unnamed x8 -> x61, local copies, waits for them, and re-layouts: 1.11 us -> 17.6 us
    cond x28 -> x0, local copies, waits for them, and re-layouts: 15.1 us -> none
    all_to_all x1, waiting for transfers between devices: 16.7 us -> 3.5 us  [shards(): lax.all_to_all(note, ('groups', 'dp'), split_axis=0, concat_axis=0, tiled...]
    ppermute x9, waiting for transfers between devices: 138 us -> 149 us  [near(): lax.ppermute(bufs[s], 'dp', [(d, d ^ s) for d in range(devices)])]
    pallas_call x12 -> x15, Pallas kernels: 37.4 us -> 46.1 us  [call(): pl.pallas_call(kernel, grid=(pieces,), in_specs=in_specs + [HERE] * len(a...]
    all_to_all x2 -> x3, waiting for transfers between devices: 21.4 us -> 22.2 us  [planes_swap(): lax.all_to_all(x, 'dp', split_axis=0, concat_axis=0, tiled=True, axis_ind...]
  transfers between devices with their start and end apart: 19 -> 20, of which waited for: 12 -> 9; matrix products, arithmetic and copies ran while one was open for 2% -> 2% of each run, Pallas kernels for 9% -> 9%
where the time goes in v4:
time: 377 us; the launch traced here: 375 us
  waiting for transfers between devices  227 us (60%)
  starting transfers between devices  52.6 us (14%)
  Pallas kernels  46.1 us (12%)
  local copies, waits for them, and re-layouts  19.9 us (5%)
  between operations  15.5 us (4%)
  other arithmetic  13.6 us (4%)
    ppermute x9, waiting for transfers between devices, near(): lax.ppermute(bufs[s], 'dp', [(d, d ^ s) for d in range(devices)])  149 us
    all_gather x4, waiting for transfers between devices, gather_all(): return lax.all_gather(x, axis, axis=0, tiled=True, axis_index_groups=groups)  51.2 us
    pallas_call x15, Pallas kernels, call(): pl.pallas_call(kernel, grid=(pieces,), in_specs=in_specs + [HERE] * len(a...  46.1 us
    all_to_all x3, starting transfers between devices, planes_swap(): lax.all_to_all(x, 'dp', split_axis=0, concat_axis=0, tiled=True, axis_ind...  34.2 us
    all_to_all x3, waiting for transfers between devices, planes_swap(): lax.all_to_all(x, 'dp', split_axis=0, concat_axis=0, tiled=True, axis_ind...  22.2 us
    unnamed x61, local copies, waits for them, and re-layouts  17.6 us
  transfers between devices with their start and end apart: 20, of which 9 were waited for; matrix products, arithmetic and copies ran while one was open for 2% of the time, Pallas kernels for 9%

profile of v4, /device:TPU:1, one launch (start us, length us, event | category | flops | bytes accessed | tf_op | source)
XLA Modules:
  0.0 374.6 jit_solution(2414373794816192683)
XLA Ops:
  19.7 3.5 shard_map.103
  25.4 2.3 collective-permute-start.13
  27.7 7.0 %all-to-all-start.3 = ((s32[32,1,384]{2,1,0:T(1,128)}), s32[32,1,384]{2,1,0:T(1,128)S(1)}, u32[]{:S(2)}, u32[]{:S(2)}) async-start(s32[32,1,384]{2,1,0:T(1,128)} %broadcast_in_dim.93.refs_2_), calls=%async_computation.3 | async-start | bytes 98304 | tf_op jit(solution)/shard_map/all_to_all | solution.py:275
  35.7 5.1 %shard_map.104.refs_5_.refs_1_ = bf16[384,5120]{1,0:T(8,128)(2,1)} custom-call(bf16[384,256]{1,0:T(8,128)(2,1)S(1)} %fusion.14.refs_0_, bf16[256,5120]{1,0:T(8,128)(2,1)} %refs_1_.3, bf16[96,1024]{1,0:T(8,128)(2,1)S(1)} %copy-done.40), custom_call_target="tpu_custom_call" | custom-call | flops 1 | bytes 1 | tf_op jit(solution)/shard_map/pallas_call | solution.py:56
  40.8 4.5 %copy.37.refs_0_ = bf16[384,5120]{1,0:T(8,128)(2,1)} copy(bf16[384,5120]{1,0:T(8,128)(2,1)} %shard_map.104.refs_5_.refs_1_) | data formatting | bytes 7864320
  45.3 3.5 all-to-all-done.3
  48.8 4.9 %all-to-all-start.4 = ((bf16[4,96,5120]{2,1,0:T(8,128)(2,1)}), bf16[4,96,5120]{2,1,0:T(8,128)(2,1)}, u32[]{:S(2)}, u32[]{:S(2)}) async-start(bf16[4,96,5120]{2,1,0:T(8,128)(2,1)} %bitcast.89), calls=%async_computation.4 | async-start | bytes 7864320 | tf_op jit(solution)/shard_map/all_to_all | solution.py:361
  58.3 2.3 shard_map.105
  60.5 51.2 %all-gather.9.cloned.1.call-done.refs_0_ = bf16[640,1024]{1,0:T(8,128)(2,1)} async-done(((bf16[160,1024]{1,0:T(8,128)(2,1)}), bf16[640,1024]{1,0:T(8,128)(2,1)}) %all-gather.9.cloned.1.call-update) | async-done | bytes 1310736 | tf_op jit(solution)/shard_map/all_gather | solution.py:366
  115.0 6.4 %collective-permute-done.16 = bf16[128,1024]{1,0:T(8,128)(2,1)S(1)} collective-permute-done((bf16[128,1024]{1,0:T(8,128)(2,1)}, bf16[128,1024]{1,0:T(8,128)(2,1)S(1)}, u32[]{:S(2)}, u32[]{:S(2)}) %collective-permute-start.16) | collective-permute-done | bytes 262176 | tf_op jit(solution)/shard_map/ppermute | solution.py:334
  121.4 6.2 %collective-permute-done.17 = bf16[128,1024]{1,0:T(8,128)(2,1)S(1)} collective-permute-done((bf16[128,1024]{1,0:T(8,128)(2,1)}, bf16[128,1024]{1,0:T(8,128)(2,1)S(1)}, u32[]{:S(2)}, u32[]{:S(2)}) %collective-permute-start.17) | collective-permute-done | bytes 262176 | tf_op jit(solution)/shard_map/ppermute | solution.py:334
  129.1 3.8 %shard_map.109 = (bf16[2,64,5120]{2,1,0:T(8,128)(2,1)}, bf16[2,64,5120]{2,1,0:T(8,128)(2,1)}, bf16[2,64,5120]{2,1,0:T(8,128)(2,1)}, bf16[2,64,5120]{2,1,0:T(8,128)(2,1)}) custom-call(bf16[2,256,128]{2,1,0:T(8,128)(2,1)S(1)} %shard_map.108.refs_0_.refs_2_, bf16[2,5120,128]{2,1,0:T(8,128)(2,1)S(1)} %copy-done.42, ...), custom_call_target="tpu_custom_call" | custom-call | flops 1 | bytes 1 | tf_op jit(solution)/shard_map/pallas_call | solution.py:56
  136.1 37.2 %collective-permute-done.19.refs_3_ = bf16[128,5120]{1,0:T(8,128)(2,1)S(1)} collective-permute-done((bf16[128,5120]{1,0:T(8,128)(2,1)}, bf16[128,5120]{1,0:T(8,128)(2,1)S(1)}, u32[]{:S(2)}, u32[]{:S(2)}) %collective-permute-start.19) | collective-permute-done | bytes 1310752 | tf_op jit(solution)/shard_map/ppermute | solution.py:334
  173.3 46.6 %collective-permute-done.20.refs_4_ = bf16[128,5120]{1,0:T(8,128)(2,1)} collective-permute-done((bf16[128,5120]{1,0:T(8,128)(2,1)}, bf16[128,5120]{1,0:T(8,128)(2,1)}, u32[]{:S(2)}, u32[]{:S(2)}) %collective-permute-start.20) | collective-permute-done | bytes 1310752 | tf_op jit(solution)/shard_map/ppermute | solution.py:334
  221.3 4.8 %shard_map.110.refs_2_ = bf16[384,3840]{1,0:T(8,128)(2,1)} custom-call(bf16[384,512]{1,0:T(8,128)(2,1)S(1)} %fusion.11.refs_0_, bf16[128,5120]{1,0:T(8,128)(2,1)S(1)} %bitcast.73, bf16[128,5120]{1,0:T(8,128)(2,1)S(1)} %collective-permute-done.18.refs_2_, bf16[128,5120]{1,0:T(8,128)(2,1)S(1)} %collective-permute-done.19.refs_3_, ...), custom_call_target="tpu_custom_call" | custom-call | flops 1 | bytes 1 | tf_op jit(solution)/shard_map/pallas_call | solution.py:56
  228.9 6.5 %shard_map.111 = (bf16[128,5120]{1,0:T(8,128)(2,1)}, bf16[128,5120]{1,0:T(8,128)(2,1)}, bf16[128,5120]{1,0:T(8,128)(2,1)}, bf16[128,5120]{1,0:T(8,128)(2,1)}) custom-call(bf16[512,384]{1,0:T(8,128)(2,1)S(1)} %copy-done.35, bf16[384,5120]{1,0:T(8,128)(2,1)} %bitcast.2.refs_1_, bf16[384,3840]{1,0:T(8,128)(2,1)S(1)} %copy-done.18), custom_call_target="tpu_custom_call" | custom-call | flops 1 | bytes 1 | tf_op jit(solution)/shard_map/pallas_call | solution.py:56
  236.7 24.4 %all-to-all-start.5 = ((bf16[4,96,3840]{2,1,0:T(8,128)(2,1)}), bf16[4,96,3840]{2,1,0:T(8,128)(2,1)}, u32[]{:S(2)}, u32[]{:S(2)}) async-start(bf16[4,96,3840]{2,1,0:T(8,128)(2,1)} %bitcast.66), calls=%async_computation.5 | async-start | bytes 5898240 | tf_op jit(solution)/shard_map/all_to_all | solution.py:361
  265.0 2.9 shard_map.113.refs_6_
  267.9 24.6 %collective-permute-done.22 = bf16[128,5120]{1,0:T(8,128)(2,1)S(1)} collective-permute-done((bf16[128,5120]{1,0:T(8,128)(2,1)}, bf16[128,5120]{1,0:T(8,128)(2,1)S(1)}, u32[]{:S(2)}, u32[]{:S(2)}) %collective-permute-start.22) | collective-permute-done | bytes 1310752 | tf_op jit(solution)/shard_map/ppermute | solution.py:334
  292.4 28.6 %collective-permute-done.23 = bf16[128,5120]{1,0:T(8,128)(2,1)S(1)} collective-permute-done((bf16[128,5120]{1,0:T(8,128)(2,1)}, bf16[128,5120]{1,0:T(8,128)(2,1)S(1)}, u32[]{:S(2)}, u32[]{:S(2)}) %collective-permute-start.23) | collective-permute-done | bytes 1310752 | tf_op jit(solution)/shard_map/ppermute | solution.py:334
  322.1 6.0 %shard_map.114 = (f32[2,256,128]{2,1,0:T(8,128)S(1)}, bf16[2,5120,128]{2,1,0:T(8,128)(2,1)}) custom-call(bf16[2,256,128]{2,1,0:T(8,128)(2,1)S(1)} %shard_map.108.refs_0_.refs_2_, bf16[2,5120,128]{2,1,0:T(8,128)(2,1)S(1)} %copy-done.43, bf16[2,64,5120]{2,1,0:T(8,128)(2,1)S(1)} %bitcast.75, bf16[2,64,5120]{2,1,0:T(8,128)(2,1)S(1)} %bitcast.79, ...), custom_call_target="tpu_custom_call" | custom-call | flops 1 | bytes 1 | tf_op jit(solution)/shard_map/pallas_call | solution.py:56
  328.5 4.8 %all-to-all-start.6 = ((bf16[4,96,1280]{2,1,0:T(8,128)(2,1)}), bf16[4,96,1280]{2,1,0:T(8,128)(2,1)S(1)}, u32[]{:S(2)}, u32[]{:S(2)}) async-start(bf16[4,96,1280]{2,1,0:T(8,128)(2,1)} %bitcast.18), calls=%async_computation.6 | async-start | bytes 1966080 | tf_op jit(solution)/shard_map/all_to_all | solution.py:361
  335.4 22.2 %all-to-all-done.6 = bf16[4,96,1280]{2,1,0:T(8,128)(2,1)S(1)} async-done(((bf16[4,96,1280]{2,1,0:T(8,128)(2,1)}), bf16[4,96,1280]{2,1,0:T(8,128)(2,1)S(1)}, u32[]{:S(2)}, u32[]{:S(2)}) %all-to-all-start.6) | async-done | bytes 983072 | tf_op jit(solution)/shard_map/all_to_all | solution.py:361
  357.6 9.4 %shard_map.117 = bf16[256,5120]{1,0:T(8,128)(2,1)} custom-call(bf16[256,1024]{1,0:T(8,128)(2,1)} %multiply_convert_fusion.refs_1_.refs_0_, bf16[2,2,2,4,160,1024]{5,4,3,2,1,0:T(8,128)(2,1)} %bitcast.90, bf16[256,384]{1,0:T(8,128)(2,1)S(1)} %fusion.15.refs_2_, bf16[384,3840]{1,0:T(8,128)(2,1)} %bitcast.16.refs_2_.refs_3_.refs_6_, ...), custom_call_target="tpu_custom_call" | custom-call | flops 1 | bytes 1 | tf_op jit(solution)/shard_map/pallas_call | solution.py:56
  (134 shorter events, 40.7 us)
Async XLA Ops:
  23.2 22.1 %collective-permute-start.12 = (bf16[96,1024]{1,0:T(8,128)(2,1)}, bf16[96,1024]{1,0:T(8,128)(2,1)S(1)}, u32[]{:S(2)}, u32[]{:S(2)}) collective-permute-start(bf16[96,1024]{1,0:T(8,128)(2,1)} %get-tuple-element.118), channel_id=1, source_target_pairs={{0,4},{1,5},{2,6},{3,7},{4,0},{5,1},{6,2},{7,3},{8,12},{9,13},{10,... | collective-permute-start | bytes 589832 | tf_op jit(solution)/shard_map/ppermute | solution.py:312
  25.4 19.9 %collective-permute-start.13 = (bf16[96,1024]{1,0:T(8,128)(2,1)}, bf16[96,1024]{1,0:T(8,128)(2,1)S(1)}, u32[]{:S(2)}, u32[]{:S(2)}) collective-permute-start(bf16[96,1024]{1,0:T(8,128)(2,1)} %get-tuple-element.119), channel_id=1, source_target_pairs={{0,8},{1,9},{2,10},{3,11},{4,12},{5,13},{6,14},{7,15},{8,0},{9,1},... | collective-permute-start | bytes 589832 | tf_op jit(solution)/shard_map/ppermute | solution.py:312
  27.7 17.6 %collective-permute-start.14 = (bf16[96,1024]{1,0:T(8,128)(2,1)}, bf16[96,1024]{1,0:T(8,128)(2,1)S(1)}, u32[]{:S(2)}, u32[]{:S(2)}) collective-permute-start(bf16[96,1024]{1,0:T(8,128)(2,1)} %get-tuple-element.120), channel_id=1, source_target_pairs={{0,12},{1,13},{2,14},{3,15},{4,8},{5,9},{6,10},{7,11},{8,4},{9,5},... | collective-permute-start | bytes 589832 | tf_op jit(solution)/shard_map/ppermute | solution.py:312
  27.7 21.1 %all-to-all-start.3 = ((s32[32,1,384]{2,1,0:T(1,128)}), s32[32,1,384]{2,1,0:T(1,128)S(1)}, u32[]{:S(2)}, u32[]{:S(2)}) async-start(s32[32,1,384]{2,1,0:T(1,128)} %broadcast_in_dim.93.refs_2_), calls=%async_computation.3 | async-start | bytes 98304 | tf_op jit(solution)/shard_map/all_to_all | solution.py:275
  48.8 177.2 %all-to-all-start.4 = ((bf16[4,96,5120]{2,1,0:T(8,128)(2,1)}), bf16[4,96,5120]{2,1,0:T(8,128)(2,1)}, u32[]{:S(2)}, u32[]{:S(2)}) async-start(bf16[4,96,5120]{2,1,0:T(8,128)(2,1)} %bitcast.89), calls=%async_computation.4 | async-start | bytes 7864320 | tf_op jit(solution)/shard_map/all_to_all | solution.py:361
  53.8 58.0 %all-gather.9.cloned.1.call-start = ((), (), s32[]{:S(2)}) async-start(), calls=%async_computation.7 | async-start | bytes 1638400 | tf_op jit(solution)/shard_map/all_gather | solution.py:366
  54.5 180.8 %all-gather.11.cloned.1.call-start = ((), (), s32[]{:S(2)}) async-start(), calls=%async_computation.8 | async-start | bytes 3932160 | tf_op jit(solution)/shard_map/all_gather | solution.py:366
  112.7 215.7 %all-gather.13.cloned.1.call-start = ((), (), s32[]{:S(2)}) async-start(), calls=%async_computation.9 | async-start | bytes 7864320 | tf_op jit(solution)/shard_map/all_gather | solution.py:366
  112.7 2.2 collective-permute-start.15
  113.3 8.1 %collective-permute-start.16 = (bf16[128,1024]{1,0:T(8,128)(2,1)}, bf16[128,1024]{1,0:T(8,128)(2,1)S(1)}, u32[]{:S(2)}, u32[]{:S(2)}) collective-permute-start(bf16[128,1024]{1,0:T(8,128)(2,1)} %get-tuple-element.123), channel_id=1, source_target_pairs={{0,2},{1,3},{2,0},{3,1},{4,6},{5,7},{6,4},{7,5},{8,10},{9,11},{10,... | collective-permute-start | bytes 786440 | tf_op jit(solution)/shard_map/ppermute | solution.py:334
  113.6 13.9 %collective-permute-start.17 = (bf16[128,1024]{1,0:T(8,128)(2,1)}, bf16[128,1024]{1,0:T(8,128)(2,1)S(1)}, u32[]{:S(2)}, u32[]{:S(2)}) collective-permute-start(bf16[128,1024]{1,0:T(8,128)(2,1)} %get-tuple-element.124), channel_id=1, source_target_pairs={{0,3},{1,2},{2,1},{3,0},{4,7},{5,6},{6,5},{7,4},{8,11},{9,10},{10,... | collective-permute-start | bytes 786440 | tf_op jit(solution)/shard_map/ppermute | solution.py:334
  132.9 3.3 collective-permute-start.18
  132.9 40.4 %collective-permute-start.19 = (bf16[128,5120]{1,0:T(8,128)(2,1)}, bf16[128,5120]{1,0:T(8,128)(2,1)S(1)}, u32[]{:S(2)}, u32[]{:S(2)}) collective-permute-start(bf16[128,5120]{1,0:T(8,128)(2,1)} %bitcast.99), channel_id=1, source_target_pairs={{0,2},{1,3},{2,0},{3,1},{4,6},{5,7},{6,4},{7,5},{8,10},{9,11},{10,... | collective-permute-start | bytes 3932168 | tf_op jit(solution)/shard_map/ppermute | solution.py:334
  133.3 86.7 %collective-permute-start.20 = (bf16[128,5120]{1,0:T(8,128)(2,1)}, bf16[128,5120]{1,0:T(8,128)(2,1)}, u32[]{:S(2)}, u32[]{:S(2)}) collective-permute-start(bf16[128,5120]{1,0:T(8,128)(2,1)} %bitcast.97), channel_id=1, source_target_pairs={{0,3},{1,2},{2,1},{3,0},{4,7},{5,6},{6,5},{7,4},{8,11},{9,10},{10,... | collective-permute-start | bytes 3932168 | tf_op jit(solution)/shard_map/ppermute | solution.py:334
  136.1 89.9 %copy-start.33 = (bf16[384,512]{1,0:T(8,128)(2,1)}, bf16[384,512]{1,0:T(8,128)(2,1)S(1)}, u32[]{:S(2)}) copy-start(bf16[384,512]{1,0:T(8,128)(2,1)S(1)} %fusion.11.refs_0_) | copy-start | bytes 1179652
  173.3 52.7 %copy-start.29 = (bf16[128,5120]{1,0:T(8,128)(2,1)}, bf16[128,5120]{1,0:T(8,128)(2,1)S(1)}, u32[]{:S(2)}) copy-start(bf16[128,5120]{1,0:T(8,128)(2,1)S(1)} %collective-permute-done.19.refs_3_) | copy-start | bytes 3932164
  236.7 91.7 %all-to-all-start.5 = ((bf16[4,96,3840]{2,1,0:T(8,128)(2,1)}), bf16[4,96,3840]{2,1,0:T(8,128)(2,1)}, u32[]{:S(2)}, u32[]{:S(2)}) async-start(bf16[4,96,3840]{2,1,0:T(8,128)(2,1)} %bitcast.66), calls=%async_computation.5 | async-start | bytes 5898240 | tf_op jit(solution)/shard_map/all_to_all | solution.py:361
  261.1 96.5 %all-gather.15.cloned.1.call-start = ((), (), s32[]{:S(2)}) async-start(), calls=%async_computation.10 | async-start | bytes 15728640 | tf_op jit(solution)/shard_map/all_gather | solution.py:366
  261.1 6.7 %collective-permute-start.21 = (bf16[128,5120]{1,0:T(8,128)(2,1)}, bf16[128,5120]{1,0:T(8,128)(2,1)S(1)}, u32[]{:S(2)}, u32[]{:S(2)}) collective-permute-start(bf16[128,5120]{1,0:T(8,128)(2,1)} %get-tuple-element.130), channel_id=1, source_target_pairs={{0,1},{1,0},{2,3},{3,2},{4,5},{5,4},{6,7},{7,6},{8,9},{9,8},{10,11... | collective-permute-start | bytes 3932168 | tf_op jit(solution)/shard_map/ppermute | solution.py:334
  261.8 30.6 %collective-permute-start.22 = (bf16[128,5120]{1,0:T(8,128)(2,1)}, bf16[128,5120]{1,0:T(8,128)(2,1)S(1)}, u32[]{:S(2)}, u32[]{:S(2)}) collective-permute-start(bf16[128,5120]{1,0:T(8,128)(2,1)} %get-tuple-element.131), channel_id=1, source_target_pairs={{0,2},{1,3},{2,0},{3,1},{4,6},{5,7},{6,4},{7,5},{8,10},{9,11},{10,... | collective-permute-start | bytes 3932168 | tf_op jit(solution)/shard_map/ppermute | solution.py:334
  262.5 59.6 %copy-start.28 = (bf16[128,5120]{1,0:T(8,128)(2,1)S(1)}, bf16[128,5120]{1,0:T(8,128)(2,1)}, u32[]{:S(2)}) copy-start(bf16[128,5120]{1,0:T(8,128)(2,1)} %get-tuple-element.129.refs_1_.refs_5_) | copy-start | bytes 3932164
  262.5 58.5 %collective-permute-start.23 = (bf16[128,5120]{1,0:T(8,128)(2,1)}, bf16[128,5120]{1,0:T(8,128)(2,1)S(1)}, u32[]{:S(2)}, u32[]{:S(2)}) collective-permute-start(bf16[128,5120]{1,0:T(8,128)(2,1)} %get-tuple-element.132), channel_id=1, source_target_pairs={{0,3},{1,2},{2,1},{3,0},{4,7},{5,6},{6,5},{7,4},{8,11},{9,10},{10,... | collective-permute-start | bytes 3932168 | tf_op jit(solution)/shard_map/ppermute | solution.py:334
  265.0 57.1 %copy-start.43 = (bf16[2,5120,128]{2,1,0:T(8,128)(2,1)S(1)}, bf16[2,5120,128]{2,1,0:T(8,128)(2,1)}, u32[]{:S(2)}) copy-start(bf16[2,5120,128]{2,1,0:T(8,128)(2,1)} %refs_1_.5) | copy-start | bytes 7864324
  328.5 29.1 %all-to-all-start.6 = ((bf16[4,96,1280]{2,1,0:T(8,128)(2,1)}), bf16[4,96,1280]{2,1,0:T(8,128)(2,1)S(1)}, u32[]{:S(2)}, u32[]{:S(2)}) async-start(bf16[4,96,1280]{2,1,0:T(8,128)(2,1)} %bitcast.18), calls=%async_computation.6 | async-start | bytes 1966080 | tf_op jit(solution)/shard_map/all_to_all | solution.py:361
  (25 other events, 203.0 us)
Sparse Core Ops, SparseCore 0:
  56.2 55.5 all-gather.8
  113.3 95.9 all-gather.10
  236.8 88.5 all-gather.12
  328.6 23.5 all-gather.14

commit v5 on v4

--- a/solution.py
+++ b/solution.py
@@ -49,22 +49,24 @@
     def call(self, body, operands, in_specs, out_specs, out_shape, pieces=1, aliases=None):
         after = self.last
         first = len(operands)
+        many = isinstance(out_shape, list)
 
         def kernel(*refs):
-            return body(*refs[:first], *refs[first + len(after) :])
+            refs[-1][...] = jnp.zeros_like(refs[-1])
+            return body(*refs[:first], *refs[first + len(after) : -1])
 
         out = pl.pallas_call(
             kernel,
             grid=(pieces,),
             in_specs=in_specs + [HERE] * len(after),
-            out_specs=out_specs,
-            out_shape=out_shape,
+            out_specs=(out_specs if many else [out_specs]) + [whole((8, 128))],
+            out_shape=(out_shape if many else [out_shape])
+            + [jax.ShapeDtypeStruct((8, 128), jnp.int32)],
             input_output_aliases=aliases or {},
-            cost_estimate=pl.CostEstimate(flops=1, bytes_accessed=1, transcendentals=0),
             compiler_params=PARAMS,
         )(*operands, *after)
-        self.last = [out[0] if isinstance(out, (list, tuple)) else out]
-        return out
+        self.last = [out[-1]]
+        return out[:-1] if many else out[0]
 
 
 def hold_body(ref, out):
@@ -406,19 +408,18 @@
             target[:, None] == spots[None, :]
         ).astype(BF)
 
-    def run(size, line):
+    weight_z = gather_all(own_share, "dp", stripes)
+    scaled_z = across(route(first, outward(most, own_goal ^ plane)[0], [scaled], [most] * PLANES))
+    scaled_sent = route(first, inward(most, True)[0], scaled_z, blocks_out)
+
+    def run(size):
+        line = Line()
         total = PLANES * size
-        back_rows = outward(size, own_goal)[1]
-        weight = gather_all(own_share, "dp", stripes)
-        scaled_z = across(
-            route(line, outward(size, own_goal ^ plane)[0], [scaled], [size] * PLANES)
-        )
-        leaving = route(line, outward(size, own_goal)[0], [acts], [total])[0]
-        line.last += scaled_z[1:]
-        acts_z = planes_swap(hold(line, leaving))
-        got_scaled = at_owner(near(route(line, inward(size, True)[0], scaled_z, blocks_out)))
-        weight = gather_all(hold(line, weight), "dp", lanes_of)
+        out_rows, back_rows = outward(size, own_goal)
         spread, gather = inward(size)
+        weight = gather_all(weight_z, "dp", lanes_of)
+        acts_z = planes_swap(route(line, out_rows, [acts], [total])[0])
+        got_scaled = at_owner(near(scaled_sent))
         back_low = back_project(line, adapter_up_slots, got_scaled)
         terms = adapter_terms(line, back_low, adapter_down_slots, owner_outs)
         terms = near(from_owner(terms))
@@ -434,16 +435,9 @@
         result = final_step(line, scaled, shape_weight(weight), back_rows, main, last)
         return result, grad_a, grad_b
 
-    size = most * 3 // 4
-
-    def again(state):
-        return (jnp.zeros_like(state[0]), *run(most, Line()))
-
-    return lax.while_loop(
-        lambda state: state[0] > 0,
-        again,
-        ((need_all > size).astype(jnp.int32), *run(size, first)),
-    )[1:]
+    steps = [most * 11 // 16, most * 13 // 16, most]
+    which = sum((need_all > s).astype(jnp.int32) for s in steps[:-1])
+    return lax.switch(which, [functools.partial(run, s) for s in steps])
 
 
 def solution(mesh):

time: 377 us -> 312 us (0.83)
  waiting for transfers between devices: 227 us -> 195 us
  starting transfers between devices: 52.6 us -> 32.7 us
  local copies, waits for them, and re-layouts: 19.9 us -> 11.7 us
  other arithmetic: 13.6 us -> 9.78 us
    all_gather x4, waiting for transfers between devices: 51.2 us -> 14.1 us  [gather_all(): return lax.all_gather(x, axis, axis=0, tiled=True, axis_index_groups=groups)]
    ppermute x3, waiting for transfers between devices: 0.01 us -> 20.8 us  [across(): lax.ppermute(bufs[s], 'dp', [(d, (d // column ^ s) * column + d % column)...]
    all_to_all x3, starting transfers between devices: 34.2 us -> 14.6 us  [planes_swap(): lax.all_to_all(x, 'dp', split_axis=0, concat_axis=0, tiled=True, axis_ind...]
    unnamed x61 -> x24, local copies, waits for them, and re-layouts: 17.6 us -> 2.69 us
    ppermute x9, waiting for transfers between devices: 149 us -> 137 us  [near(): lax.ppermute(bufs[s], 'dp', [(d, d ^ s) for d in range(devices)])]
    cond x0 -> x44, local copies, waits for them, and re-layouts: none -> 6.8 us
    pallas_call x15 -> x13, Pallas kernels: 46.1 us -> 45 us  [call(): pl.pallas_call(kernel, grid=(pieces,), in_specs=in_specs + [HERE] * len(a...]
  transfers between devices with their start and end apart: 20 -> 20, of which waited for: 9 -> 11; matrix products, arithmetic and copies ran while one was open for 2% -> 3% of each run, Pallas kernels for 9% -> 10%
where the time goes in v5:
time: 312 us; the launch traced here: 310 us
  waiting for transfers between devices  195 us (62%)
  Pallas kernels  45 us (14%)
  starting transfers between devices  32.7 us (10%)
  between operations  16 us (5%)
  local copies, waits for them, and re-layouts  11.7 us (4%)
  other arithmetic  9.78 us (3%)
    ppermute x9, waiting for transfers between devices, near(): lax.ppermute(bufs[s], 'dp', [(d, d ^ s) for d in range(devices)])  137 us
    pallas_call x13, Pallas kernels, call(): pl.pallas_call(kernel, grid=(pieces,), in_specs=in_specs + [HERE] * len(a...  45 us
    all_to_all x3, waiting for transfers between devices, planes_swap(): lax.all_to_all(x, 'dp', split_axis=0, concat_axis=0, tiled=True, axis_ind...  22.5 us
    ppermute x3, waiting for transfers between devices, across(): lax.ppermute(bufs[s], 'dp', [(d, (d // column ^ s) * column + d % column)...  20.8 us
    all_to_all x3, starting transfers between devices, planes_swap(): lax.all_to_all(x, 'dp', split_axis=0, concat_axis=0, tiled=True, axis_ind...  14.6 us
    all_gather x4, waiting for transfers between devices, gather_all(): return lax.all_gather(x, axis, axis=0, tiled=True, axis_index_groups=groups)  14.1 us
    ppermute x9, starting transfers between devices, near(): lax.ppermute(bufs[s], 'dp', [(d, d ^ s) for d in range(devices)])  7.36 us
    all_to_all x1, starting transfers between devices, shards(): lax.all_to_all(note, ('groups', 'dp'), split_axis=0, concat_axis=0, tiled...  7.1 us
  transfers between devices with their start and end apart: 20, of which 11 were waited for; matrix products, arithmetic and copies ran while one was open for 3% of the time, Pallas kernels for 10%

profile of v5, /device:TPU:1, one launch (start us, length us, event | category | flops | bytes accessed | tf_op | source)
XLA Modules:
  0.0 310.1 jit_solution(13083046568215135009)
XLA Ops:
  10.1 7.1 %all-to-all-start.9 = ((s32[32,1,384]{2,1,0:T(1,128)}), s32[32,1,384]{2,1,0:T(1,128)S(1)}, u32[]{:S(2)}, u32[]{:S(2)}) async-start(s32[32,1,384]{2,1,0:T(1,128)} %broadcast_in_dim.92.refs_2_), calls=%async_computation.9 | async-start | bytes 98304 | tf_op jit(solution)/shard_map/all_to_all | solution.py:277
  34.2 5.6 %collective-permute-done.27.refs_2_ = bf16[128,1024]{1,0:T(8,128)(2,1)S(1)} collective-permute-done((bf16[128,1024]{1,0:T(8,128)(2,1)}, bf16[128,1024]{1,0:T(8,128)(2,1)S(1)}, u32[]{:S(2)}, u32[]{:S(2)}) %collective-permute-start.27) | collective-permute-done | bytes 262176 | tf_op jit(solution)/shard_map/ppermute | solution.py:314
  39.8 2.4 collective-permute-done.28.refs_3_
  42.2 12.8 %collective-permute-done.29.refs_4_ = bf16[128,1024]{1,0:T(8,128)(2,1)S(1)} collective-permute-done((bf16[128,1024]{1,0:T(8,128)(2,1)}, bf16[128,1024]{1,0:T(8,128)(2,1)S(1)}, u32[]{:S(2)}, u32[]{:S(2)}) %collective-permute-start.29) | collective-permute-done | bytes 262176 | tf_op jit(solution)/shard_map/ppermute | solution.py:314
  56.0 2.3 shard_map.104
  58.3 14.1 %all-gather.29.cloned.1.call-done = bf16[640,1024]{1,0:T(8,128)(2,1)} async-done(((bf16[160,1024]{1,0:T(8,128)(2,1)}), bf16[640,1024]{1,0:T(8,128)(2,1)}) %all-gather.29.cloned.1.call-update) | async-done | bytes 1310736 | tf_op jit(solution)/shard_map/all_gather | solution.py:368
  72.4 230.1 %conditional.1 = (bf16[256,5120]{1,0:T(8,128)(2,1)}, bf16[2,5120,128]{2,1,0:T(8,128)(2,1)}, bf16[2,128,1024]{2,1,0:T(8,128)(2,1)}) conditional(s32[]{:T(128)} %clamp.11, (bf16[640,1024]{1,0:T(8,128)(2,1)}, s32[4,256]{1,0:T(4,128)S(1)}, s32[4,256]{1,0:T(4,128)S(1)}, s32[256]{0:T(256)S(1)}, s32[256]{0:T(256)S(1)}, ...), branch_computations={%region_11.13_spmd, %region_13.15_spmd, %region_15.17_spmd} | conditional | flops 2099712 | bytes 205828192 | solution.py:440
  72.5 3.4 %branch_0_fun.11 = (bf16[352,5120]{1,0:T(8,128)(2,1)}, s32[8,128]{1,0:T(8,128)S(1)}) custom-call(bf16[352,256]{1,0:T(8,128)(2,1)S(1)} %fusion.4.refs_0_, bf16[256,5120]{1,0:T(8,128)(2,1)S(1)} %get-tuple-element.84.refs_1_), custom_call_target="tpu_custom_call" | custom-call | tf_op jit(solution)/shard_map/cond/branch_0_fun/pallas_call | solution.py:58
  75.8 4.9 %all-to-all-start = ((bf16[4,88,5120]{2,1,0:T(8,128)(2,1)}), bf16[4,88,5120]{2,1,0:T(8,128)(2,1)}, u32[]{:S(2)}, u32[]{:S(2)}) async-start(bf16[4,88,5120]{2,1,0:T(8,128)(2,1)} %bitcast.130), calls=%async_computation | async-start | bytes 7208960 | tf_op jit(solution)/shard_map/cond/branch_0_fun/all_to_all | solution.py:363
  83.8 6.3 %collective-permute-done.1 = bf16[128,1024]{1,0:T(8,128)(2,1)S(1)} collective-permute-done((bf16[128,1024]{1,0:T(8,128)(2,1)S(1)}, bf16[128,1024]{1,0:T(8,128)(2,1)S(1)}, u32[]{:S(2)}, u32[]{:S(2)}) %collective-permute-start.1) | collective-permute-done | bytes 262176 | tf_op jit(solution)/shard_map/cond/branch_0_fun/ppermute | solution.py:336
  90.1 7.2 %collective-permute-done.2 = bf16[128,1024]{1,0:T(8,128)(2,1)S(1)} collective-permute-done((bf16[128,1024]{1,0:T(8,128)(2,1)S(1)}, bf16[128,1024]{1,0:T(8,128)(2,1)S(1)}, u32[]{:S(2)}, u32[]{:S(2)}) %collective-permute-start.2) | collective-permute-done | bytes 262176 | tf_op jit(solution)/shard_map/cond/branch_0_fun/ppermute | solution.py:336
  98.5 5.4 %branch_0_fun.13 = (bf16[2,64,5120]{2,1,0:T(8,128)(2,1)}, bf16[2,64,5120]{2,1,0:T(8,128)(2,1)}, bf16[2,64,5120]{2,1,0:T(8,128)(2,1)}, bf16[2,64,5120]{2,1,0:T(8,128)(2,1)}, s32[8,128]{1,0:T(8,128)S(1)}) custom-call(bf16[2,256,128]{2,1,0:T(8,128)(2,1)S(1)} %get-tuple-element.92.refs_0_, bf16[2,5120,128]{2,1,0:T(8,128)(2,1)} %get-tuple-element.93.refs_1_, ...), custom_call_target="tpu_custom_call" | custom-call | tf_op jit(solution)/shard_map/cond/branch_0_fun/pallas_call | solution.py:58
  107.3 44.8 %collective-permute-done.4.refs_3_ = bf16[128,5120]{1,0:T(8,128)(2,1)S(1)} collective-permute-done((bf16[128,5120]{1,0:T(8,128)(2,1)}, bf16[128,5120]{1,0:T(8,128)(2,1)S(1)}, u32[]{:S(2)}, u32[]{:S(2)}) %collective-permute-start.4) | collective-permute-done | bytes 1310752 | tf_op jit(solution)/shard_map/cond/branch_0_fun/ppermute | solution.py:336
  152.1 28.1 %collective-permute-done.5.refs_4_ = bf16[128,5120]{1,0:T(8,128)(2,1)} collective-permute-done((bf16[128,5120]{1,0:T(8,128)(2,1)}, bf16[128,5120]{1,0:T(8,128)(2,1)}, u32[]{:S(2)}, u32[]{:S(2)}) %collective-permute-start.5) | collective-permute-done | bytes 1310752 | tf_op jit(solution)/shard_map/cond/branch_0_fun/ppermute | solution.py:336
  181.5 4.6 %branch_0_fun.14 = (bf16[352,3840]{1,0:T(8,128)(2,1)}, s32[8,128]{1,0:T(8,128)S(1)}) custom-call(bf16[352,512]{1,0:T(8,128)(2,1)S(1)} %fusion.1.refs_0_, bf16[128,5120]{1,0:T(8,128)(2,1)S(1)} %bitcast.84, bf16[128,5120]{1,0:T(8,128)(2,1)S(1)} %collective-permute-done.3.refs_2_, bf16[128,5120]{1,0:T(8,128)(2,1)S(1)} %collective-permute-done.4.refs_3_, ...), custom_call_target="tpu_custom_call" | custom-call | tf_op jit(solution)/shard_map/cond/branch_0_fun/pallas_call | solution.py:58
  186.1 6.4 %branch_0_fun.15 = (bf16[128,5120]{1,0:T(8,128)(2,1)}, bf16[128,5120]{1,0:T(8,128)(2,1)}, bf16[128,5120]{1,0:T(8,128)(2,1)}, bf16[128,5120]{1,0:T(8,128)(2,1)}, s32[8,128]{1,0:T(8,128)S(1)}) custom-call(bf16[512,352]{1,0:T(8,128)(2,1)S(1)} %fusion.refs_0_, bf16[352,5120]{1,0:T(8,128)(2,1)} %bitcast.1.refs_1_, s32[8,128]{1,0:T(8,128)S(1)} %get-tuple-element.100.refs_2_), custom_call_target="tpu_custom_call" | custom-call | tf_op jit(solution)/shard_map/cond/branch_0_fun/pallas_call | solution.py:58
  193.1 4.8 %all-to-all-start.1 = ((bf16[4,88,3840]{2,1,0:T(8,128)(2,1)}), bf16[4,88,3840]{2,1,0:T(8,128)(2,1)S(1)}, u32[]{:S(2)}, u32[]{:S(2)}) async-start(bf16[4,88,3840]{2,1,0:T(8,128)(2,1)} %bitcast.132), calls=%async_computation.1 | async-start | bytes 5406720 | tf_op jit(solution)/shard_map/cond/branch_0_fun/all_to_all | solution.py:363
  204.8 2.7 branch_0_fun.17
  207.6 21.7 %collective-permute-done.7 = bf16[128,5120]{1,0:T(8,128)(2,1)S(1)} collective-permute-done((bf16[128,5120]{1,0:T(8,128)(2,1)}, bf16[128,5120]{1,0:T(8,128)(2,1)S(1)}, u32[]{:S(2)}, u32[]{:S(2)}) %collective-permute-start.7) | collective-permute-done | bytes 1310752 | tf_op jit(solution)/shard_map/cond/branch_0_fun/ppermute | solution.py:336
  229.2 28.6 %collective-permute-done.8 = bf16[128,5120]{1,0:T(8,128)(2,1)S(1)} collective-permute-done((bf16[128,5120]{1,0:T(8,128)(2,1)}, bf16[128,5120]{1,0:T(8,128)(2,1)S(1)}, u32[]{:S(2)}, u32[]{:S(2)}) %collective-permute-start.8) | collective-permute-done | bytes 1310752 | tf_op jit(solution)/shard_map/cond/branch_0_fun/ppermute | solution.py:336
  257.8 6.1 %branch_0_fun.18 = (f32[2,256,128]{2,1,0:T(8,128)S(1)}, bf16[2,5120,128]{2,1,0:T(8,128)(2,1)}, s32[8,128]{1,0:T(8,128)S(1)}) custom-call(bf16[2,256,128]{2,1,0:T(8,128)(2,1)S(1)} %copy-done.41, bf16[2,5120,128]{2,1,0:T(8,128)(2,1)} %get-tuple-element.93.refs_1_, bf16[2,64,5120]{2,1,0:T(8,128)(2,1)S(1)} %bitcast.88, bf16[2,64,5120]{2,1,0:T(8,128)(2,1)S(1)} %bitcast.91, ...), custom_call_target="tpu_custom_call" | custom-call | tf_op jit(solution)/shard_map/cond/branch_0_fun/pallas_call | solution.py:58
  265.7 5.0 %all-to-all-start.2 = ((bf16[4,88,1280]{2,1,0:T(8,128)(2,1)}), bf16[4,88,1280]{2,1,0:T(8,128)(2,1)}, u32[]{:S(2)}, u32[]{:S(2)}) async-start(bf16[4,88,1280]{2,1,0:T(8,128)(2,1)} %bitcast.134), calls=%async_computation.2 | async-start | bytes 1802240 | tf_op jit(solution)/shard_map/cond/branch_0_fun/all_to_all | solution.py:363
  270.7 22.5 %all-to-all-done.2 = bf16[4,88,1280]{2,1,0:T(8,128)(2,1)} async-done(((bf16[4,88,1280]{2,1,0:T(8,128)(2,1)}), bf16[4,88,1280]{2,1,0:T(8,128)(2,1)}, u32[]{:S(2)}, u32[]{:S(2)}) %all-to-all-start.2) | async-done | bytes 901152 | tf_op jit(solution)/shard_map/cond/branch_0_fun/all_to_all | solution.py:363
  293.3 9.2 %branch_0_fun.21 = (bf16[256,5120]{1,0:T(8,128)(2,1)}, s32[8,128]{1,0:T(8,128)}) custom-call(bf16[256,1024]{1,0:T(8,128)(2,1)S(1)} %copy-done.49, bf16[2,2,2,4,160,1024]{5,4,3,2,1,0:T(8,128)(2,1)} %bitcast.118, bf16[256,352]{1,0:T(8,128)(2,1)S(1)} %fusion.2.refs_2_, bf16[352,3840]{1,0:T(8,128)(2,1)S(1)} %bitcast.79, bf16[352,1280]{1,0:T(8,128)(2,1)} %bitcast.18.refs_4_, ...), custom_call_target="tpu_custom_call" | custom-call | tf_op jit(solution)/shard_map/cond/branch_0_fun/pallas_call | solution.py:58
  (142 shorter events, 38.2 us)
Async XLA Ops:
  10.1 18.0 %all-to-all-start.9 = ((s32[32,1,384]{2,1,0:T(1,128)}), s32[32,1,384]{2,1,0:T(1,128)S(1)}, u32[]{:S(2)}, u32[]{:S(2)}) async-start(s32[32,1,384]{2,1,0:T(1,128)} %broadcast_in_dim.92.refs_2_), calls=%async_computation.9 | async-start | bytes 98304 | tf_op jit(solution)/shard_map/all_to_all | solution.py:277
  17.2 55.2 %all-gather.29.cloned.1.call-start = ((), (), s32[]{:S(2)}) async-start(), calls=%async_computation.19 | async-start | bytes 1638400 | tf_op jit(solution)/shard_map/all_gather | solution.py:368
  19.7 52.7 %copy-start.47 = (bf16[256,5120]{1,0:T(8,128)(2,1)S(1)}, bf16[256,5120]{1,0:T(8,128)(2,1)}, u32[]{:S(2)}) copy-start(bf16[256,5120]{1,0:T(8,128)(2,1)} %param.11) | copy-start | bytes 7864324
  23.3 16.5 %collective-permute-start.27 = (bf16[128,1024]{1,0:T(8,128)(2,1)}, bf16[128,1024]{1,0:T(8,128)(2,1)S(1)}, u32[]{:S(2)}, u32[]{:S(2)}) collective-permute-start(bf16[128,1024]{1,0:T(8,128)(2,1)} %get-tuple-element.208), channel_id=1, source_target_pairs={{0,4},{1,5},{2,6},{3,7},{4,0},{5,1},{6,2},{7,3},{8,12},{9,13},{10,... | collective-permute-start | bytes 786440 | tf_op jit(solution)/shard_map/ppermute | solution.py:314
  24.7 17.5 %collective-permute-start.28 = (bf16[128,1024]{1,0:T(8,128)(2,1)}, bf16[128,1024]{1,0:T(8,128)(2,1)S(1)}, u32[]{:S(2)}, u32[]{:S(2)}) collective-permute-start(bf16[128,1024]{1,0:T(8,128)(2,1)} %get-tuple-element.209), channel_id=1, source_target_pairs={{0,8},{1,9},{2,10},{3,11},{4,12},{5,13},{6,14},{7,15},{8,0},{9,1},... | collective-permute-start | bytes 786440 | tf_op jit(solution)/shard_map/ppermute | solution.py:314
  26.8 28.2 %collective-permute-start.29 = (bf16[128,1024]{1,0:T(8,128)(2,1)}, bf16[128,1024]{1,0:T(8,128)(2,1)S(1)}, u32[]{:S(2)}, u32[]{:S(2)}) collective-permute-start(bf16[128,1024]{1,0:T(8,128)(2,1)} %get-tuple-element.210), channel_id=1, source_target_pairs={{0,12},{1,13},{2,14},{3,15},{4,8},{5,9},{6,10},{7,11},{8,4},{9,5},... | collective-permute-start | bytes 786440 | tf_op jit(solution)/shard_map/ppermute | solution.py:314
  75.8 110.3 %all-to-all-start = ((bf16[4,88,5120]{2,1,0:T(8,128)(2,1)}), bf16[4,88,5120]{2,1,0:T(8,128)(2,1)}, u32[]{:S(2)}, u32[]{:S(2)}) async-start(bf16[4,88,5120]{2,1,0:T(8,128)(2,1)} %bitcast.130), calls=%async_computation | async-start | bytes 7208960 | tf_op jit(solution)/shard_map/cond/branch_0_fun/all_to_all | solution.py:363
  80.7 111.8 %all-gather.11.cloned.1.call-start = ((), (), s32[]{:S(2)}) async-start(), calls=%async_computation.10 | async-start | bytes 3932160 | tf_op jit(solution)/shard_map/cond/branch_0_fun/all_gather | solution.py:368
  81.5 183.6 %all-gather.13.cloned.1.call-start = ((), (), s32[]{:S(2)}) async-start(), calls=%async_computation.11 | async-start | bytes 7864320 | tf_op jit(solution)/shard_map/cond/branch_0_fun/all_gather | solution.py:368
  81.6 2.2 collective-permute-start
  82.1 8.0 %collective-permute-start.1 = (bf16[128,1024]{1,0:T(8,128)(2,1)S(1)}, bf16[128,1024]{1,0:T(8,128)(2,1)S(1)}, u32[]{:S(2)}, u32[]{:S(2)}) collective-permute-start(bf16[128,1024]{1,0:T(8,128)(2,1)S(1)} %copy-done.66), channel_id=1, source_target_pairs={{0,2},{1,3},{2,0},{3,1},{4,6},{5,7},{6,4},{7,5},{8,10},{9,11},{10,... | collective-permute-start | bytes 786440 | tf_op jit(solution)/shard_map/cond/branch_0_fun/ppermute | solution.py:336
  83.3 14.0 %collective-permute-start.2 = (bf16[128,1024]{1,0:T(8,128)(2,1)S(1)}, bf16[128,1024]{1,0:T(8,128)(2,1)S(1)}, u32[]{:S(2)}, u32[]{:S(2)}) collective-permute-start(bf16[128,1024]{1,0:T(8,128)(2,1)S(1)} %copy-done.67), channel_id=1, source_target_pairs={{0,3},{1,2},{2,1},{3,0},{4,7},{5,6},{6,5},{7,4},{8,11},{9,10},{10,... | collective-permute-start | bytes 786440 | tf_op jit(solution)/shard_map/cond/branch_0_fun/ppermute | solution.py:336
  104.0 3.4 %collective-permute-start.3 = (bf16[128,5120]{1,0:T(8,128)(2,1)}, bf16[128,5120]{1,0:T(8,128)(2,1)S(1)}, u32[]{:S(2)}, u32[]{:S(2)}) collective-permute-start(bf16[128,5120]{1,0:T(8,128)(2,1)} %bitcast.146), channel_id=1, source_target_pairs={{0,1},{1,0},{2,3},{3,2},{4,5},{5,4},{6,7},{7,6},{8,9},{9,8},{10,11... | collective-permute-start | bytes 3932168 | tf_op jit(solution)/shard_map/cond/branch_0_fun/ppermute | solution.py:336
  104.5 47.7 %collective-permute-start.4 = (bf16[128,5120]{1,0:T(8,128)(2,1)}, bf16[128,5120]{1,0:T(8,128)(2,1)S(1)}, u32[]{:S(2)}, u32[]{:S(2)}) collective-permute-start(bf16[128,5120]{1,0:T(8,128)(2,1)} %bitcast.143), channel_id=1, source_target_pairs={{0,2},{1,3},{2,0},{3,1},{4,6},{5,7},{6,4},{7,5},{8,10},{9,11},{10,... | collective-permute-start | bytes 3932168 | tf_op jit(solution)/shard_map/cond/branch_0_fun/ppermute | solution.py:336
  106.4 73.8 %collective-permute-start.5 = (bf16[128,5120]{1,0:T(8,128)(2,1)}, bf16[128,5120]{1,0:T(8,128)(2,1)}, u32[]{:S(2)}, u32[]{:S(2)}) collective-permute-start(bf16[128,5120]{1,0:T(8,128)(2,1)} %bitcast.140), channel_id=1, source_target_pairs={{0,3},{1,2},{2,1},{3,0},{4,7},{5,6},{6,5},{7,4},{8,11},{9,10},{10,... | collective-permute-start | bytes 3932168 | tf_op jit(solution)/shard_map/cond/branch_0_fun/ppermute | solution.py:336
  107.3 78.8 %copy-start.8 = (bf16[128,5120]{1,0:T(8,128)(2,1)}, bf16[128,5120]{1,0:T(8,128)(2,1)S(1)}, u32[]{:S(2)}) copy-start(bf16[128,5120]{1,0:T(8,128)(2,1)S(1)} %collective-permute-done.3.refs_2_) | copy-start | bytes 3932164 | tf_op jit(solution)/shard_map/cond
  193.1 71.9 %all-to-all-start.1 = ((bf16[4,88,3840]{2,1,0:T(8,128)(2,1)}), bf16[4,88,3840]{2,1,0:T(8,128)(2,1)S(1)}, u32[]{:S(2)}, u32[]{:S(2)}) async-start(bf16[4,88,3840]{2,1,0:T(8,128)(2,1)} %bitcast.132), calls=%async_computation.1 | async-start | bytes 5406720 | tf_op jit(solution)/shard_map/cond/branch_0_fun/all_to_all | solution.py:363
  197.9 95.4 %all-gather.15.cloned.1.call-start = ((), (), s32[]{:S(2)}) async-start(), calls=%async_computation.12 | async-start | bytes 15728640 | tf_op jit(solution)/shard_map/cond/branch_0_fun/all_gather | solution.py:368
  197.9 9.7 %collective-permute-start.6 = (bf16[128,5120]{1,0:T(8,128)(2,1)}, bf16[128,5120]{1,0:T(8,128)(2,1)S(1)}, u32[]{:S(2)}, u32[]{:S(2)}) collective-permute-start(bf16[128,5120]{1,0:T(8,128)(2,1)} %get-tuple-element.104), channel_id=1, source_target_pairs={{0,1},{1,0},{2,3},{3,2},{4,5},{5,4},{6,7},{7,6},{8,9},{9,8},{10,11... | collective-permute-start | bytes 3932168 | tf_op jit(solution)/shard_map/cond/branch_0_fun/ppermute | solution.py:336
  198.6 30.6 %collective-permute-start.7 = (bf16[128,5120]{1,0:T(8,128)(2,1)}, bf16[128,5120]{1,0:T(8,128)(2,1)S(1)}, u32[]{:S(2)}, u32[]{:S(2)}) collective-permute-start(bf16[128,5120]{1,0:T(8,128)(2,1)} %get-tuple-element.105), channel_id=1, source_target_pairs={{0,2},{1,3},{2,0},{3,1},{4,6},{5,7},{6,4},{7,5},{8,10},{9,11},{10,... | collective-permute-start | bytes 3932168 | tf_op jit(solution)/shard_map/cond/branch_0_fun/ppermute | solution.py:336
  199.7 58.1 %collective-permute-start.8 = (bf16[128,5120]{1,0:T(8,128)(2,1)}, bf16[128,5120]{1,0:T(8,128)(2,1)S(1)}, u32[]{:S(2)}, u32[]{:S(2)}) collective-permute-start(bf16[128,5120]{1,0:T(8,128)(2,1)} %get-tuple-element.106), channel_id=1, source_target_pairs={{0,3},{1,2},{2,1},{3,0},{4,7},{5,6},{6,5},{7,4},{8,11},{9,10},{10,... | collective-permute-start | bytes 3932168 | tf_op jit(solution)/shard_map/cond/branch_0_fun/ppermute | solution.py:336
  204.8 52.9 %copy-start.23 = (bf16[128,5120]{1,0:T(8,128)(2,1)S(1)}, bf16[128,5120]{1,0:T(8,128)(2,1)}, u32[]{:S(2)}) copy-start(bf16[128,5120]{1,0:T(8,128)(2,1)} %get-tuple-element.103) | copy-start | bytes 3932164 | tf_op jit(solution)/shard_map/cond
  204.8 52.9 %copy-start.41 = (bf16[2,256,128]{2,1,0:T(8,128)(2,1)S(1)}, bf16[2,256,128]{2,1,0:T(8,128)(2,1)}, u32[]{:S(2)}) copy-start(bf16[2,256,128]{2,1,0:T(8,128)(2,1)} %copy-done.40) | copy-start | bytes 393220 | tf_op jit(solution)/shard_map/cond
  265.7 27.6 %all-to-all-start.2 = ((bf16[4,88,1280]{2,1,0:T(8,128)(2,1)}), bf16[4,88,1280]{2,1,0:T(8,128)(2,1)}, u32[]{:S(2)}, u32[]{:S(2)}) async-start(bf16[4,88,1280]{2,1,0:T(8,128)(2,1)} %bitcast.134), calls=%async_computation.2 | async-start | bytes 1802240 | tf_op jit(solution)/shard_map/cond/branch_0_fun/all_to_all | solution.py:363
  (29 other events, 266.6 us)
Sparse Core Ops, SparseCore 0:
  20.2 52.1 all-gather.28
  83.1 57.2 all-gather.10
  193.2 69.5 all-gather.12
  265.8 24.0 all-gather.14
